TPU v7x, 32 devices: a whole 2x2x4 slice. The times are simulated.
32 devices in a mesh: dp: 8 (over z, y), tensor: 4 (over x, core).
Axes of the slice: x: 2, y: 2, z: 4, core: 2. Of those that a mesh axis runs over, the one named last changes fastest.
Arguments:
- tokens: bfloat16 [3, 2048, 2048], P(None, 'dp'), may hold values from -6 to 6
- seg_ids: int32 [3, 2048], P(None, 'dp'), may hold values from 0 to 3, as said below
- norm1_gain: float32 [2048], replicated, may hold values from 0.5 to 1.5
- w_query: bfloat16 [2048, 2048], P(None, 'tensor'), may hold values from -0.5 to 0.5
- w_keyval: bfloat16 [2048, 8, 128], P(None, 'tensor'), may hold values from -0.5 to 0.5
- w_out: bfloat16 [2048, 2048], P('tensor'), may hold values from -0.75 to 0.75
- norm2_gain: float32 [2048], replicated, may hold values from 0.5 to 1.5
- w_gate: bfloat16 [2048, 8192], P(None, 'tensor'), may hold values from -0.125 to 0.125
- w_up: bfloat16 [2048, 8192], P(None, 'tensor'), may hold values from -0.125 to 0.125
- w_down: bfloat16 [8192, 2048], P('tensor'), may hold values from -0.5 to 0.5
- cotangent: bfloat16 [3, 2048, 2048], P(None, 'dp'), may hold values from -6 to 6
Outputs:
- layer_out: bfloat16 [3, 2048, 2048], P(None, ('dp', 'tensor'))
- grad_tokens: float32 [3, 2048, 2048], P(None, ('dp', 'tensor'))
- grad_gain1: float32 [2048], P(('dp', 'tensor'))
- grad_query: float32 [2048, 2048], P('dp', 'tensor')
- grad_keyval: float32 [2048, 8, 128], P('dp', 'tensor')
- grad_outproj: float32 [2048, 2048], P('tensor', 'dp')
- grad_gain2: float32 [2048], P(('dp', 'tensor'))
- grad_gate: float32 [2048, 8192], P('dp', 'tensor')
- grad_up: float32 [2048, 8192], P('dp', 'tensor')
- grad_down: float32 [8192, 2048], P('tensor', 'dp')
Inputs may be any that keep to these rules, and one draw needn't show every extreme that they name: `seg_ids`: document numbers never fall along a sequence and start at 0; each sequence holds at most 4 documents, and one sequence, drawn from the seed, is a single document.
All inputs are finite; a program needn't handle non-finite values.
Results may differ from a plain program's by a relative error of at most 0.02.
Values may be sent and summed in bfloat16 or wider, within the bound.
No kernel may reach another device: no remote copies, remote signals or barrier semaphores. Data moves between devices by JAX's collectives and lax.ppermute only.
A program may use at most 256 MiB of HBM per device.

v0:
```python
import jax
import jax.numpy as jnp
from jax import lax
from jax.sharding import PartitionSpec as P

EPS = 1e-05
SCALE = 0.015625
RESID = 0.22
THETA = 10000000.0
NEG = -1e30


def rope_tables(positions, head_dim):
    half = head_dim // 2
    inverse = jnp.power(
        jnp.float32(THETA), -(jnp.arange(half).astype(jnp.float32) * (2.0 / head_dim))
    )
    angle = positions.astype(jnp.float32)[:, None] * inverse[None, :]
    return (jnp.cos(angle), jnp.sin(angle))


def rotate(vector, cosine, sine):
    half = vector.shape[-1] // 2
    first = vector[..., :half]
    second = vector[..., half:]
    return jnp.concatenate([first * cosine - second * sine, second * cosine + first * sine], -1)


def rms_scale(vector):
    return lax.rsqrt(jnp.mean(vector * vector, axis=-1, keepdims=True) + EPS)


def normalize_back(grad, source, scale, gain):
    scaled = gain * grad
    return scale * scaled - source * scale**3 * jnp.mean(scaled * source, axis=-1, keepdims=True)


def gain_part(grad, source, scale):
    return jnp.sum(grad * source * scale, axis=(0, 1))


def body(
    tokens,
    seg_ids,
    norm1_gain,
    w_query,
    w_keyval,
    w_out,
    norm2_gain,
    w_gate,
    w_up,
    w_down,
    cotangent,
):
    seqs, block, width = tokens.shape
    kv_local = w_keyval.shape[1]
    head_dim = w_keyval.shape[2] // 2
    q_local = w_query.shape[1] // head_dim
    group = q_local // kv_local
    length = block * lax.axis_size("dp")
    share = block // lax.axis_size("tensor")
    first_row = lax.axis_index("tensor") * share

    def share_of(array):
        return lax.dynamic_slice_in_dim(array, first_row, share, 1)

    positions = lax.axis_index("dp") * block + jnp.arange(block)
    cosine, sine = rope_tables(positions, head_dim)
    cosine = cosine[:, None, :]
    sine = sine[:, None, :]
    xf = tokens.astype(jnp.float32)
    scale1 = rms_scale(xf)
    xf_share = share_of(xf)
    scale1_share = share_of(scale1)
    first_normed = (xf * scale1 * norm1_gain).astype(jnp.bfloat16)
    query_projected = jnp.einsum(
        "sbd,de->sbe", first_normed, w_query, preferred_element_type=jnp.float32
    )
    keyval_projected = jnp.einsum(
        "sbd,dke->sbke", first_normed, w_keyval, preferred_element_type=jnp.float32
    )
    query = rotate(query_projected.reshape(seqs, block, q_local, head_dim), cosine, sine).astype(
        jnp.bfloat16
    )
    query = (
        query.reshape(seqs, block, kv_local, group, head_dim)
        .transpose(0, 2, 3, 1, 4)
        .reshape(seqs * kv_local, group, block, head_dim)
    )
    keyval = jnp.concatenate(
        [rotate(keyval_projected[..., :head_dim], cosine, sine), keyval_projected[..., head_dim:]],
        -1,
    )
    keyval = keyval.astype(jnp.bfloat16).transpose(0, 2, 1, 3)
    keyval_all, seg_all = (
        lax.all_gather(keyval, "dp", axis=2, tiled=True),
        lax.all_gather(seg_ids, "dp", axis=1, tiled=True),
    )
    keyval_all = keyval_all.reshape(seqs * kv_local, length, 2 * head_dim)
    key_pos = jnp.arange(length)

    def scores_of(pair):
        row = pair // kv_local
        own = lax.dynamic_index_in_dim(seg_ids, row, 0, keepdims=False)
        other = lax.dynamic_index_in_dim(seg_all, row, 0, keepdims=False)
        visible = (own[:, None] == other[None, :]) & (key_pos[None, :] <= positions[:, None])
        queries = query[pair]
        pair_kv = keyval_all[pair]
        scores = (
            jnp.einsum(
                "gbd,kd->gbk", queries, pair_kv[:, :head_dim], preferred_element_type=jnp.float32
            )
            * SCALE
        )
        return (queries, pair_kv, jnp.where(visible[None], scores, NEG))

    def attend(pair):
        queries, pair_kv, scores = scores_of(pair)
        peak = jnp.max(scores, axis=-1, keepdims=True)
        total = jnp.log(jnp.sum(jnp.exp(scores - peak), axis=-1, keepdims=True)) + peak
        probs = jnp.exp(scores - total).astype(jnp.bfloat16)
        result = jnp.einsum(
            "gbk,kd->gbd", probs, pair_kv[:, head_dim:], preferred_element_type=jnp.float32
        )
        return (result.astype(jnp.bfloat16), total)

    pairs = jnp.arange(seqs * kv_local)
    attention_output, totals = lax.map(attend, pairs)
    attention_output = (
        attention_output.reshape(seqs, kv_local, group, block, head_dim)
        .transpose(0, 3, 1, 2, 4)
        .reshape(seqs, block, q_local * head_dim)
    )
    mixed_part = jnp.einsum(
        "sbe,ed->sbd", attention_output, w_out, preferred_element_type=jnp.float32
    )
    mixed_tokens = lax.psum(mixed_part, "tensor")
    resid = xf + RESID * mixed_tokens
    scale2 = rms_scale(resid)
    second_normed = (resid * scale2 * norm2_gain).astype(jnp.bfloat16)
    resid_share = share_of(resid)
    scale2_share = share_of(scale2)
    gate_activation = jnp.einsum(
        "sbd,df->sbf", second_normed, w_gate, preferred_element_type=jnp.float32
    )
    up_activation = jnp.einsum(
        "sbd,df->sbf", second_normed, w_up, preferred_element_type=jnp.float32
    )
    sigma = jax.nn.sigmoid(gate_activation)
    swish = gate_activation * sigma
    hidden_activation = (swish * up_activation).astype(jnp.bfloat16)
    ffn_part = jnp.einsum(
        "sbf,fd->sbd", hidden_activation, w_down, preferred_element_type=jnp.float32
    )
    ffn_share = share_of(lax.psum(ffn_part.astype(jnp.bfloat16), "tensor").astype(jnp.float32))
    layer_out = (resid_share + RESID * ffn_share).astype(jnp.bfloat16)
    d_out = cotangent.astype(jnp.float32)
    d_ffn = (RESID * d_out).astype(jnp.bfloat16)
    d_hidden = jnp.einsum("sbd,fd->sbf", d_ffn, w_down, preferred_element_type=jnp.float32)
    grad_down = jnp.einsum(
        "sbf,sbd->fd", hidden_activation, d_ffn, preferred_element_type=jnp.float32
    )
    d_gate = (d_hidden * up_activation * sigma * (1.0 + gate_activation * (1.0 - sigma))).astype(
        jnp.bfloat16
    )
    d_up = (d_hidden * swish).astype(jnp.bfloat16)
    grad_gate = jnp.einsum("sbd,sbf->df", second_normed, d_gate, preferred_element_type=jnp.float32)
    grad_up = jnp.einsum("sbd,sbf->df", second_normed, d_up, preferred_element_type=jnp.float32)
    d_norm2 = jnp.einsum("sbf,df->sbd", d_gate, w_gate, preferred_element_type=jnp.float32)
    d_norm2 = d_norm2 + jnp.einsum("sbf,df->sbd", d_up, w_up, preferred_element_type=jnp.float32)
    d_norm2_full = lax.psum(d_norm2, "tensor")
    d_resid = d_out + normalize_back(d_norm2_full, resid, scale2, norm2_gain)
    d_mixed = (RESID * d_resid).astype(jnp.bfloat16)
    d_norm2_share = share_of(d_norm2_full)
    d_resid_share = share_of(d_resid)
    grad_gain2 = gain_part(d_norm2_share, resid_share, scale2_share)
    grad_outproj = jnp.einsum(
        "sbe,sbd->ed", attention_output, d_mixed, preferred_element_type=jnp.float32
    )
    d_att = jnp.einsum("sbd,ed->sbe", d_mixed, w_out, preferred_element_type=jnp.float32).astype(
        jnp.bfloat16
    )
    d_att = (
        d_att.reshape(seqs, block, kv_local, group, head_dim)
        .transpose(0, 2, 3, 1, 4)
        .reshape(seqs * kv_local, group, block, head_dim)
    )

    def attend_back(pair):
        queries, pair_kv, scores = scores_of(pair)
        probs = jnp.exp(scores - totals[pair])
        rounded = probs.astype(jnp.bfloat16)
        incoming = d_att[pair]
        d_value = jnp.einsum("gbk,gbd->kd", rounded, incoming, preferred_element_type=jnp.float32)
        d_probs = jnp.einsum(
            "gbd,kd->gbk", incoming, pair_kv[:, head_dim:], preferred_element_type=jnp.float32
        )
        d_scores = (probs * (d_probs - jnp.sum(probs * d_probs, axis=-1, keepdims=True))).astype(
            jnp.bfloat16
        )
        d_query = (
            jnp.einsum(
                "gbk,kd->gbd", d_scores, pair_kv[:, :head_dim], preferred_element_type=jnp.float32
            )
            * SCALE
        )
        d_key = (
            jnp.einsum("gbk,gbd->kd", d_scores, queries, preferred_element_type=jnp.float32) * SCALE
        )
        return (d_query, jnp.concatenate([d_key, d_value], -1))

    d_query, d_keyval = lax.map(attend_back, pairs)
    d_keyval = lax.psum_scatter(
        d_keyval.reshape(seqs, kv_local, length, 2 * head_dim).astype(jnp.bfloat16),
        "dp",
        scatter_dimension=2,
        tiled=True,
    ).astype(jnp.float32)
    d_keyval = d_keyval.transpose(0, 2, 1, 3)
    d_query = (
        d_query.reshape(seqs, kv_local, group, block, head_dim)
        .transpose(0, 3, 1, 2, 4)
        .reshape(seqs, block, q_local, head_dim)
    )
    d_q_raw = (
        rotate(d_query, cosine, -sine).astype(jnp.bfloat16).reshape(seqs, block, q_local * head_dim)
    )
    d_kv_raw = jnp.concatenate(
        [rotate(d_keyval[..., :head_dim], cosine, -sine), d_keyval[..., head_dim:]], -1
    ).astype(jnp.bfloat16)
    grad_query = jnp.einsum(
        "sbd,sbe->de", first_normed, d_q_raw, preferred_element_type=jnp.float32
    )
    grad_keyval = jnp.einsum(
        "sbd,sbke->dke", first_normed, d_kv_raw, preferred_element_type=jnp.float32
    )
    d_norm1 = jnp.einsum("sbe,de->sbd", d_q_raw, w_query, preferred_element_type=jnp.float32)
    d_norm1 = d_norm1 + jnp.einsum(
        "sbke,dke->sbd", d_kv_raw, w_keyval, preferred_element_type=jnp.float32
    )
    d_norm1_share = share_of(lax.psum(d_norm1.astype(jnp.bfloat16), "tensor").astype(jnp.float32))
    grad_tokens = d_resid_share + normalize_back(d_norm1_share, xf_share, scale1_share, norm1_gain)
    grad_gain1 = gain_part(d_norm1_share, xf_share, scale1_share)
    summed = (
        lax.psum_scatter(
            grad_query.astype(jnp.bfloat16), "dp", scatter_dimension=0, tiled=True
        ).astype(jnp.float32),
        lax.psum_scatter(
            grad_keyval.astype(jnp.bfloat16), "dp", scatter_dimension=0, tiled=True
        ).astype(jnp.float32),
        lax.psum_scatter(
            grad_outproj.astype(jnp.bfloat16), "dp", scatter_dimension=1, tiled=True
        ).astype(jnp.float32),
        lax.psum_scatter(
            grad_gate.astype(jnp.bfloat16), "dp", scatter_dimension=0, tiled=True
        ).astype(jnp.float32),
        lax.psum_scatter(
            grad_up.astype(jnp.bfloat16), "dp", scatter_dimension=0, tiled=True
        ).astype(jnp.float32),
        lax.psum_scatter(
            grad_down.astype(jnp.bfloat16), "dp", scatter_dimension=1, tiled=True
        ).astype(jnp.float32),
    )
    gains = (
        lax.psum_scatter(grad_gain1, ("dp", "tensor"), scatter_dimension=0, tiled=True),
        lax.psum_scatter(grad_gain2, ("dp", "tensor"), scatter_dimension=0, tiled=True),
    )
    return (
        layer_out,
        grad_tokens,
        gains[0],
        summed[0],
        summed[1],
        summed[2],
        gains[1],
        summed[3],
        summed[4],
        summed[5],
    )


def solution(mesh):
    placed = (
        P(None, "dp", None),
        P(None, "dp"),
        P(),
        P(None, "tensor"),
        P(None, "tensor", None),
        P("tensor", None),
        P(),
        P(None, "tensor"),
        P(None, "tensor"),
        P("tensor", None),
        P(None, "dp", None),
    )
    return jax.shard_map(
        body,
        mesh=mesh,
        in_specs=placed,
        out_specs=(
            P(None, ("dp", "tensor"), None),
            P(None, ("dp", "tensor"), None),
            P(("dp", "tensor")),
            P("dp", "tensor"),
            P("dp", "tensor", None),
            P("tensor", "dp"),
            P(("dp", "tensor")),
            P("dp", "tensor"),
            P("dp", "tensor"),
            P("tensor", "dp"),
        ),
        check_vma=False,
    )
```

profile of v0, /device:TPU:0, one launch (start us, length us, event | category | flops | bytes accessed | tf_op | source)
XLA Modules:
  0.0 1515.7 jit_solution(16517575461565897123)
XLA Ops:
  17.3 32.6 %all_gather.6 = s32[3,2048]{1,0:T(4,128)S(1)} all-gather(s32[3,256]{1,0:T(4,128)S(1)} %copy-done.12), channel_id=1, replica_groups=mesh['dp'=8,'tensor'=4] {'dp'}, dimensions={1}, use_global_device_ids=true | all-gather | bytes 27648 | tf_op jit(solution)/shard_map/all_gather | solution.py:97
  54.9 28.4 %all-gather.2.cloned.1.call-done = bf16[3,2,2048,128]{2,3,1,0:T(8,128)(2,1)} async-done(((bf16[3,2,256,128]{2,3,1,0:T(8,128)(2,1)}), bf16[3,2,2048,128]{2,3,1,0:T(8,128)(2,1)}) %all-gather.2.cloned.1.call-update) | async-done | bytes 3145744 | tf_op jit(solution)/shard_map/all_gather | solution.py:96
  83.3 78.3 %while.30 = (s32[]{:T(128)}, bf16[6,4,256,64]{2,3,1,0:T(8,128)(2,1)}, f32[6,4,256,1]{2,1,3,0:T(4,128)S(1)}, s32[6]{0:T(128)S(1)}, s32[3,256]{1,0:T(4,128)S(1)}, ...) while((s32[]{:T(128)}, ...), condition=%wide.region_4.5_spmd.clone, body=%wide.region_1.4_spmd.clone.sunk | while | flops 561577216 | bytes 29161336 | solution.py:128
  161.6 5.6 fusion.84
  167.5 11.8 fusion.49
  179.4 105.7 %all-reduce.8.cloned.1.call-done = f32[3,256,2048]{2,1,0:T(8,128)} async-done(((f32[3,256,2048]{2,1,0:T(8,128)}), f32[3,256,2048]{2,1,0:T(8,128)}) %all-reduce.8.cloned.1.call-update) | async-done | bytes 6291472 | tf_op jit(solution)/shard_map/psum | solution.py:137
  293.3 12.0 fusion.55
  305.3 16.9 %multiply_convert_fusion.3 = (bf16[3,256,2048]{2,1,0:T(8,128)(2,1)}, bf16[3,256,2048]{2,1,0:T(8,128)(2,1)}, bf16[3,256,2048]{2,1,0:T(8,128)(2,1)}) fusion(f32[3,256,2048]{2,1,0:T(8,128)} %fusion.49, f32[3,256,2048]{2,1,0:T(8,128)} %fusion.55, bf16[3,256,2048]{2,1,0:T(8,128)(2,1)S(1)} %multiply_convert_fusion.5, bf16[2048,2048]{1,0:T(8,128)(2,1)} %param.22), kind=kOutput, calls=%fused_computation.91 | convolution fusion | flops 6466043904 | bytes 33554432 | tf_op jit(solution)/shard_map/sbd,df->sbf/dot_general | solution.py:143
  322.2 10.5 fusion.53
  332.8 13.4 fusion.64
  346.2 119.9 %all-reduce.10.cloned.1.call-done = f32[3,256,2048]{2,1,0:T(8,128)} async-done(((f32[3,256,2048]{2,1,0:T(8,128)}), f32[3,256,2048]{2,1,0:T(8,128)}) %all-reduce.10.cloned.1.call-update) | async-done | bytes 6291472 | tf_op jit(solution)/shard_map/psum | solution.py:171
  485.1 157.7 %while.31 = (s32[]{:T(128)}, f32[6,4,256,64]{2,3,1,0:T(8,128)}, bf16[6,2048,128]{1,2,0:T(8,128)(2,1)}, s32[6]{0:T(128)S(1)}, s32[3,256]{1,0:T(4,128)S(1)}, /*ind...) while((s32[]{:T(128)}, f32[6,4,256,64]{2,3,1,0:T(8,128)}, ...), condition=%wide.region_12.13_spmd.clone, body=%wide.region_10.12_spmd.clone.sunk | while | flops 1376582912 | bytes 94431672 | solution.py:212
  496.0 5.6 multiply_reduce_fusion.6
  522.4 5.6 multiply_reduce_fusion.6
  548.7 5.6 multiply_reduce_fusion.6
  574.9 5.6 multiply_reduce_fusion.6
  601.2 5.6 multiply_reduce_fusion.6
  627.5 5.6 multiply_reduce_fusion.6
  643.2 6.2 bitcast_convert_fusion.3
  656.7 61.6 %reduce-scatter.8.cloned.1.call-done = bf16[3,2,256,128]{2,3,1,0:T(8,128)(2,1)} async-done(((bf16[3,2,2048,128]{2,3,1,0:T(8,128)(2,1)}), bf16[3,2,256,128]{2,3,1,0:T(8,128)(2,1)}) %reduce-scatter.8.cloned.1.call-update) | async-done | bytes 393232 | tf_op jit(solution)/shard_map/reduce_scatter | solution.py:213
  724.6 12.0 fusion.67
  741.5 11.5 bitcast_convert_fusion.2
  753.1 11.5 bitcast_convert_fusion.1
  765.1 11.5 bitcast_convert_fusion
  782.1 7.6 reduce-scatter.14.cloned.1.call-done
  791.4 68.9 %reduce-scatter.10.cloned.1.call-done = bf16[256,512]{1,0:T(8,128)(2,1)} async-done(((bf16[2048,512]{1,0:T(8,128)(2,1)}), bf16[256,512]{1,0:T(8,128)(2,1)}) %reduce-scatter.10.cloned.1.call-update) | async-done | bytes 262160 | tf_op jit(solution)/shard_map/reduce_scatter | solution.py:245
  862.1 64.7 %reduce-scatter.12.cloned.1.call-done = bf16[256,2,128]{2,0,1:T(8,128)(2,1)} async-done(((bf16[2048,2,128]{2,0,1:T(8,128)(2,1)}), bf16[256,2,128]{2,0,1:T(8,128)(2,1)}) %reduce-scatter.12.cloned.1.call-update) | async-done | bytes 131088 | tf_op jit(solution)/shard_map/reduce_scatter | solution.py:248
  928.5 119.6 %all-reduce.12.cloned.1.call-done = (bf16[3,256,2048]{2,1,0:T(8,128)(2,1)}, bf16[3,256,2048]{2,1,0:T(8,128)(2,1)}) async-done(((bf16[3,256,2048]{2,1,0:T(8,128)(2,1)}, bf16[3,256,2048]{2,1,0:T(8,128)(2,1)}), (bf16[3,256,2048]{2,1,0:T(8,128)(2,1)}, bf16[3,256,2048]{2,1,0:T(8,128)(2,1)})) %all-reduce.12.cloned.1.call-update) | async-done | bytes 6291472 | tf_op jit(solution)/shard_map/psum | solution.py:155
  1053.6 42.9 %all-reduce.2 = (f32[2048]{0:T(1024)S(1)}, f32[2048]{0:T(1024)S(1)}) all-reduce(f32[2048]{0:T(1024)S(1)} %get-tuple-element.370, f32[2048]{0:T(1024)S(1)} %get-tuple-element.429), channel_id=3, replica_groups=mesh['dp'=8,'tensor'=4] {'dp','tensor'}, use_global_device_ids=true, to_apply=%region_17.18.clone | all-reduce | flops 4096 | bytes 32768
  1101.7 100.6 %reduce-scatter.16.cloned.1.call-done = bf16[256,2048]{1,0:T(8,128)(2,1)} async-done(((bf16[2048,2048]{1,0:T(8,128)(2,1)}), bf16[256,2048]{1,0:T(8,128)(2,1)}) %reduce-scatter.16.cloned.1.call-update) | async-done | bytes 1048592 | tf_op jit(solution)/shard_map/reduce_scatter | solution.py:254
  1205.2 148.7 %reduce-scatter.18.cloned.1.call-done = bf16[256,2048]{1,0:T(8,128)(2,1)} async-done(((bf16[2048,2048]{1,0:T(8,128)(2,1)}), bf16[256,2048]{1,0:T(8,128)(2,1)}) %reduce-scatter.18.cloned.1.call-update) | async-done | bytes 1048592 | tf_op jit(solution)/shard_map/reduce_scatter | solution.py:257
  1356.7 149.7 %reduce-scatter.20.cloned.1.call-done = bf16[2048,256]{1,0:T(8,128)(2,1)} async-done(((bf16[2048,2048]{1,0:T(8,128)(2,1)}), bf16[2048,256]{1,0:T(8,128)(2,1)}) %reduce-scatter.20.cloned.1.call-update) | async-done | bytes 1048592 | tf_op jit(solution)/shard_map/reduce_scatter | solution.py:260
  (286 shorter events, 245.8 us)
Async XLA Ops:
  7.2 154.4 %copy-start = (bf16[512,2048]{1,0:T(8,128)(2,1)S(1)}, bf16[512,2048]{1,0:T(8,128)(2,1)}, u32[]{:S(2)}) copy-start(bf16[512,2048]{1,0:T(8,128)(2,1)} %param.20) | copy-start | bytes 6291460
  7.2 76.1 %all-gather.2.cloned.1.call-start = ((), (), s32[]{:S(2)}) async-start(), calls=%async_computation.7 | async-start | bytes 3538944 | tf_op jit(solution)/shard_map/all_gather | solution.py:96
  10.0 39.9 %copy-start.17 = (f32[3,256]{1,0:T(4,128)}, f32[3,256]{1,0:T(4,128)S(1)}, u32[]{:S(2)}) copy-start(f32[3,256]{1,0:T(4,128)S(1)} %add_rsqrt_fusion.1) | copy-start | bytes 9220
  10.0 7.3 copy-start.12
  10.0 39.9 %copy-start.15 = (f32[2048]{0:T(1024)S(1)}, f32[2048]{0:T(1024)}, u32[]{:S(2)}) copy-start(f32[2048]{0:T(1024)} %param.17) | copy-start | bytes 24580
  16.3 38.2 %copy-start.8 = (f32[256,32]{0,1:T(8,128)}, f32[256,32]{0,1:T(8,128)S(1)}, u32[]{:S(2)}) copy-start(f32[256,32]{0,1:T(8,128)S(1)} %get-tuple-element.443) | copy-start | bytes 98308
  17.2 267.9 %all-reduce.8.cloned.1.call-start = ((), (), s32[]{:S(2)}) async-start(), calls=%async_computation.8 | async-start | bytes 12582912 | tf_op jit(solution)/shard_map/psum | solution.py:137
  167.2 298.9 %all-reduce.10.cloned.1.call-start = ((), (), s32[]{:S(2)}) async-start(), calls=%async_computation.9 | async-start | bytes 12582912 | tf_op jit(solution)/shard_map/psum | solution.py:171
  179.4 113.3 %copy-start.11 = (f32[2048]{0:T(1024)S(1)}, f32[2048]{0:T(1024)}, u32[]{:S(2)}) copy-start(f32[2048]{0:T(1024)} %param.21) | copy-start | bytes 24580
  289.9 181.7 %copy-start.13 = (f32[3,256]{1,0:T(4,128)}, f32[3,256]{1,0:T(4,128)S(1)}, u32[]{:S(2)}) copy-start(f32[3,256]{1,0:T(4,128)S(1)} %get-tuple-element.440) | copy-start | bytes 9220
  293.3 12.0 copy-start.6
  293.3 28.9 %slice-start.2 = ((s8[8388608]{0:T(1024)(128)(4,1)}), s8[4194304]{0:T(1024)(128)(4,1)S(1)}, s32[]{:S(2)}) async-start(s8[8388608]{0:T(1024)(128)(4,1)} %bitcast.260), calls=%async_computation.20 | async-start | bytes 8388608
  305.3 16.9 %slice-start.3 = ((s8[8388608]{0:T(1024)(128)(4,1)}), s8[4194304]{0:T(1024)(128)(4,1)S(1)}, s32[]{:S(2)}) async-start(s8[8388608]{0:T(1024)(128)(4,1)} %bitcast.260), calls=%async_computation.21 | async-start | bytes 8388608
  346.2 372.1 %reduce-scatter.8.cloned.1.call-start = ((), (), s32[]{:S(2)}) async-start(), calls=%async_computation.10 | async-start | bytes 3538944 | tf_op jit(solution)/shard_map/reduce_scatter | solution.py:213
  466.1 7.3 copy-start.7
  495.3 6.4 slice-start
  521.6 6.4 slice-start
  547.9 6.4 slice-start
  600.4 6.4 slice-start
  642.9 6.6 copy-start.9
  642.9 6.6 copy-start.10
  642.9 8.5 copy-start.16
  642.9 8.5 copy-start.18
  642.9 146.7 %reduce-scatter.14.cloned.1.call-start = ((), (), s32[]{:S(2)}) async-start(), calls=%async_computation.13 | async-start | bytes 2359296 | tf_op jit(solution)/shard_map/reduce_scatter | solution.py:251
  649.4 210.9 %reduce-scatter.10.cloned.1.call-start = ((), (), s32[]{:S(2)}) async-start(), calls=%async_computation.11 | async-start | bytes 2359296 | tf_op jit(solution)/shard_map/reduce_scatter | solution.py:245
  656.7 270.0 %reduce-scatter.12.cloned.1.call-start = ((), (), s32[]{:S(2)}) async-start(), calls=%async_computation.12 | async-start | bytes 1179648 | tf_op jit(solution)/shard_map/reduce_scatter | solution.py:248
  724.6 323.5 %all-reduce.12.cloned.1.call-start = ((), (), s32[]{:S(2)}) async-start(), calls=%async_computation.17 | async-start | bytes 12582912 | tf_op jit(solution)/shard_map/psum | solution.py:155
  724.6 12.0 copy-start.19
  741.2 461.2 %reduce-scatter.16.cloned.1.call-start = ((), (), s32[]{:S(2)}) async-start(), calls=%async_computation.14 | async-start | bytes 9437184 | tf_op jit(solution)/shard_map/reduce_scatter | solution.py:254
  753.0 600.8 %reduce-scatter.18.cloned.1.call-start = ((), (), s32[]{:S(2)}) async-start(), calls=%async_computation.15 | async-start | bytes 9437184 | tf_op jit(solution)/shard_map/reduce_scatter | solution.py:257
  764.6 741.8 %reduce-scatter.20.cloned.1.call-start = ((), (), s32[]{:S(2)}) async-start(), calls=%async_computation.16 | async-start | bytes 9437184 | tf_op jit(solution)/shard_map/reduce_scatter | solution.py:260
  1097.7 411.4 %copy-start.1 = (bf16[512,2048]{1,0:T(8,128)(2,1)S(1)}, bf16[512,2048]{1,0:T(8,128)(2,1)}, u32[]{:S(2)}) copy-start(bf16[512,2048]{1,0:T(8,128)(2,1)} %param.20) | copy-start | bytes 6291460
  (13 other events, 66.0 us)
Sparse Core Ops, SparseCore 0:
  17.3 65.9 all-gather.1
  167.3 117.7 all-reduce.7
  346.3 119.7 all-reduce.9
  643.0 75.2 reduce-scatter.7
  722.2 67.3 reduce-scatter.13
  793.6 66.6 reduce-scatter.9
  864.2 62.4 reduce-scatter.11
  929.2 118.8 all-reduce.11
  1052.2 150.1 reduce-scatter.15
  1205.9 147.9 reduce-scatter.17
  1357.9 148.3 reduce-scatter.19
where the time goes:
time: 1520 us
  waiting for transfers between devices  976 us (64%)
  matrix products  273 us (18%)
  other arithmetic  91.5 us (6%)
  blocking collectives  75.6 us (5%)
  loops' own time  47.8 us (3%)
  local copies, waits for them, and re-layouts  36.3 us (2%)
    reduce_scatter x1, waiting for transfers between devices, body(): lax.psum_scatter(grad_down.astype(jnp.bfloat16), 'dp', scatter_dimension=...  150 us
    reduce_scatter x1, waiting for transfers between devices, body(): lax.psum_scatter(grad_up.astype(jnp.bfloat16), 'dp', scatter_dimension=0,...  149 us
    psum x1, waiting for transfers between devices, body(): d_norm2_full = lax.psum(d_norm2, 'tensor')  120 us
    psum x1, waiting for transfers between devices, body(): lax.psum(ffn_part.astype(jnp.bfloat16), 'tensor').astype(jnp.float32)  120 us
    psum x1, waiting for transfers between devices, body(): mixed_tokens = lax.psum(mixed_part, 'tensor')  106 us
    reduce_scatter x1, waiting for transfers between devices, body(): lax.psum_scatter(grad_gate.astype(jnp.bfloat16), 'dp', scatter_dimension=...  101 us
    reduce_scatter x1, waiting for transfers between devices, body(): lax.psum_scatter(grad_query.astype(jnp.bfloat16), 'dp', scatter_dimension...  68.9 us
    reduce_scatter x1, waiting for transfers between devices, body(): lax.psum_scatter(grad_keyval.astype(jnp.bfloat16), 'dp', scatter_dimensio...  64.7 us
  transfers between devices with their start and end apart: 11, of which 11 were waited for; matrix products, arithmetic and copies ran while one was open for 8% of the time, Pallas kernels for 0%

commit v1 on v0

v1 whole, which is shorter than its diff:
```python
import math

import jax
import jax.numpy as jnp
from jax import lax
from jax.experimental import pallas as pl
from jax.experimental.pallas import tpu as pltpu
from jax.sharding import PartitionSpec as P

EPS = 1e-05
SCALE = 0.015625
RESID = 0.22
THETA = 10000000.0
NEG = -1e30
PAD = 16
VMEM = 56 * 1024 * 1024
F32 = jnp.float32
BF16 = jnp.bfloat16
NT = (((1,), (1,)), ((), ()))
TN = (((0,), (0,)), ((), ()))


def dot(a, b, dims=None):
    if dims is None:
        return jnp.dot(a, b, preferred_element_type=F32)
    return lax.dot_general(a, b, dims, preferred_element_type=F32)


def params():
    return pltpu.CompilerParams(vmem_limit_bytes=VMEM)


def cost(flops, nbytes):
    return pl.CostEstimate(flops=int(flops), bytes_accessed=int(nbytes), transcendentals=0)


def slot_order(bits):
    slots = [0]
    for bit in reversed(bits):
        slots = slots + [k ^ (1 << bit) for k in slots]
    return slots


def swap(value, axis, distance):
    size = lax.axis_size(axis)
    return lax.ppermute(value, axis, [(i, i ^ distance) for i in range(size)])


def rope_tables(positions, head_dim):
    half = head_dim // 2
    inverse = jnp.power(F32(THETA), -(jnp.arange(half).astype(F32) * (2.0 / head_dim)))
    angle = positions.astype(F32)[:, None] * inverse[None, :]
    return (jnp.cos(angle), jnp.sin(angle))


def rotate_lanes(x, cosine, sine, half):
    width = x.shape[1]
    lane = lax.broadcasted_iota(jnp.int32, x.shape, 1)
    ahead = pltpu.roll(x, width - half, 1)
    behind = pltpu.roll(x, half, 1)
    partner = jnp.where((lane & (2 * half - 1)) < half, ahead, behind)
    times = width // cosine.shape[1]
    if times > 1:
        cosine = jnp.concatenate([cosine] * times, 1)
        sine = jnp.concatenate([sine] * times, 1)
    return x * cosine + partner * sine


def norm_keyval(tokens, gain, weight, counts, cosine, sine, half):
    seqs, block, width = tokens.shape
    out = weight.shape[1]

    def kernel(tok_ref, gain_ref, w_ref, count_ref, cos_ref, sin_ref, n_ref, kv_ref):
        xf = tok_ref[0].astype(F32)
        scale = lax.rsqrt(jnp.mean(xf * xf, axis=-1, keepdims=True) + EPS)
        normed = (xf * scale * gain_ref[...]).astype(BF16)
        n_ref[0] = normed
        raw = dot(normed, w_ref[...])
        kv_ref[0, :block, :] = rotate_lanes(raw, cos_ref[...], sin_ref[...], half).astype(BF16)
        kv_ref[0, block:, :] = count_ref[0]

    whole = lambda shape: pl.BlockSpec(shape, lambda s: (0,) * len(shape))
    return pl.pallas_call(
        kernel,
        grid=(seqs,),
        in_specs=[
            pl.BlockSpec((1, block, width), lambda s: (s, 0, 0)),
            whole((1, width)),
            whole((width, out)),
            pl.BlockSpec((1, PAD, out), lambda s: (s, 0, 0)),
            whole(cosine.shape),
            whole(sine.shape),
        ],
        out_specs=[
            pl.BlockSpec((1, block, width), lambda s: (s, 0, 0)),
            pl.BlockSpec((1, block + PAD, out), lambda s: (s, 0, 0)),
        ],
        out_shape=[
            jax.ShapeDtypeStruct((seqs, block, width), BF16),
            jax.ShapeDtypeStruct((seqs, block + PAD, out), BF16),
        ],
        compiler_params=params(),
        cost_estimate=cost(2 * seqs * block * width * out, 4 * seqs * block * width),
        name="norm_keyval",
    )(tokens, gain.reshape(1, width), weight, counts, cosine, sine)


def project_query(normed, weight, cosine, sine, half):
    seqs, block, width = normed.shape
    out = weight.shape[1]

    def kernel(n_ref, w_ref, cos_ref, sin_ref, q_ref):
        raw = dot(n_ref[0], w_ref[...])
        q_ref[0] = rotate_lanes(raw, cos_ref[...], sin_ref[...], half).astype(BF16)

    whole = lambda shape: pl.BlockSpec(shape, lambda s: (0,) * len(shape))
    return pl.pallas_call(
        kernel,
        grid=(seqs,),
        in_specs=[
            pl.BlockSpec((1, block, width), lambda s: (s, 0, 0)),
            whole((width, out)),
            whole(cosine.shape),
            whole(sine.shape),
        ],
        out_specs=pl.BlockSpec((1, block, out), lambda s: (s, 0, 0)),
        out_shape=jax.ShapeDtypeStruct((seqs, block, out), BF16),
        compiler_params=params(),
        cost_estimate=cost(2 * seqs * block * width * out, 2 * seqs * block * width),
        name="project_query",
    )(normed, weight, cosine, sine)


def stacked_lanes(x, group, hd, low):
    rows = x.shape[1]
    flat = jnp.concatenate([x[h * hd : (h + 1) * hd] for h in range(group)], 1)
    zero = jnp.zeros((hd, group * rows), flat.dtype)
    return jnp.concatenate([flat, zero] if low else [zero, flat], 0)


def stacked_rows(x, group, hd, low):
    parts = []
    for h in range(group):
        at = (h * hd) // (2 * hd) * (2 * hd)
        piece = x[:, at : at + 2 * hd]
        if (h % 2 == 0) != low:
            piece = pltpu.roll(piece, hd, 1)
        lane = lax.broadcasted_iota(jnp.int32, piece.shape, 1)
        parts.append(jnp.where((lane < hd) == low, piece, 0.0))
    return jnp.concatenate(parts, 0)


def mask_bias(chunk, block, position_block, doc_start, group):
    key_pos = chunk * block + lax.broadcasted_iota(jnp.int32, (block, block), 0)
    query_pos = position_block * block + lax.broadcasted_iota(jnp.int32, (block, block), 1)
    visible = (key_pos >= doc_start) & (key_pos <= query_pos)
    bias = jnp.where(visible, 0.0, NEG)
    return jnp.concatenate([bias] * group, 1)


def attend(query, keyval_all, doc_start, scalars, kv_local, hd):
    seqs, block, q_width = query.shape
    blocks = keyval_all.shape[0]
    group = q_width // kv_local // hd
    wide = group * block

    def kernel(sc, q_ref, kv_ref, doc_ref, o_ref, lse_ref, acc):
        seq = pl.program_id(0)
        mine = sc[0]
        start = sc[1 + seq]
        clear = sc[1 + seqs + seq]
        q_lanes = stacked_lanes((q_ref[0].astype(F32) * SCALE).T.astype(BF16), group, hd, True)
        doc = doc_ref[0]

        def scores_of(chunk, masked):
            kv = kv_ref[chunk, 0, :block, :]
            scores = dot(kv, q_lanes)
            if masked:
                scores = scores + mask_bias(chunk, block, mine, doc, group)
            return kv, scores

        kv, scores = scores_of(mine, True)
        peak = jnp.max(scores, axis=0, keepdims=True)
        probs = jnp.exp(scores - peak)
        total = jnp.sum(probs, axis=0, keepdims=True)
        acc[...] = dot(kv, probs.astype(BF16), TN)

        def step(masked):
            def run(chunk, carry):
                peak, total = carry
                kv, scores = scores_of(chunk, masked)
                higher = jnp.maximum(peak, jnp.max(scores, axis=0, keepdims=True))
                shrink = jnp.exp(peak - higher)
                probs = jnp.exp(scores - higher)
                total = total * shrink + jnp.sum(probs, axis=0, keepdims=True)
                acc[...] = acc[...] * shrink + dot(kv, probs.astype(BF16), TN)
                return higher, total

            return run

        carry = lax.fori_loop(start, clear, step(True), (peak, total))
        peak, total = lax.fori_loop(clear, mine, step(False), carry)
        lse_ref[0, 0] = peak + jnp.log(total)
        result = acc[hd:] / total
        result = jnp.concatenate([result[:, h * block : (h + 1) * block] for h in range(group)], 0)
        o_ref[0] = result.T.astype(BF16)

    return pl.pallas_call(
        kernel,
        grid_spec=pltpu.PrefetchScalarGridSpec(
            num_scalar_prefetch=1,
            grid=(seqs, kv_local),
            in_specs=[
                pl.BlockSpec((1, block, group * hd), lambda s, h, sc: (s, 0, h)),
                pl.BlockSpec((blocks, 1, block + PAD, 2 * hd), lambda s, h, sc: (0, s, 0, h)),
                pl.BlockSpec((1, 1, block), lambda s, h, sc: (s, 0, 0)),
            ],
            out_specs=[
                pl.BlockSpec((1, block, group * hd), lambda s, h, sc: (s, 0, h)),
                pl.BlockSpec((1, 1, 1, wide), lambda s, h, sc: (s, h, 0, 0)),
            ],
            scratch_shapes=[pltpu.VMEM((2 * hd, wide), F32)],
        ),
        out_shape=[
            jax.ShapeDtypeStruct((seqs, block, q_width), BF16),
            jax.ShapeDtypeStruct((seqs, kv_local, 1, wide), F32),
        ],
        compiler_params=params(),
        cost_estimate=cost(
            8 * seqs * block * q_width * blocks * block, 4 * seqs * blocks * block * 2 * hd
        ),
        name="attend",
    )(scalars, query, keyval_all, doc_start)


def attend_back(query, keyval_all, doc_start, attended, d_att, lse, cosine, sine, scalars, kv_local, hd):
    seqs, block, q_width = query.shape
    blocks = keyval_all.shape[0]
    group = q_width // kv_local // hd
    wide = group * block
    base = 1 + 2 * seqs

    def kernel(
        sc, q_ref, kv_ref, doc_ref, o_ref, do_ref, lse_ref, cos_ref, sin_ref, dq_ref, dkv_ref, acc
    ):
        seq = pl.program_id(0)
        mine = sc[0]
        start = sc[1 + seq]
        clear = sc[1 + seqs + seq]
        doc = doc_ref[0]
        q = q_ref[0].astype(F32) * SCALE
        d_out = do_ref[0].astype(F32)
        d_out_t = d_out.T
        q_lanes = stacked_lanes(q.T.astype(BF16), group, hd, True)
        o_lanes = d_out_t * o_ref[0].astype(F32).T
        delta = jnp.concatenate(
            [
                jnp.sum(o_lanes[h * hd : (h + 1) * hd], axis=0, keepdims=True)
                for h in range(group)
            ],
            1,
        )
        d_lanes = stacked_lanes(d_out_t.astype(BF16), group, hd, False)
        q_rows = stacked_rows(q, group, hd, True).astype(BF16)
        d_rows = stacked_rows(d_out, group, hd, False).astype(BF16)
        total = lse_ref[0, 0]
        acc[...] = jnp.zeros_like(acc)

        def work(chunk, masked):
            kv = kv_ref[chunk, 0, :block, :]
            scores = dot(kv, q_lanes)
            if masked:
                scores = scores + mask_bias(chunk, block, mine, doc, group)
            probs = jnp.exp(scores - total)
            d_probs = dot(kv, d_lanes)
            d_scores = (probs * (d_probs - delta)).astype(BF16)
            d_kv = dot(probs.astype(BF16), d_rows) + dot(d_scores, q_rows)
            dkv_ref[sc[base + chunk], 0] = d_kv.astype(BF16)
            acc[...] += dot(kv, d_scores, TN)

        def clean(chunk, carry):
            dkv_ref[sc[base + chunk], 0] = jnp.zeros((block, 2 * hd), BF16)
            return carry

        def step(masked):
            def run(chunk, carry):
                work(chunk, masked)
                return carry

            return run

        lax.fori_loop(0, start, clean, 0)
        lax.fori_loop(start, clear, step(True), 0)
        lax.fori_loop(clear, mine, step(False), 0)
        work(mine, True)
        lax.fori_loop(mine + 1, blocks, clean, 0)
        dq = acc[:hd] * SCALE
        dq = jnp.concatenate([dq[:, h * block : (h + 1) * block] for h in range(group)], 0)
        dq_ref[0] = rotate_lanes(dq.T, cos_ref[...], -sin_ref[...], hd // 2).astype(BF16)

    queries = pl.BlockSpec((1, block, group * hd), lambda s, h, sc: (s, 0, h))
    return pl.pallas_call(
        kernel,
        grid_spec=pltpu.PrefetchScalarGridSpec(
            num_scalar_prefetch=1,
            grid=(seqs, kv_local),
            in_specs=[
                queries,
                pl.BlockSpec((blocks, 1, block + PAD, 2 * hd), lambda s, h, sc: (0, s, 0, h)),
                pl.BlockSpec((1, 1, block), lambda s, h, sc: (s, 0, 0)),
                queries,
                queries,
                pl.BlockSpec((1, 1, 1, wide), lambda s, h, sc: (s, h, 0, 0)),
                pl.BlockSpec(cosine.shape, lambda s, h, sc: (0, 0)),
                pl.BlockSpec(sine.shape, lambda s, h, sc: (0, 0)),
            ],
            out_specs=[
                queries,
                pl.BlockSpec((blocks, 1, block, 2 * hd), lambda s, h, sc: (0, s, 0, h)),
            ],
            scratch_shapes=[pltpu.VMEM((2 * hd, wide), F32)],
        ),
        out_shape=[
            jax.ShapeDtypeStruct((seqs, block, q_width), BF16),
            jax.ShapeDtypeStruct((blocks, seqs, block, kv_local * 2 * hd), BF16),
        ],
        compiler_params=params(),
        cost_estimate=cost(
            20 * seqs * block * q_width * blocks * block, 8 * seqs * blocks * block * 2 * hd
        ),
        name="attend_back",
    )(scalars, query, keyval_all, doc_start, attended, d_att, lse, cosine, sine)


def feed_forward(normed, d_ffn, w_gate, w_up, w_down):
    rows, width = normed.shape
    hidden = w_gate.shape[1]
    tile = math.gcd(hidden, 512)
    steps = hidden // tile
    half = rows // 2

    def kernel(
        n_ref, dy_ref, wg_ref, wu_ref, wd_ref, h_ref, dg_ref, du_ref, fk, fs, nk, ns, f_acc, n_acc
    ):
        at = pl.program_id(0)
        normed = n_ref[...]
        gate = dot(normed, wg_ref[...])
        up = dot(normed, wu_ref[...])
        d_hidden = dot(dy_ref[...], wd_ref[...], NT)
        sigma = jax.nn.sigmoid(gate)
        swish = gate * sigma
        hidden_tile = (swish * up).astype(BF16)
        d_gate = (d_hidden * up * sigma * (1.0 + gate * (1.0 - sigma))).astype(BF16)
        d_up = (d_hidden * swish).astype(BF16)
        h_ref[...] = hidden_tile
        dg_ref[...] = d_gate
        du_ref[...] = d_up
        ffn = dot(hidden_tile, wd_ref[...])
        d_normed = dot(d_gate, wg_ref[...], NT) + dot(d_up, wu_ref[...], NT)

        @pl.when(at == 0)
        def _():
            f_acc[...] = ffn
            n_acc[...] = d_normed

        @pl.when(at > 0)
        def _():
            f_acc[...] += ffn
            n_acc[...] += d_normed

        @pl.when(at == steps - 1)
        def _():
            fk[...] = f_acc[:half].astype(BF16)
            fs[...] = f_acc[half:].astype(BF16)
            nk[...] = n_acc[:half].astype(BF16)
            ns[...] = n_acc[half:].astype(BF16)

    whole = lambda r: pl.BlockSpec((r, width), lambda j: (0, 0))
    return pl.pallas_call(
        kernel,
        grid=(steps,),
        in_specs=[
            whole(rows),
            whole(rows),
            pl.BlockSpec((width, tile), lambda j: (0, j)),
            pl.BlockSpec((width, tile), lambda j: (0, j)),
            pl.BlockSpec((tile, width), lambda j: (j, 0)),
        ],
        out_specs=[pl.BlockSpec((rows, tile), lambda j: (0, j))] * 3 + [whole(half)] * 4,
        out_shape=[jax.ShapeDtypeStruct((rows, hidden), BF16)] * 3
        + [jax.ShapeDtypeStruct((half, width), BF16)] * 4,
        scratch_shapes=[pltpu.VMEM((rows, width), F32)] * 2,
        compiler_params=params(),
        cost_estimate=cost(12 * rows * width * hidden, 6 * width * hidden + 6 * rows * hidden),
        name="feed_forward",
    )(normed, d_ffn, w_gate, w_up, w_down)


def transposed_slots(array, blocks_at):
    rows, width = array.shape
    count = blocks_at.shape[0]
    piece = width // count

    def kernel(at, a_ref, o_ref):
        o_ref[...] = a_ref[...].astype(F32).T.astype(BF16)

    return pl.pallas_call(
        kernel,
        grid_spec=pltpu.PrefetchScalarGridSpec(
            num_scalar_prefetch=1,
            grid=(count,),
            in_specs=[pl.BlockSpec((rows, piece), lambda i, at: (0, at[i]))],
            out_specs=pl.BlockSpec((piece, rows), lambda i, at: (i, 0)),
        ),
        out_shape=jax.ShapeDtypeStruct((width, rows), BF16),
        compiler_params=params(),
        cost_estimate=cost(0, 4 * rows * width),
        name="transposed_slots",
    )(blocks_at, array)


def body(
    tokens,
    seg_ids,
    norm1_gain,
    w_query,
    w_keyval,
    w_out,
    norm2_gain,
    w_gate,
    w_up,
    w_down,
    cotangent,
):
    seqs, block, width = tokens.shape
    kv_local = w_keyval.shape[1]
    hd = w_keyval.shape[2] // 2
    q_width = w_query.shape[1]
    kv_width = kv_local * 2 * hd
    dp = lax.axis_size("dp")
    nt = lax.axis_size("tensor")
    share = block // nt
    rows = seqs * block
    d_at = lax.axis_index("dp")
    t_at = lax.axis_index("tensor")
    t_bits = list(range(nt.bit_length() - 1))
    d_bits = list(range(dp.bit_length() - 1))
    t_slots = slot_order(t_bits)
    d_slots = slot_order(d_bits)
    d_order = d_at ^ jnp.array(d_slots, jnp.int32)

    def token_slots(array):
        return jnp.stack(
            [lax.dynamic_slice_in_dim(array, (t_at ^ k) * share, share, 1) for k in t_slots]
        )

    def token_order(array):
        where = jnp.array([t_slots.index(k) for k in range(nt)], jnp.int32)
        return jnp.concatenate(
            [
                lax.dynamic_index_in_dim(array, where[t_at ^ j], 0, keepdims=False)
                for j in range(nt)
            ],
            1,
        )

    def sum_shares(keep, send):
        for at, bit in enumerate(t_bits):
            total = keep.astype(F32) + swap(send, "tensor", 1 << bit).astype(F32)
            if at + 1 < len(t_bits):
                half = total.shape[0] // 2
                keep, send = total[:half], total[half:].astype(BF16)
        return total

    def gather_shares(array):
        for bit in reversed(t_bits):
            array = jnp.concatenate([array, swap(array, "tensor", 1 << bit)], 0)
        return array

    def summed_rows(left, right):
        half = left.shape[0] // 2
        send = dot(left[half:], right).astype(BF16)
        got = swap(send, "dp", 1 << d_bits[0])
        keep = dot(left[:half], right)
        for bit in d_bits[1:]:
            half = half // 2
            send = (keep[half:] + got[half:].astype(F32)).astype(BF16)
            keep = keep[:half] + got[:half].astype(F32)
            got = swap(send, "dp", 1 << bit)
        return keep + got.astype(F32)

    positions = d_at * block + jnp.arange(block)
    cosine, sine = rope_tables(positions, hd)
    cos_q = jnp.concatenate([cosine] * 4, 1)
    sin_q = jnp.concatenate([-sine, sine] * 2, 1)
    ones = jnp.ones((block, hd), F32)
    cos_kv = jnp.concatenate([cosine, cosine, ones], 1)
    sin_kv = jnp.concatenate([-sine, sine, 0.0 * ones], 1)
    counts = jnp.stack([jnp.sum((seg_ids == v).astype(F32), axis=1) for v in range(3)], 1)
    counts = jnp.pad(counts[:, None, :], ((0, 0), (0, PAD - 1), (0, kv_width - 3))).astype(BF16)
    keyval_weight = w_keyval.reshape(width, kv_width)
    first_normed, keyval = norm_keyval(
        tokens, norm1_gain, keyval_weight, counts, cos_kv, sin_kv, hd // 2
    )
    keyval_all = lax.all_gather(keyval, "dp", axis=0)
    query = project_query(first_normed, w_query, cos_q, sin_q, hd // 2)

    cot_slots = token_slots(cotangent)
    d_ffn = (RESID * cot_slots.astype(F32)).astype(BF16).reshape(rows, width)
    d_ffn_t = transposed_slots(d_ffn, d_order)
    first_normed_t = transposed_slots(first_normed.reshape(rows, width), d_order)
    xf_share = lax.dynamic_slice_in_dim(tokens, t_at * share, share, 1).astype(F32)

    before = jnp.sum(keyval_all[:, :, block, :3].astype(F32), axis=0).astype(jnp.int32)
    doc_start = jnp.sum(
        jnp.where(seg_ids[:, :, None] > jnp.arange(3), before[:, None, :], 0), axis=2
    )
    start = doc_start[:, 0] // block
    clear = jnp.clip((doc_start[:, -1] + block - 1) // block, start, d_at)
    where = jnp.array([d_slots.index(k) for k in range(dp)], jnp.int32)
    slot_of = where[d_at ^ jnp.arange(dp)]
    scalars = jnp.concatenate([d_at[None].astype(jnp.int32), start, clear, slot_of])
    doc_start = doc_start[:, None, :]
    attended, lse = attend(query, keyval_all, doc_start, scalars, kv_local, hd)

    att_slots = token_slots(attended)
    half = nt // 2
    mixed_send = dot(att_slots[half:], w_out, (((3,), (0,)), ((), ()))).astype(BF16)
    mixed_keep = dot(att_slots[:half], w_out, (((3,), (0,)), ((), ())))
    mixed = sum_shares(mixed_keep, mixed_send)[0]
    resid = xf_share + RESID * mixed
    scale2 = lax.rsqrt(jnp.mean(resid * resid, axis=-1, keepdims=True) + EPS)
    second_normed = (resid * scale2 * norm2_gain).astype(BF16)
    second_all = gather_shares(second_normed[None]).reshape(rows, width)
    hidden, d_gate, d_up, ffn_keep, ffn_send, d_keep, d_send = feed_forward(
        second_all, d_ffn, w_gate, w_up, w_down
    )
    halves = (half, seqs, share, width)
    d_norm2 = sum_shares(d_keep.reshape(halves), d_send.reshape(halves))[0]
    second_t = transposed_slots(second_all, d_order)
    grad_down = summed_rows(d_ffn_t, hidden).T
    grad_gate = summed_rows(second_t, d_gate)
    grad_up = summed_rows(second_t, d_up)
    ffn = sum_shares(ffn_keep.reshape(halves), ffn_send.reshape(halves))[0]
    layer_out = (resid + RESID * ffn).astype(BF16)

    d_out = cot_slots[0].astype(F32)
    scaled = norm2_gain * d_norm2
    d_resid = (
        d_out
        + scale2 * scaled
        - resid * scale2**3 * jnp.mean(scaled * resid, axis=-1, keepdims=True)
    )
    d_mixed = gather_shares((RESID * d_resid).astype(BF16)[None])
    d_att = token_order(dot(d_mixed, w_out, (((3,), (1,)), ((), ()))).astype(BF16))
    d_mixed = d_mixed.reshape(rows, width)
    d_query, d_keyval = attend_back(
        query, keyval_all, doc_start, attended, d_att, lse, cos_q, sin_q, scalars, kv_local, hd
    )
    grad_outproj = summed_rows(
        transposed_slots(d_mixed, d_order), att_slots.reshape(rows, q_width)
    ).T
    grad_query = summed_rows(first_normed_t, d_query.reshape(rows, q_width))
    for bit in d_bits:
        part = d_keyval.shape[0] // 2
        d_keyval = d_keyval[:part].astype(F32) + swap(
            d_keyval[part:].astype(BF16), "dp", 1 << bit
        ).astype(F32)
    d_keyval = d_keyval[0].reshape(seqs, block, kv_local, 2 * hd)
    first = d_keyval[..., : hd // 2]
    second = d_keyval[..., hd // 2 : hd]
    cosine = cosine[:, None, :]
    sine = sine[:, None, :]
    d_keyval = (
        jnp.concatenate(
            [first * cosine + second * sine, second * cosine - first * sine, d_keyval[..., hd:]], -1
        )
        .astype(BF16)
        .reshape(seqs, block, kv_width)
    )
    grad_keyval = summed_rows(first_normed_t, d_keyval.reshape(rows, kv_width))
    dq_slots = token_slots(d_query)
    dkv_slots = token_slots(d_keyval)
    contract = (((3,), (1,)), ((), ()))

    def back(at):
        return dot(dq_slots[at], w_query, contract) + dot(dkv_slots[at], keyval_weight, contract)

    d_norm1 = sum_shares(back(slice(0, half)), back(slice(half, nt)).astype(BF16))[0]
    scale1 = lax.rsqrt(jnp.mean(xf_share * xf_share, axis=-1, keepdims=True) + EPS)
    scaled = norm1_gain * d_norm1
    grad_tokens = (
        d_resid
        + scale1 * scaled
        - xf_share * scale1**3 * jnp.mean(scaled * xf_share, axis=-1, keepdims=True)
    )

    piece = width // dp

    def own_rows(array):
        return lax.dynamic_slice_in_dim(array, d_at * piece, piece, 0).astype(F32)

    def gain_share(parts, gain):
        total = sum(jnp.sum(own_rows(w) * g, axis=1) for w, g in parts)
        total = (total / own_rows(gain)).reshape(nt, piece // nt)
        total = jnp.stack(
            [lax.dynamic_index_in_dim(total, t_at ^ k, 0, keepdims=False) for k in t_slots]
        )
        for bit in t_bits:
            part = total.shape[0] // 2
            total = total[:part] + swap(total[part:], "tensor", 1 << bit)
        return total[0]

    grad_gain1 = gain_share([(w_query, grad_query), (keyval_weight, grad_keyval)], norm1_gain)
    grad_gain2 = gain_share([(w_gate, grad_gate), (w_up, grad_up)], norm2_gain)
    return (
        layer_out,
        grad_tokens,
        grad_gain1,
        grad_query,
        grad_keyval.reshape(piece, kv_local, 2 * hd),
        grad_outproj,
        grad_gain2,
        grad_gate,
        grad_up,
        grad_down,
    )


def solution(mesh):
    placed = (
        P(None, "dp", None),
        P(None, "dp"),
        P(),
        P(None, "tensor"),
        P(None, "tensor", None),
        P("tensor", None),
        P(),
        P(None, "tensor"),
        P(None, "tensor"),
        P("tensor", None),
        P(None, "dp", None),
    )
    return jax.shard_map(
        body,
        mesh=mesh,
        in_specs=placed,
        out_specs=(
            P(None, ("dp", "tensor"), None),
            P(None, ("dp", "tensor"), None),
            P(("dp", "tensor")),
            P("dp", "tensor"),
            P("dp", "tensor", None),
            P("tensor", "dp"),
            P(("dp", "tensor")),
            P("dp", "tensor"),
            P("dp", "tensor"),
            P("tensor", "dp"),
        ),
        check_vma=False,
    )
```

time: 1520 us -> 895 us (0.59)
  waiting for transfers between devices: 976 us -> 491 us
  matrix products: 273 us -> 59.7 us
  Pallas kernels: 0 us -> 117 us
  starting transfers between devices: 1.68 us -> 80.2 us
  blocking collectives: 75.6 us -> 0 us
  loops' own time: 47.8 us -> 0 us
    reduce_scatter x7 -> x0, waiting for transfers between devices: 602 us -> none  [the longest x1 150 us: body(): lax.psum_scatter(grad_down.astype(jnp.bfloat16), 'dp', scatter_dimension=...]
    ppermute x0 -> x37, waiting for transfers between devices: none -> 432 us  [swap(): return lax.ppermute(value, axis, [(i, i ^ distance) for i in range(size)])]
    psum x3 -> x0, waiting for transfers between devices: 345 us -> none  [the longest x1 120 us: body(): d_norm2_full = lax.psum(d_norm2, 'tensor')]
    dot_general x60 -> x19, matrix products: 273 us -> 59.7 us  [the longest x12 44.2 us: dot(): return jnp.dot(a, b, preferred_element_type=F32)]
    pallas_call x0 -> x9, Pallas kernels: none -> 117 us  [the longest x1 55.6 us: feed_forward(): pl.pallas_call(kernel, grid=(steps,), in_specs=[whole(rows), whole(rows),...]
    ppermute x0 -> x37, starting transfers between devices: none -> 80.2 us  [swap(): return lax.ppermute(value, axis, [(i, i ^ distance) for i in range(size)])]
    another operation x2 -> x0, loops' own time: 47.8 us -> none  [the longest x1 24.1 us: body(): d_query, d_keyval = lax.map(attend_back, pairs)]
    unnamed x1 -> x0, blocking collectives: 42.9 us -> none
  transfers between devices with their start and end apart: 11 -> 38, of which waited for: 11 -> 19; matrix products, arithmetic and copies ran while one was open for 8% -> 16% of each run, Pallas kernels for 0% -> 5%
where the time goes in v1:
time: 895 us; the launch traced here: 887 us
  waiting for transfers between devices  491 us (55%)
  Pallas kernels  117 us (13%)
  other arithmetic  85.6 us (10%)
  starting transfers between devices  80.2 us (9%)
  matrix products  59.7 us (7%)
  local copies, waits for them, and re-layouts  30.5 us (3%)
  between operations  23.1 us (3%)
    ppermute x37, waiting for transfers between devices, swap(): return lax.ppermute(value, axis, [(i, i ^ distance) for i in range(size)])  432 us
    ppermute x37, starting transfers between devices, swap(): return lax.ppermute(value, axis, [(i, i ^ distance) for i in range(size)])  80.2 us
    all_gather x1, waiting for transfers between devices, body(): keyval_all = lax.all_gather(keyval, 'dp', axis=0)  58.9 us
    pallas_call x1, Pallas kernels, feed_forward(): pl.pallas_call(kernel, grid=(steps,), in_specs=[whole(rows), whole(rows),...  55.6 us
    dot_general x12, matrix products, dot(): return jnp.dot(a, b, preferred_element_type=F32)  44.2 us
    convert_element_type x12, other arithmetic, summed_rows(): send = (keep[half:] + got[half:].astype(F32)).astype(BF16)  36.3 us
    pallas_call x4, Pallas kernels, transposed_slots(): pl.pallas_call(kernel, grid_spec=pltpu.PrefetchScalarGridSpec(num_scalar_...  29.6 us
  transfers between devices with their start and end apart: 38, of which 19 were waited for; matrix products, arithmetic and copies ran while one was open for 16% of the time, Pallas kernels for 5%

profile of v1, /device:TPU:0, one launch (start us, length us, event | category | flops | bytes accessed | tf_op | source)
XLA Modules:
  0.0 887.2 jit_solution(12891469076790247644)
XLA Ops:
  19.9 6.0 project_query.1.q_ref
  25.8 58.9 %all-gather.3.cloned.1.call-done = bf16[24,272,256]{2,1,0:T(8,128)(2,1)} async-done(((bf16[3,272,256]{2,1,0:T(8,128)(2,1)}), bf16[24,272,256]{2,1,0:T(8,128)(2,1)}) %all-gather.3.cloned.1.call-update) | async-done | bytes 3342352 | tf_op jit(solution)/shard_map/all_gather | solution.py:505
  87.1 8.2 attend.1
  103.7 18.1 %collective-permute-done.1 = bf16[1,3,64,2048]{3,2,1,0:T(8,128)(2,1)S(1)} collective-permute-done((bf16[1,3,64,2048]{3,2,1,0:T(8,128)(2,1)S(1)}, bf16[1,3,64,2048]{3,2,1,0:T(8,128)(2,1)S(1)}, u32[]{:S(2)}, u32[]{:S(2)}) %collective-permute-start.1) | collective-permute-done | bytes 786464 | tf_op jit(solution)/shard_map/ppermute | solution.py:46
  125.9 17.3 %collective-permute-done.2 = bf16[1,3,64,2048]{3,2,1,0:T(8,128)(2,1)S(1)} collective-permute-done((bf16[1,3,64,2048]{3,2,1,0:T(8,128)(2,1)S(1)}, bf16[1,3,64,2048]{3,2,1,0:T(8,128)(2,1)S(1)}, u32[]{:S(2)}, u32[]{:S(2)}) %collective-permute-start.2) | collective-permute-done | bytes 786464 | tf_op jit(solution)/shard_map/ppermute | solution.py:46
  160.3 7.4 transposed_slots.7
  167.6 7.5 transposed_slots.4
  183.1 7.4 transposed_slots.6
  190.5 55.6 %feed_forward.1 = (bf16[768,2048]{1,0:T(8,128)(2,1)}, bf16[768,2048]{1,0:T(8,128)(2,1)}, bf16[768,2048]{1,0:T(8,128)(2,1)}, bf16[384,2048]{1,0:T(8,128)(2,1)}, b...) custom-call(bf16[768,2048]{1,0:T(8,128)(2,1)} %bitcast.164, ...), custom_call_target="tpu_custom_call" | custom-call | flops 38654705664 | bytes 34603008 | tf_op jit(solution)/shard_map/feed_forward/pallas_call | solution.py:379
  246.7 5.7 convolution_convert_fusion
  276.2 10.0 %collective-permute-done.7 = bf16[1,3,64,2048]{3,2,1,0:T(8,128)(2,1)S(1)} collective-permute-done((bf16[1,3,64,2048]{3,2,1,0:T(8,128)(2,1)S(1)}, bf16[1,3,64,2048]{3,2,1,0:T(8,128)(2,1)S(1)}, u32[]{:S(2)}, u32[]{:S(2)}) %collective-permute-start.7) | collective-permute-done | bytes 786464 | tf_op jit(solution)/shard_map/ppermute | solution.py:46
  286.6 15.7 %collective-permute-done.5 = bf16[1,3,64,2048]{3,2,1,0:T(8,128)(2,1)S(1)} collective-permute-done((bf16[1,3,64,2048]{3,2,1,0:T(8,128)(2,1)S(1)}, bf16[1,3,64,2048]{3,2,1,0:T(8,128)(2,1)S(1)}, u32[]{:S(2)}, u32[]{:S(2)}) %collective-permute-start.5) | collective-permute-done | bytes 786464 | tf_op jit(solution)/shard_map/ppermute | solution.py:46
  307.2 7.6 fusion.48
  314.8 5.7 fusion.50
  324.9 22.8 %collective-permute-done.34 = bf16[1024,2048]{1,0:T(8,128)(2,1)} collective-permute-done((bf16[1024,2048]{1,0:T(8,128)(2,1)S(1)}, bf16[1024,2048]{1,0:T(8,128)(2,1)}, u32[]{:S(2)}, u32[]{:S(2)}) %collective-permute-start.34) | collective-permute-done | bytes 4194336 | tf_op jit(solution)/shard_map/ppermute | solution.py:46
  352.9 8.9 collective-permute-start.35
  361.7 75.8 %collective-permute-done.26 = bf16[1024,2048]{1,0:T(8,128)(2,1)} collective-permute-done((bf16[1024,2048]{1,0:T(8,128)(2,1)}, bf16[1024,2048]{1,0:T(8,128)(2,1)}, u32[]{:S(2)}, u32[]{:S(2)}) %collective-permute-start.26) | collective-permute-done | bytes 4194336 | tf_op jit(solution)/shard_map/ppermute | solution.py:46
  437.6 9.1 %fusion.2 = (bf16[512,2048]{1,0:T(8,128)(2,1)}, f32[512,2048]{1,0:T(8,128)}) fusion(f32[1024,2048]{1,0:T(8,128)} %fusion.50, bf16[1024,2048]{1,0:T(8,128)(2,1)} %collective-permute-done.26), kind=kLoop, calls=%fused_computation.9 | loop fusion | flops 5242880 | bytes 18874368 | tf_op jit(solution)/shard_map/convert_element_type | solution.py:487
  446.7 8.9 collective-permute-start.27
  455.6 71.6 %collective-permute-done.29 = bf16[1024,2048]{1,0:T(8,128)(2,1)} collective-permute-done((bf16[1024,2048]{1,0:T(8,128)(2,1)}, bf16[1024,2048]{1,0:T(8,128)(2,1)}, u32[]{:S(2)}, u32[]{:S(2)}) %collective-permute-start.29) | collective-permute-done | bytes 4194336 | tf_op jit(solution)/shard_map/ppermute | solution.py:46
  527.2 9.1 %fusion.1 = (bf16[512,2048]{1,0:T(8,128)(2,1)}, f32[512,2048]{1,0:T(8,128)}) fusion(f32[1024,2048]{1,0:T(8,128)} %fusion.48, bf16[1024,2048]{1,0:T(8,128)(2,1)} %collective-permute-done.29), kind=kLoop, calls=%fused_computation.6 | loop fusion | flops 5242880 | bytes 18874368 | tf_op jit(solution)/shard_map/convert_element_type | solution.py:487
  536.3 8.9 %collective-permute-start.30 = (bf16[512,2048]{1,0:T(8,128)(2,1)}, bf16[512,2048]{1,0:T(8,128)(2,1)}, u32[]{:S(2)}, u32[]{:S(2)}) collective-permute-start(bf16[512,2048]{1,0:T(8,128)(2,1)} %get-tuple-element.99), channel_id=1, source_target_pairs={{0,8},{4,12},{8,0},{12,4},{16,24},{20,28},{24,16},{28,20},{1,9},{5... | collective-permute-start | bytes 6291464 | tf_op jit(solution)/shard_map/ppermute | solution.py:46
  548.6 7.4 transposed_slots.5
  565.6 12.3 %attend_back.1 = (bf16[3,256,512]{2,1,0:T(8,128)(2,1)}, bf16[8,3,256,256]{3,2,1,0:T(8,128)(2,1)}) custom-call(s32[15]{0:T(128)} %pad_add_fusion.sc, bf16[3,256,512]{2,1,0:T(8,128)(2,1)} %project_query.1.q_ref, bf16[8,3,272,256]{3,2,1,0:T(8,128)(2,1)} %bitcast.183, s32[3,1,256]{2,1,0:T(1,128)} %broadcast_in_dim.49.doc_ref, ...), custom_call_target="tpu_custom_call" | custom-call | flops 16106127360 | bytes 6291456 | tf_op jit(solution)/shard_map/attend_back/pallas_call | solution.py:302
  592.8 16.9 %collective-permute-done.15 = bf16[1024,512]{0,1:T(8,128)(2,1)S(1)} collective-permute-done((bf16[1024,512]{0,1:T(8,128)(2,1)S(1)}, bf16[1024,512]{0,1:T(8,128)(2,1)S(1)}, u32[]{:S(2)}, u32[]{:S(2)}) %collective-permute-start.15) | collective-permute-done | bytes 1048608 | tf_op jit(solution)/shard_map/ppermute | solution.py:46
  609.7 9.2 %collective-permute-start.24 = (bf16[512,512]{1,0:T(8,128)(2,1)S(1)}, bf16[512,512]{1,0:T(8,128)(2,1)S(1)}, u32[]{:S(2)}, u32[]{:S(2)}) collective-permute-start(bf16[512,512]{1,0:T(8,128)(2,1)S(1)} %get-tuple-element.103), channel_id=1, source_target_pairs={{0,8},{4,12},{8,0},{12,4},{16,24},{20,28},{24,16},{28,20},{1,9},{5... | collective-permute-start | bytes 1572872 | tf_op jit(solution)/shard_map/ppermute | solution.py:46
  622.0 12.7 %collective-permute-start.36 = (bf16[256,2048]{1,0:T(8,128)(2,1)}, bf16[256,2048]{1,0:T(8,128)(2,1)}, u32[]{:S(2)}, u32[]{:S(2)}) collective-permute-start(bf16[256,2048]{1,0:T(8,128)(2,1)} %fusion.3), channel_id=1, source_target_pairs={{0,16},{4,20},{8,24},{12,28},{16,0},{20,4},{24,8},{28,12},{1,17},{... | collective-permute-start | bytes 3145736 | tf_op jit(solution)/shard_map/ppermute | solution.py:46
  637.3 21.6 %collective-permute-done.16 = bf16[512,512]{0,1:T(8,128)(2,1)S(1)} collective-permute-done((bf16[512,512]{0,1:T(8,128)(2,1)S(1)}, bf16[512,512]{0,1:T(8,128)(2,1)S(1)}, u32[]{:S(2)}, u32[]{:S(2)}) %collective-permute-start.16) | collective-permute-done | bytes 524320 | tf_op jit(solution)/shard_map/ppermute | solution.py:46
  668.3 94.3 %collective-permute-done.17 = bf16[256,512]{0,1:T(8,128)(2,1)S(1)} collective-permute-done((bf16[256,512]{0,1:T(8,128)(2,1)S(1)}, bf16[256,512]{0,1:T(8,128)(2,1)S(1)}, u32[]{:S(2)}, u32[]{:S(2)}) %collective-permute-start.17) | collective-permute-done | bytes 262176 | tf_op jit(solution)/shard_map/ppermute | solution.py:46
  762.8 27.2 %collective-permute-done.25 = bf16[256,512]{1,0:T(8,128)(2,1)S(1)} collective-permute-done((bf16[256,512]{1,0:T(8,128)(2,1)S(1)}, bf16[256,512]{1,0:T(8,128)(2,1)S(1)}, u32[]{:S(2)}, u32[]{:S(2)}) %collective-permute-start.25) | collective-permute-done | bytes 262176 | tf_op jit(solution)/shard_map/ppermute | solution.py:46
  825.2 7.9 collective-permute-done.18
  860.8 15.9 %collective-permute-done.22 = f32[1,64]{1,0:T(1,128)S(1)} collective-permute-done((f32[1,64]{1,0:T(1,128)S(1)}, f32[1,64]{1,0:T(1,128)S(1)}, u32[]{:S(2)}, u32[]{:S(2)}) %collective-permute-start.22) | collective-permute-done | bytes 288 | tf_op jit(solution)/shard_map/ppermute | solution.py:46
  (282 shorter events, 192.4 us)
Async XLA Ops:
  7.2 77.6 %all-gather.3.cloned.1.call-start = ((), (), s32[]{:S(2)}) async-start(), calls=%async_computation | async-start | bytes 3760128 | tf_op jit(solution)/shard_map/all_gather | solution.py:505
  102.2 19.6 %collective-permute-start.1 = (bf16[1,3,64,2048]{3,2,1,0:T(8,128)(2,1)S(1)}, bf16[1,3,64,2048]{3,2,1,0:T(8,128)(2,1)S(1)}, u32[]{:S(2)}, u32[]{:S(2)}) collective-permute-start(bf16[1,3,64,2048]{3,2,1,0:T(8,128)(2,1)S(1)} %slice.602), channel_id=1, source_target_pairs={{0,2},{1,3},{2,0},{3,1},{4,6},{5,7},{6,4},{7,5},{8,10},{9,11},{10,... | collective-permute-start | bytes 2359304 | tf_op jit(solution)/shard_map/ppermute | solution.py:46
  124.3 18.8 %collective-permute-start.2 = (bf16[1,3,64,2048]{3,2,1,0:T(8,128)(2,1)S(1)}, bf16[1,3,64,2048]{3,2,1,0:T(8,128)(2,1)S(1)}, u32[]{:S(2)}, u32[]{:S(2)}) collective-permute-start(bf16[1,3,64,2048]{3,2,1,0:T(8,128)(2,1)S(1)} %fusion.68), channel_id=1, source_target_pairs={{0,2},{1,3},{2,0},{3,1},{4,6},{5,7},{6,4},{7,5},{8,10},{9,11},{10,... | collective-permute-start | bytes 2359304 | tf_op jit(solution)/shard_map/ppermute | solution.py:46
  145.3 34.4 %collective-permute-start.3 = (bf16[2,3,64,2048]{3,2,1,0:T(8,128)(2,1)}, bf16[2,3,64,2048]{3,2,1,0:T(8,128)(2,1)}, u32[]{:S(2)}, u32[]{:S(2)}) collective-permute-start(bf16[2,3,64,2048]{3,2,1,0:T(8,128)(2,1)} %pad_maximum_fusion.2), channel_id=1, source_target_pairs={{0,1},{1,0},{2,3},{3,2},{4,5},{5,4},{6,7},{7,6},{8,9},{9,8},{10,11... | collective-permute-start | bytes 4718600 | tf_op jit(solution)/shard_map/ppermute | solution.py:46
  246.1 21.2 %collective-permute-start.4 = (bf16[2,3,64,2048]{3,2,1,0:T(8,128)(2,1)}, bf16[2,3,64,2048]{3,2,1,0:T(8,128)(2,1)S(1)}, u32[]{:S(2)}, u32[]{:S(2)}) collective-permute-start(bf16[2,3,64,2048]{3,2,1,0:T(8,128)(2,1)} %bitcast.184), channel_id=1, source_target_pairs={{0,1},{1,0},{2,3},{3,2},{4,5},{5,4},{6,7},{7,6},{8,9},{9,8},{10,11... | collective-permute-start | bytes 4718600 | tf_op jit(solution)/shard_map/ppermute | solution.py:46
  246.6 18.4 %collective-permute-start.6 = (bf16[2,3,64,2048]{3,2,1,0:T(8,128)(2,1)}, bf16[2,3,64,2048]{3,2,1,0:T(8,128)(2,1)S(1)}, u32[]{:S(2)}, u32[]{:S(2)}) collective-permute-start(bf16[2,3,64,2048]{3,2,1,0:T(8,128)(2,1)} %bitcast.185), channel_id=1, source_target_pairs={{0,1},{1,0},{2,3},{3,2},{4,5},{5,4},{6,7},{7,6},{8,9},{9,8},{10,11... | collective-permute-start | bytes 4718600 | tf_op jit(solution)/shard_map/ppermute | solution.py:46
  252.5 95.2 %collective-permute-start.34 = (bf16[1024,2048]{1,0:T(8,128)(2,1)S(1)}, bf16[1024,2048]{1,0:T(8,128)(2,1)}, u32[]{:S(2)}, u32[]{:S(2)}) collective-permute-start(bf16[1024,2048]{1,0:T(8,128)(2,1)S(1)} %convolution_convert_fusion), channel_id=1, source_target_pairs={{0,4},{4,0},{8,12},{12,8},{16,20},{20,16},{24,28},{28,24},{1,5},{5... | collective-permute-start | bytes 12582920 | tf_op jit(solution)/shard_map/ppermute | solution.py:46
  261.6 176.0 %collective-permute-start.26 = (bf16[1024,2048]{1,0:T(8,128)(2,1)}, bf16[1024,2048]{1,0:T(8,128)(2,1)}, u32[]{:S(2)}, u32[]{:S(2)}) collective-permute-start(bf16[1024,2048]{1,0:T(8,128)(2,1)} %convolution_convert_fusion.2), channel_id=1, source_target_pairs={{0,4},{4,0},{8,12},{12,8},{16,20},{20,16},{24,28},{28,24},{1,5},{5... | collective-permute-start | bytes 12582920 | tf_op jit(solution)/shard_map/ppermute | solution.py:46
  265.8 20.4 %collective-permute-start.7 = (bf16[1,3,64,2048]{3,2,1,0:T(8,128)(2,1)S(1)}, bf16[1,3,64,2048]{3,2,1,0:T(8,128)(2,1)S(1)}, u32[]{:S(2)}, u32[]{:S(2)}) collective-permute-start(bf16[1,3,64,2048]{3,2,1,0:T(8,128)(2,1)S(1)} %slice.600), channel_id=1, source_target_pairs={{0,2},{1,3},{2,0},{3,1},{4,6},{5,7},{6,4},{7,5},{8,10},{9,11},{10,... | collective-permute-start | bytes 2359304 | tf_op jit(solution)/shard_map/ppermute | solution.py:46
  268.0 34.3 %collective-permute-start.5 = (bf16[1,3,64,2048]{3,2,1,0:T(8,128)(2,1)S(1)}, bf16[1,3,64,2048]{3,2,1,0:T(8,128)(2,1)S(1)}, u32[]{:S(2)}, u32[]{:S(2)}) collective-permute-start(bf16[1,3,64,2048]{3,2,1,0:T(8,128)(2,1)S(1)} %slice.601), channel_id=1, source_target_pairs={{0,2},{1,3},{2,0},{3,1},{4,6},{5,7},{6,4},{7,5},{8,10},{9,11},{10,... | collective-permute-start | bytes 2359304 | tf_op jit(solution)/shard_map/ppermute | solution.py:46
  274.3 252.9 %collective-permute-start.29 = (bf16[1024,2048]{1,0:T(8,128)(2,1)}, bf16[1024,2048]{1,0:T(8,128)(2,1)}, u32[]{:S(2)}, u32[]{:S(2)}) collective-permute-start(bf16[1024,2048]{1,0:T(8,128)(2,1)} %convolution_convert_fusion.1), channel_id=1, source_target_pairs={{0,4},{4,0},{8,12},{12,8},{16,20},{20,16},{24,28},{28,24},{1,5},{5... | collective-permute-start | bytes 12582920 | tf_op jit(solution)/shard_map/ppermute | solution.py:46
  305.8 18.9 %collective-permute-start.8 = (bf16[1,3,64,2048]{3,2,1,0:T(8,128)(2,1)S(1)}, bf16[1,3,64,2048]{3,2,1,0:T(8,128)(2,1)S(1)}, u32[]{:S(2)}, u32[]{:S(2)}) collective-permute-start(bf16[1,3,64,2048]{3,2,1,0:T(8,128)(2,1)S(1)} %get-tuple-element.91), channel_id=1, source_target_pairs={{0,2},{1,3},{2,0},{3,1},{4,6},{5,7},{6,4},{7,5},{8,10},{9,11},{10,... | collective-permute-start | bytes 2359304 | tf_op jit(solution)/shard_map/ppermute | solution.py:46
  324.8 220.4 %collective-permute-start.9 = (bf16[2,3,64,2048]{3,2,1,0:T(8,128)(2,1)S(1)}, bf16[2,3,64,2048]{3,2,1,0:T(8,128)(2,1)}, u32[]{:S(2)}, u32[]{:S(2)}) collective-permute-start(bf16[2,3,64,2048]{3,2,1,0:T(8,128)(2,1)S(1)} %pad_maximum_fusion.3), channel_id=1, source_target_pairs={{0,1},{1,0},{2,3},{3,2},{4,5},{5,4},{6,7},{7,6},{8,9},{9,8},{10,11... | collective-permute-start | bytes 4718600 | tf_op jit(solution)/shard_map/ppermute | solution.py:46
  352.9 266.4 %collective-permute-start.35 = (bf16[512,2048]{1,0:T(8,128)(2,1)}, bf16[512,2048]{1,0:T(8,128)(2,1)}, u32[]{:S(2)}, u32[]{:S(2)}) collective-permute-start(bf16[512,2048]{1,0:T(8,128)(2,1)} %get-tuple-element.97), channel_id=1, source_target_pairs={{0,8},{4,12},{8,0},{12,4},{16,24},{20,28},{24,16},{28,20},{1,9},{5... | collective-permute-start | bytes 6291464 | tf_op jit(solution)/shard_map/ppermute | solution.py:46
  446.7 175.3 %collective-permute-start.27 = (bf16[512,2048]{1,0:T(8,128)(2,1)}, bf16[512,2048]{1,0:T(8,128)(2,1)}, u32[]{:S(2)}, u32[]{:S(2)}) collective-permute-start(bf16[512,2048]{1,0:T(8,128)(2,1)} %get-tuple-element.101), channel_id=1, source_target_pairs={{0,8},{4,12},{8,0},{12,4},{16,24},{20,28},{24,16},{28,20},{1,9},{5... | collective-permute-start | bytes 6291464 | tf_op jit(solution)/shard_map/ppermute | solution.py:46
  536.3 127.1 %collective-permute-start.30 = (bf16[512,2048]{1,0:T(8,128)(2,1)}, bf16[512,2048]{1,0:T(8,128)(2,1)}, u32[]{:S(2)}, u32[]{:S(2)}) collective-permute-start(bf16[512,2048]{1,0:T(8,128)(2,1)} %get-tuple-element.99), channel_id=1, source_target_pairs={{0,8},{4,12},{8,0},{12,4},{16,24},{20,28},{24,16},{28,20},{1,9},{5... | collective-permute-start | bytes 6291464 | tf_op jit(solution)/shard_map/ppermute | solution.py:46
  559.5 31.4 %collective-permute-start.23 = (bf16[1024,512]{1,0:T(8,128)(2,1)}, bf16[1024,512]{1,0:T(8,128)(2,1)}, u32[]{:S(2)}, u32[]{:S(2)}) collective-permute-start(bf16[1024,512]{1,0:T(8,128)(2,1)} %fusion.40), channel_id=1, source_target_pairs={{0,4},{4,0},{8,12},{12,8},{16,20},{20,16},{24,28},{28,24},{1,5},{5... | collective-permute-start | bytes 3145736 | tf_op jit(solution)/shard_map/ppermute | solution.py:46
  580.7 29.0 %collective-permute-start.15 = (bf16[1024,512]{0,1:T(8,128)(2,1)S(1)}, bf16[1024,512]{0,1:T(8,128)(2,1)S(1)}, u32[]{:S(2)}, u32[]{:S(2)}) collective-permute-start(bf16[1024,512]{0,1:T(8,128)(2,1)S(1)} %convolution_convert_fusion.4), channel_id=1, source_target_pairs={{0,4},{4,0},{8,12},{12,8},{16,20},{20,16},{24,28},{28,24},{1,5},{5... | collective-permute-start | bytes 3145736 | tf_op jit(solution)/shard_map/ppermute | solution.py:46
  590.9 68.1 %collective-permute-start.10 = (bf16[4,3,256,256]{3,2,1,0:T(8,128)(2,1)S(1)}, bf16[4,3,256,256]{3,2,1,0:T(8,128)(2,1)S(1)}, u32[]{:S(2)}, u32[]{:S(2)}) collective-permute-start(bf16[4,3,256,256]{3,2,1,0:T(8,128)(2,1)S(1)} %slice.280), channel_id=1, source_target_pairs={{0,4},{4,0},{8,12},{12,8},{16,20},{20,16},{24,28},{28,24},{1,5},{5... | collective-permute-start | bytes 4718600 | tf_op jit(solution)/shard_map/ppermute | solution.py:46
  609.7 58.5 %collective-permute-start.24 = (bf16[512,512]{1,0:T(8,128)(2,1)S(1)}, bf16[512,512]{1,0:T(8,128)(2,1)S(1)}, u32[]{:S(2)}, u32[]{:S(2)}) collective-permute-start(bf16[512,512]{1,0:T(8,128)(2,1)S(1)} %get-tuple-element.103), channel_id=1, source_target_pairs={{0,8},{4,12},{8,0},{12,4},{16,24},{20,28},{24,16},{28,20},{1,9},{5... | collective-permute-start | bytes 1572872 | tf_op jit(solution)/shard_map/ppermute | solution.py:46
  619.3 39.6 %collective-permute-start.16 = (bf16[512,512]{0,1:T(8,128)(2,1)S(1)}, bf16[512,512]{0,1:T(8,128)(2,1)S(1)}, u32[]{:S(2)}, u32[]{:S(2)}) collective-permute-start(bf16[512,512]{0,1:T(8,128)(2,1)S(1)} %get-tuple-element.105), channel_id=1, source_target_pairs={{0,8},{4,12},{8,0},{12,4},{16,24},{20,28},{24,16},{28,20},{1,9},{5... | collective-permute-start | bytes 1572872 | tf_op jit(solution)/shard_map/ppermute | solution.py:46
  622.0 173.3 %collective-permute-start.36 = (bf16[256,2048]{1,0:T(8,128)(2,1)}, bf16[256,2048]{1,0:T(8,128)(2,1)}, u32[]{:S(2)}, u32[]{:S(2)}) collective-permute-start(bf16[256,2048]{1,0:T(8,128)(2,1)} %fusion.3), channel_id=1, source_target_pairs={{0,16},{4,20},{8,24},{12,28},{16,0},{20,4},{24,8},{28,12},{1,17},{... | collective-permute-start | bytes 3145736 | tf_op jit(solution)/shard_map/ppermute | solution.py:46
  658.9 140.0 %collective-permute-start.28 = (bf16[256,2048]{1,0:T(8,128)(2,1)}, bf16[256,2048]{1,0:T(8,128)(2,1)}, u32[]{:S(2)}, u32[]{:S(2)}) collective-permute-start(bf16[256,2048]{1,0:T(8,128)(2,1)} %fusion.8), channel_id=1, source_target_pairs={{0,16},{4,20},{8,24},{12,28},{16,0},{20,4},{24,8},{28,12},{1,17},{... | collective-permute-start | bytes 3145736 | tf_op jit(solution)/shard_map/ppermute | solution.py:46
  659.0 103.6 %collective-permute-start.17 = (bf16[256,512]{0,1:T(8,128)(2,1)S(1)}, bf16[256,512]{0,1:T(8,128)(2,1)S(1)}, u32[]{:S(2)}, u32[]{:S(2)}) collective-permute-start(bf16[256,512]{0,1:T(8,128)(2,1)S(1)} %fusion.74), channel_id=1, source_target_pairs={{0,16},{4,20},{8,24},{12,28},{16,0},{20,4},{24,8},{28,12},{1,17},{... | collective-permute-start | bytes 786440 | tf_op jit(solution)/shard_map/ppermute | solution.py:46
  663.4 128.6 %collective-permute-start.11 = (bf16[2,3,256,256]{3,2,1,0:T(8,128)(2,1)}, bf16[2,3,256,256]{3,2,1,0:T(8,128)(2,1)}, u32[]{:S(2)}, u32[]{:S(2)}) collective-permute-start(bf16[2,3,256,256]{3,2,1,0:T(8,128)(2,1)} %slice.599), channel_id=1, source_target_pairs={{0,8},{4,12},{8,0},{12,4},{16,24},{20,28},{24,16},{28,20},{1,9},{5... | collective-permute-start | bytes 2359304 | tf_op jit(solution)/shard_map/ppermute | solution.py:46
  668.2 137.5 %collective-permute-start.31 = (bf16[256,2048]{1,0:T(8,128)(2,1)}, bf16[256,2048]{1,0:T(8,128)(2,1)}, u32[]{:S(2)}, u32[]{:S(2)}) collective-permute-start(bf16[256,2048]{1,0:T(8,128)(2,1)} %fusion.6), channel_id=1, source_target_pairs={{0,16},{4,20},{8,24},{12,28},{16,0},{20,4},{24,8},{28,12},{1,17},{... | collective-permute-start | bytes 3145736 | tf_op jit(solution)/shard_map/ppermute | solution.py:46
  762.6 27.4 %collective-permute-start.25 = (bf16[256,512]{1,0:T(8,128)(2,1)S(1)}, bf16[256,512]{1,0:T(8,128)(2,1)S(1)}, u32[]{:S(2)}, u32[]{:S(2)}) collective-permute-start(bf16[256,512]{1,0:T(8,128)(2,1)S(1)} %fusion.70), channel_id=1, source_target_pairs={{0,16},{4,20},{8,24},{12,28},{16,0},{20,4},{24,8},{28,12},{1,17},{... | collective-permute-start | bytes 786440 | tf_op jit(solution)/shard_map/ppermute | solution.py:46
  795.3 17.1 %collective-permute-start.12 = (bf16[1,3,256,256]{3,2,1,0:T(8,128)(2,1)S(1)}, bf16[1,3,256,256]{3,2,1,0:T(8,128)(2,1)S(1)}, u32[]{:S(2)}, u32[]{:S(2)}) collective-permute-start(bf16[1,3,256,256]{3,2,1,0:T(8,128)(2,1)S(1)} %slice.603), channel_id=1, source_target_pairs={{0,16},{4,20},{8,24},{12,28},{16,0},{20,4},{24,8},{28,12},{1,17},{... | collective-permute-start | bytes 1179656 | tf_op jit(solution)/shard_map/ppermute | solution.py:46
  837.3 15.4 %collective-permute-start.13 = (bf16[2,3,64,2048]{3,2,1,0:T(8,128)(2,1)}, bf16[2,3,64,2048]{3,2,1,0:T(8,128)(2,1)}, u32[]{:S(2)}, u32[]{:S(2)}) collective-permute-start(bf16[2,3,64,2048]{3,2,1,0:T(8,128)(2,1)} %add_convert_fusion), channel_id=1, source_target_pairs={{0,1},{1,0},{2,3},{3,2},{4,5},{5,4},{6,7},{7,6},{8,9},{9,8},{10,11... | collective-permute-start | bytes 4718600 | tf_op jit(solution)/shard_map/ppermute | solution.py:46
  857.0 20.7 %collective-permute-start.14 = (bf16[1,3,64,2048]{3,2,1,0:T(8,128)(2,1)S(1)}, bf16[1,3,64,2048]{3,2,1,0:T(8,128)(2,1)S(1)}, u32[]{:S(2)}, u32[]{:S(2)}) collective-permute-start(bf16[1,3,64,2048]{3,2,1,0:T(8,128)(2,1)S(1)} %slice.598), channel_id=1, source_target_pairs={{0,2},{1,3},{2,0},{3,1},{4,6},{5,7},{6,4},{7,5},{8,10},{9,11},{10,... | collective-permute-start | bytes 2359304 | tf_op jit(solution)/shard_map/ppermute | solution.py:46
  858.6 18.1 %collective-permute-start.22 = (f32[1,64]{1,0:T(1,128)S(1)}, f32[1,64]{1,0:T(1,128)S(1)}, u32[]{:S(2)}, u32[]{:S(2)}) collective-permute-start(f32[1,64]{1,0:T(1,128)S(1)} %slice.309), channel_id=1, source_target_pairs={{0,2},{1,3},{2,0},{3,1},{4,6},{5,7},{6,4},{7,5},{8,10},{9,11},{10,... | collective-permute-start | bytes 776 | tf_op jit(solution)/shard_map/ppermute | solution.py:46
  859.2 18.0 %collective-permute-start.33 = (f32[1,64]{1,0:T(1,128)S(1)}, f32[1,64]{1,0:T(1,128)S(1)}, u32[]{:S(2)}, u32[]{:S(2)}) collective-permute-start(f32[1,64]{1,0:T(1,128)S(1)} %slice.339), channel_id=1, source_target_pairs={{0,2},{1,3},{2,0},{3,1},{4,6},{5,7},{6,4},{7,5},{8,10},{9,11},{10,... | collective-permute-start | bytes 776 | tf_op jit(solution)/shard_map/ppermute | solution.py:46
  (59 other events, 993.0 us)
Sparse Core Ops, SparseCore 0:
  19.3 65.4 all-gather.2

commit v2 on v1

v2 whole, which is shorter than its diff:
```python
import math

import jax
import jax.numpy as jnp
from jax import lax
from jax.experimental import pallas as pl
from jax.experimental.pallas import tpu as pltpu
from jax.sharding import PartitionSpec as P

EPS = 1e-05
SCALE = 0.015625
RESID = 0.22
THETA = 10000000.0
NEG = -1e30
PAD = 16
VMEM = 56 * 1024 * 1024
F32 = jnp.float32
BF16 = jnp.bfloat16
NT = (((1,), (1,)), ((), ()))
TN = (((0,), (0,)), ((), ()))


def dot(a, b, dims=None):
    if dims is None:
        return jnp.dot(a, b, preferred_element_type=F32)
    return lax.dot_general(a, b, dims, preferred_element_type=F32)


def params():
    return pltpu.CompilerParams(vmem_limit_bytes=VMEM)


def cost(flops, nbytes):
    return pl.CostEstimate(flops=int(flops) // 1024, bytes_accessed=int(nbytes) // 1024, transcendentals=0)


def slot_order(bits):
    slots = [0]
    for bit in reversed(bits):
        slots = slots + [k ^ (1 << bit) for k in slots]
    return slots


def swap(value, axis, distance, up=False):
    pairs = [(i, i ^ distance) for i in range(lax.axis_size(axis))]
    return lax.ppermute(value, axis, [(i, j) for i, j in pairs if j > i or not up])


def rope_tables(positions, head_dim):
    half = head_dim // 2
    inverse = jnp.power(F32(THETA), -(jnp.arange(half).astype(F32) * (2.0 / head_dim)))
    angle = positions.astype(F32)[:, None] * inverse[None, :]
    return (jnp.cos(angle), jnp.sin(angle))


def rotate_lanes(x, cosine, sine, half):
    width = x.shape[1]
    lane = lax.broadcasted_iota(jnp.int32, x.shape, 1)
    ahead = pltpu.roll(x, width - half, 1)
    behind = pltpu.roll(x, half, 1)
    partner = jnp.where((lane & (2 * half - 1)) < half, ahead, behind)
    times = width // cosine.shape[1]
    if times > 1:
        cosine = jnp.concatenate([cosine] * times, 1)
        sine = jnp.concatenate([sine] * times, 1)
    return x * cosine + partner * sine


def whole(array):
    rank = array.ndim
    return pl.BlockSpec(array.shape, lambda *_: (0,) * rank)


def norm_keyval(tokens, seg_ids, gain, weight, cosine, sine, core, half, split):
    seqs, block, width = tokens.shape
    out = weight.shape[1]
    share = block // (2 * split)

    def kernel(at, tok_ref, seg_ref, gain_ref, w_ref, cos_ref, sin_ref, n_ref, a_ref, b_ref):
        pieces = []
        for rel in range(2):
            for x in range(split):
                begin = pl.multiple_of((2 * x + (at[0] ^ rel)) * share, share)
                pieces.append(tok_ref[0, pl.ds(begin, share), :])
        xf = jnp.concatenate(pieces, 0).astype(F32)
        scale = lax.rsqrt(jnp.mean(xf * xf, axis=-1, keepdims=True) + EPS)
        normed = (xf * scale * gain_ref[...]).astype(BF16)
        n_ref[...] = normed.reshape(n_ref.shape)
        raw = dot(normed, w_ref[...])
        keyval = rotate_lanes(raw, cos_ref[...], sin_ref[...], half).astype(BF16)
        a_ref[0, : block // 2, :] = keyval[: block // 2]
        b_ref[0] = keyval[block // 2 :]
        lane = lax.broadcasted_iota(jnp.int32, (PAD, out), 1)
        row = jnp.zeros((PAD, out), F32)
        for v in range(3):
            count = jnp.sum(jnp.where(seg_ref[0] == v, 1.0, 0.0))
            row = jnp.where(lane == v, count, row)
        a_ref[0, block // 2 :, :] = row.astype(BF16)

    return pl.pallas_call(
        kernel,
        grid_spec=pltpu.PrefetchScalarGridSpec(
            num_scalar_prefetch=1,
            grid=(seqs,),
            in_specs=[
                pl.BlockSpec((1, block, width), lambda s, at: (s, 0, 0)),
                pl.BlockSpec((1, 1, block), lambda s, at: (s, 0, 0)),
                pl.BlockSpec((1, width), lambda s, at: (0, 0)),
                whole(weight),
                whole(cosine),
                whole(sine),
            ],
            out_specs=[
                pl.BlockSpec((2, split, 1, share, width), lambda s, at: (0, 0, s, 0, 0)),
                pl.BlockSpec((1, block // 2 + PAD, out), lambda s, at: (s, 0, 0)),
                pl.BlockSpec((1, block // 2, out), lambda s, at: (s, 0, 0)),
            ],
        ),
        out_shape=[
            jax.ShapeDtypeStruct((2, split, seqs, share, width), BF16),
            jax.ShapeDtypeStruct((seqs, block // 2 + PAD, out), BF16),
            jax.ShapeDtypeStruct((seqs, block // 2, out), BF16),
        ],
        compiler_params=params(),
        cost_estimate=cost(2 * seqs * block * width * out, 4 * seqs * block * width),
        name="norm_keyval",
    )(core, tokens, seg_ids[:, None, :], gain.reshape(1, width), weight, cosine, sine)


def project_query(normed, weight, cosine, sine, half):
    _, split, seqs, share, width = normed.shape
    block = 2 * split * share
    out = weight.shape[1]

    def kernel(n_ref, w_ref, cos_ref, sin_ref, q_ref):
        raw = dot(n_ref[...].reshape(block, width), w_ref[...])
        q_ref[0] = rotate_lanes(raw, cos_ref[...], sin_ref[...], half).astype(BF16)

    return pl.pallas_call(
        kernel,
        grid=(seqs,),
        in_specs=[
            pl.BlockSpec((2, split, 1, share, width), lambda s: (0, 0, s, 0, 0)),
            whole(weight),
            whole(cosine),
            whole(sine),
        ],
        out_specs=pl.BlockSpec((1, block, out), lambda s: (s, 0, 0)),
        out_shape=jax.ShapeDtypeStruct((seqs, block, out), BF16),
        compiler_params=params(),
        cost_estimate=cost(2 * seqs * block * width * out, 2 * seqs * block * width),
        name="project_query",
    )(normed, weight, cosine, sine)


def stacked_lanes(x, group, hd, low):
    rows = x.shape[1]
    flat = jnp.concatenate([x[h * hd : (h + 1) * hd] for h in range(group)], 1)
    zero = jnp.zeros((hd, group * rows), flat.dtype)
    return jnp.concatenate([flat, zero] if low else [zero, flat], 0)


def stacked_rows(x, group, hd, low):
    parts = []
    for h in range(group):
        at = (h * hd) // (2 * hd) * (2 * hd)
        piece = x[:, at : at + 2 * hd]
        if (h % 2 == 0) != low:
            piece = pltpu.roll(piece, hd, 1)
        lane = lax.broadcasted_iota(jnp.int32, piece.shape, 1)
        parts.append(jnp.where((lane < hd) == low, piece, 0.0))
    return jnp.concatenate(parts, 0)


def keyval_of(chunk, sc, base, refs, blocks, half):
    parts = []
    for low, high, table in ((refs[0], refs[1], 0), (refs[2], refs[3], blocks)):
        at = sc[base + table + chunk]
        one = low[jnp.minimum(at, blocks // 2 - 1), 0, :half, :]
        two = high[jnp.maximum(at - blocks // 2, 0), 0, :half, :]
        parts.append(jnp.where(at < blocks // 2, one, two))
    return jnp.concatenate(parts, 0)


def keyval_specs(blocks, half, width):
    return [
        pl.BlockSpec((blocks // 2, 1, rows, width), lambda s, h, sc: (0, s, 0, h))
        for rows in (half + PAD, half + PAD, half, half)
    ]


def mask_bias(chunk, block, position_block, doc_start, core, share, group):
    half = block // 2

    def place(axis):
        row = lax.broadcasted_iota(jnp.int32, (block, block), axis)
        rel = jnp.where(row >= half, 1, 0)
        row = row - half * rel
        return (row // share * 2 + (rel ^ core)) * share + row % share

    key_pos = chunk * block + place(0)
    query_pos = position_block * block + place(1)
    visible = (key_pos >= doc_start) & (key_pos <= query_pos)
    bias = jnp.where(visible, 0.0, NEG)
    return jnp.concatenate([bias] * group, 1)


def attend(query, keyval_all, doc_start, scalars, kv_local, hd, split):
    seqs, block, q_width = query.shape
    blocks = 2 * keyval_all[0].shape[0]
    group = q_width // kv_local // hd
    wide = group * block
    share = block // (2 * split)

    base = 2 + 2 * seqs
    half = block // 2

    def kernel(sc, q_ref, *refs):
        kv_refs, (doc_ref, keep_ref, send_ref, lse_ref, acc) = refs[:4], refs[4:]
        seq = pl.program_id(0)
        mine = sc[0]
        core = sc[1]
        start = sc[2 + seq]
        clear = sc[2 + seqs + seq]
        q_lanes = stacked_lanes((q_ref[0].astype(F32) * SCALE).T.astype(BF16), group, hd, True)
        doc = doc_ref[0]

        def scores_of(chunk, masked):
            kv = keyval_of(chunk, sc, base, kv_refs, blocks, half)
            scores = dot(kv, q_lanes)
            if masked:
                scores = scores + mask_bias(chunk, block, mine, doc, core, share, group)
            return kv, scores

        kv, scores = scores_of(mine, True)
        peak = jnp.max(scores, axis=0, keepdims=True)
        probs = jnp.exp(scores - peak)
        total = jnp.sum(probs, axis=0, keepdims=True)
        acc[...] = dot(kv, probs.astype(BF16), TN)

        def step(masked):
            def run(chunk, carry):
                peak, total = carry
                kv, scores = scores_of(chunk, masked)
                higher = jnp.maximum(peak, jnp.max(scores, axis=0, keepdims=True))
                shrink = jnp.exp(peak - higher)
                probs = jnp.exp(scores - higher)
                total = total * shrink + jnp.sum(probs, axis=0, keepdims=True)
                acc[...] = acc[...] * shrink + dot(kv, probs.astype(BF16), TN)
                return higher, total

            return run

        carry = lax.fori_loop(start, clear, step(True), (peak, total))
        peak, total = lax.fori_loop(clear, mine, step(False), carry)
        lse_ref[0, 0] = peak + jnp.log(total)
        result = acc[hd:] / total
        result = jnp.concatenate([result[:, h * block : (h + 1) * block] for h in range(group)], 0)
        result = result.T.astype(BF16)
        keep_ref[...] = result[:half].reshape(keep_ref.shape)
        send_ref[...] = result[half:].reshape(send_ref.shape)

    return pl.pallas_call(
        kernel,
        grid_spec=pltpu.PrefetchScalarGridSpec(
            num_scalar_prefetch=1,
            grid=(seqs, kv_local),
            in_specs=[
                pl.BlockSpec((1, block, group * hd), lambda s, h, sc: (s, 0, h)),
                *keyval_specs(blocks, half, 2 * hd),
                pl.BlockSpec((1, 1, block), lambda s, h, sc: (s, 0, 0)),
            ],
            out_specs=[
                pl.BlockSpec((split, 1, share, group * hd), lambda s, h, sc: (0, s, 0, h)),
                pl.BlockSpec((split, 1, share, group * hd), lambda s, h, sc: (0, s, 0, h)),
                pl.BlockSpec((1, 1, 1, wide), lambda s, h, sc: (s, h, 0, 0)),
            ],
            scratch_shapes=[pltpu.VMEM((2 * hd, wide), F32)],
        ),
        out_shape=[
            jax.ShapeDtypeStruct((split, seqs, share, q_width), BF16),
            jax.ShapeDtypeStruct((split, seqs, share, q_width), BF16),
            jax.ShapeDtypeStruct((seqs, kv_local, 1, wide), F32),
        ],
        compiler_params=params(),
        cost_estimate=cost(
            8 * seqs * block * q_width * blocks * block, 4 * seqs * blocks * block * 2 * hd
        ),
        name="attend",
    )(scalars, query, *keyval_all, doc_start)


def attend_back(
    query, keyval_all, doc_start, attended, d_mixed, w_out, lse, cosine, sine, scalars, kv_local, hd
):
    seqs, block, q_width = query.shape
    split, _, share, _ = attended[0].shape
    width = w_out.shape[1]
    blocks = 2 * keyval_all[0].shape[0]
    group = q_width // kv_local // hd
    wide = group * block
    base = 2 + 2 * seqs
    half = block // 2

    def kernel(sc, q_ref, *refs):
        kv_refs, refs = refs[:4], refs[4:]
        doc_ref, ok_ref, os_ref, keep_ref, send_ref, w_ref, lse_ref, cos_ref, sin_ref = refs[:9]
        dqk_ref, dqs_ref, ako, aso, bko, bso, acc, ak_ref, as_ref, bk_ref, bs_ref = refs[9:]
        seq = pl.program_id(0)
        mine = sc[0]
        core = sc[1]
        start = sc[2 + seq]
        clear = sc[2 + seqs + seq]
        doc = doc_ref[0]
        q = q_ref[0].astype(F32) * SCALE
        mixed = jnp.concatenate(
            [keep_ref[...].reshape(half, width), send_ref[...].reshape(half, width)], 0
        )
        d_out = dot(mixed, w_ref[...], NT).astype(BF16).astype(F32)
        d_out_t = d_out.T
        q_lanes = stacked_lanes(q.T.astype(BF16), group, hd, True)
        attended = jnp.concatenate(
            [ok_ref[...].reshape(half, group * hd), os_ref[...].reshape(half, group * hd)], 0
        )
        o_lanes = d_out_t * attended.astype(F32).T
        delta = jnp.concatenate(
            [
                jnp.sum(o_lanes[h * hd : (h + 1) * hd], axis=0, keepdims=True)
                for h in range(group)
            ],
            1,
        )
        d_lanes = stacked_lanes(d_out_t.astype(BF16), group, hd, False)
        q_rows = stacked_rows(q, group, hd, True).astype(BF16)
        d_rows = stacked_rows(d_out, group, hd, False).astype(BF16)
        total = lse_ref[0, 0]
        acc[...] = jnp.zeros_like(acc)

        def put(chunk, value):
            for table, kept, sent, rows in (
                (0, ak_ref, as_ref, value[:half]),
                (blocks, bk_ref, bs_ref, value[half:]),
            ):
                at = sc[base + table + chunk]
                kept[jnp.minimum(at, blocks // 2)] = rows
                sent[jnp.where(at < blocks // 2, blocks // 2, at - blocks // 2)] = rows

        def work(chunk, masked):
            kv = keyval_of(chunk, sc, base, kv_refs, blocks, half)
            scores = dot(kv, q_lanes)
            if masked:
                scores = scores + mask_bias(chunk, block, mine, doc, core, share, group)
            probs = jnp.exp(scores - total)
            d_probs = dot(kv, d_lanes)
            d_scores = (probs * (d_probs - delta)).astype(BF16)
            d_kv = dot(probs.astype(BF16), d_rows) + dot(d_scores, q_rows)
            put(chunk, d_kv.astype(BF16))
            acc[...] += dot(kv, d_scores, TN)

        def clean(chunk, carry):
            put(chunk, jnp.zeros((block, 2 * hd), BF16))
            return carry

        def step(masked):
            def run(chunk, carry):
                work(chunk, masked)
                return carry

            return run

        lax.fori_loop(0, start, clean, 0)
        lax.fori_loop(start, clear, step(True), 0)
        lax.fori_loop(clear, mine, step(False), 0)
        work(mine, True)
        lax.fori_loop(mine + 1, blocks, clean, 0)
        for out, ref in ((ako, ak_ref), (aso, as_ref), (bko, bk_ref), (bso, bs_ref)):
            out[:, 0] = ref[: blocks // 2]
        dq = acc[:hd] * SCALE
        dq = jnp.concatenate([dq[:, h * block : (h + 1) * block] for h in range(group)], 0)
        dq = rotate_lanes(dq.T, cos_ref[...], -sin_ref[...], hd // 2)
        dq = dq.astype(BF16)
        dqk_ref[...] = dq[:half].reshape(dqk_ref.shape)
        dqs_ref[...] = dq[half:].reshape(dqs_ref.shape)

    ordered = pl.BlockSpec((split, 1, share, group * hd), lambda s, h, sc: (0, s, 0, h))
    mixed = pl.BlockSpec((split, 1, share, width), lambda s, h, sc: (0, s, 0, 0))
    parts = pl.BlockSpec((blocks // 2, 1, half, 2 * hd), lambda s, h, sc: (0, s, 0, h))
    return pl.pallas_call(
        kernel,
        grid_spec=pltpu.PrefetchScalarGridSpec(
            num_scalar_prefetch=1,
            grid=(seqs, kv_local),
            in_specs=[
                pl.BlockSpec((1, block, group * hd), lambda s, h, sc: (s, 0, h)),
                *keyval_specs(blocks, half, 2 * hd),
                pl.BlockSpec((1, 1, block), lambda s, h, sc: (s, 0, 0)),
                ordered,
                ordered,
                mixed,
                mixed,
                pl.BlockSpec((group * hd, width), lambda s, h, sc: (h, 0)),
                pl.BlockSpec((1, 1, 1, wide), lambda s, h, sc: (s, h, 0, 0)),
                whole(cosine),
                whole(sine),
            ],
            out_specs=[ordered] * 2 + [parts] * 4,
            scratch_shapes=[pltpu.VMEM((2 * hd, wide), F32)]
            + [pltpu.VMEM((blocks // 2 + 1, half, 2 * hd), BF16)] * 4,
        ),
        out_shape=[jax.ShapeDtypeStruct((split, seqs, share, q_width), BF16)] * 2
        + [jax.ShapeDtypeStruct((blocks // 2, seqs, half, kv_local * 2 * hd), BF16)] * 4,
        compiler_params=params(),
        cost_estimate=cost(
            20 * seqs * block * q_width * blocks * block, 8 * seqs * blocks * block * 2 * hd
        ),
        name="attend_back",
    )(scalars, query, *keyval_all, doc_start, *attended, *d_mixed, w_out, lse, cosine, sine)


def finish_keyval(first, last, cosine, sine, half, split):
    _, seqs, part, width = first[0].shape
    share = part // split
    terms = first + last
    count = len(first)

    def kernel(*refs):
        cos_ref, sin_ref, keep_ref, send_ref = refs[2 * count :]
        halves = [
            sum(ref[0, 0].astype(F32) for ref in some)
            for some in (refs[:count], refs[count : 2 * count])
        ]
        x = jnp.concatenate(halves, 0)
        x = rotate_lanes(x, cos_ref[...], -sin_ref[...], half).astype(BF16)
        keep_ref[...] = x[:part].reshape(keep_ref.shape)
        send_ref[...] = x[part:].reshape(send_ref.shape)

    out = pl.BlockSpec((split, 1, share, width), lambda s: (0, s, 0, 0))
    return pl.pallas_call(
        kernel,
        grid=(seqs,),
        in_specs=[pl.BlockSpec((1, 1, part, width), lambda s: (0, s, 0, 0))] * (2 * count)
        + [whole(cosine), whole(sine)],
        out_specs=[out] * 2,
        out_shape=[jax.ShapeDtypeStruct((split, seqs, share, width), BF16)] * 2,
        compiler_params=params(),
        cost_estimate=cost(0, 16 * seqs * part * width),
        name="finish_keyval",
    )(*terms, cosine, sine)


def mix(parts, weights, xf, gain):
    rows, deep = parts[0].shape
    width = weights[0].shape[1]
    count = len(parts)
    tile = math.gcd(width, 512)
    steps = width // tile

    def kernel(*refs):
        x_ref, gain_ref, resid_ref, n_ref, acc = refs[2 * count :]
        j = pl.program_id(0)
        left = jnp.concatenate([refs[k][...] for k in range(count)], 1)
        right = jnp.concatenate([refs[count + k][...] for k in range(count)], 0)
        resid = x_ref[...].astype(F32) + RESID * dot(left, right)
        resid_ref[...] = resid
        acc[j] = resid

        @pl.when(j == steps - 1)
        def _():
            square = sum(jnp.sum(acc[i] * acc[i], axis=-1, keepdims=True) for i in range(steps))
            scale = lax.rsqrt(square / width + EPS)
            for i in range(steps):
                at = pl.ds(i * tile, tile)
                n_ref[:, at] = (acc[i] * scale * gain_ref[:, at]).astype(BF16)

    fixed = lambda r, c: pl.BlockSpec((r, c), lambda j: (0, 0))
    return pl.pallas_call(
        kernel,
        grid=(steps,),
        in_specs=[fixed(rows, deep)] * count
        + [pl.BlockSpec((deep, tile), lambda j: (0, j))] * count
        + [pl.BlockSpec((rows, tile), lambda j: (0, j)), fixed(1, width)],
        out_specs=[pl.BlockSpec((rows, tile), lambda j: (0, j)), fixed(rows, width)],
        out_shape=[
            jax.ShapeDtypeStruct((rows, width), F32),
            jax.ShapeDtypeStruct((rows, width), BF16),
        ],
        scratch_shapes=[pltpu.VMEM((steps, rows, tile), F32)],
        compiler_params=params(),
        cost_estimate=cost(2 * rows * count * deep * width, 2 * count * deep * width),
        name="mix",
    )(*parts, *weights, xf, gain.reshape(1, width))


def resid_back(terms, resid, d_out, gain):
    rows, width = resid.shape
    tile = math.gcd(rows, 128)
    count = len(terms)

    def kernel(*refs):
        resid_ref, dy_ref, gain_ref, d_ref, mixed_ref = refs[count:]
        d_norm = sum(ref[...].astype(F32) for ref in refs[:count])
        resid = resid_ref[...]
        scale = lax.rsqrt(jnp.mean(resid * resid, axis=-1, keepdims=True) + EPS)
        scaled = gain_ref[...] * d_norm
        inner = jnp.mean(scaled * resid, axis=-1, keepdims=True)
        d_resid = dy_ref[...].astype(F32) + scale * scaled - resid * (scale**3 * inner)
        d_ref[...] = d_resid
        mixed_ref[...] = (RESID * d_resid).astype(BF16)

    one = pl.BlockSpec((tile, width), lambda i: (i, 0))
    return pl.pallas_call(
        kernel,
        grid=(rows // tile,),
        in_specs=[one] * (count + 2) + [pl.BlockSpec((1, width), lambda i: (0, 0))],
        out_specs=[one] * 2,
        out_shape=[
            jax.ShapeDtypeStruct((rows, width), F32),
            jax.ShapeDtypeStruct((rows, width), BF16),
        ],
        compiler_params=params(),
        cost_estimate=cost(0, 16 * rows * width),
        name="resid_back",
    )(*terms, resid, d_out, gain.reshape(1, width))


def hidden_back(d_ffn, w_down):
    rows, width = d_ffn.shape
    hidden = w_down.shape[0]
    tile = math.gcd(hidden, 512)

    def kernel(dy_ref, w_ref, o_ref):
        o_ref[...] = dot(dy_ref[...], w_ref[...], NT)

    return pl.pallas_call(
        kernel,
        grid=(hidden // tile,),
        in_specs=[whole(d_ffn), pl.BlockSpec((tile, width), lambda j: (j, 0))],
        out_specs=pl.BlockSpec((rows, tile), lambda j: (0, j)),
        out_shape=jax.ShapeDtypeStruct((rows, hidden), F32),
        compiler_params=params(),
        cost_estimate=cost(2 * rows * width * hidden, 2 * hidden * (rows + width)),
        name="hidden_back",
    )(d_ffn, w_down)


def feed_forward(normed, d_ffn, d_hidden, w_gate, w_up, w_down):
    back = d_hidden is not None
    part, width = normed[0].shape
    rows = 2 * part
    hidden = w_gate.shape[1]
    tile = math.gcd(hidden, 512)
    steps = hidden // tile

    sources = (d_hidden,) if back else d_ffn
    count = len(sources)

    def kernel(nk, ns, *refs):
        wg_ref, wu_ref, wd_ref, h_ref, dg_ref, du_ref, n_ref, *rest = refs[count:]
        at = pl.program_id(0)
        if not back:
            dy_ref, *rest = rest

        @pl.when(at == 0)
        def _():
            n_ref[:part] = nk[...]
            n_ref[part:] = ns[...]
            if not back:
                dy_ref[:part] = refs[0][...]
                dy_ref[part:] = refs[1][...]

        normed = n_ref[...]
        gate = dot(normed, wg_ref[...])
        up = dot(normed, wu_ref[...])
        d_hidden = refs[0][...] if back else dot(dy_ref[...], wd_ref[...], NT)
        sigma = jax.nn.sigmoid(gate)
        swish = gate * sigma
        hidden_tile = (swish * up).astype(BF16)
        d_gate = (d_hidden * up * sigma * (1.0 + gate * (1.0 - sigma))).astype(BF16)
        d_up = (d_hidden * swish).astype(BF16)
        h_ref[...] = hidden_tile
        dg_ref[...] = d_gate
        du_ref[...] = d_up
        if not back:
            return
        f_keep, f_send, dn_keep, dn_send, f_acc, n_acc = rest
        ffn = dot(hidden_tile, wd_ref[...])
        d_normed = dot(d_gate, wg_ref[...], NT) + dot(d_up, wu_ref[...], NT)

        @pl.when(at == 0)
        def _():
            f_acc[...] = ffn
            n_acc[...] = d_normed

        @pl.when(at > 0)
        def _():
            f_acc[...] += ffn
            n_acc[...] += d_normed

        @pl.when(at == steps - 1)
        def _():
            f_keep[...] = f_acc[:part].astype(BF16)
            f_send[...] = f_acc[part:].astype(BF16)
            dn_keep[...] = n_acc[:part].astype(BF16)
            dn_send[...] = n_acc[part:].astype(BF16)

    fixed = lambda r: pl.BlockSpec((r, width), lambda j: (0, 0))
    once = lambda r: pl.BlockSpec((r, width), lambda j: (0, 0), pipeline_mode=pl.Buffered(1))
    extra = 4 if back else 0
    return pl.pallas_call(
        kernel,
        grid=(steps,),
        in_specs=[once(part)] * 2
        + (
            [pl.BlockSpec((rows, tile), lambda j: (0, j))] if back else [once(part)] * 2
        )
        + [
            pl.BlockSpec((width, tile), lambda j: (0, j)),
            pl.BlockSpec((width, tile), lambda j: (0, j)),
            pl.BlockSpec((tile, width), lambda j: (j, 0)),
        ],
        out_specs=[pl.BlockSpec((rows, tile), lambda j: (0, j))] * 3
        + [fixed(rows)] * count
        + [fixed(part)] * extra,
        out_shape=[jax.ShapeDtypeStruct((rows, hidden), BF16)] * 3
        + [jax.ShapeDtypeStruct((rows, width), BF16)] * count
        + [jax.ShapeDtypeStruct((part, width), BF16)] * extra,
        scratch_shapes=[pltpu.VMEM((rows, width), F32)] * (extra // 2),
        compiler_params=params(),
        cost_estimate=cost(
            (10 if back else 6) * rows * width * hidden, 6 * width * hidden
        ),
        name="feed_forward" if back else "feed_forward_other",
    )(*normed, *sources, w_gate, w_up, w_down)


def grad_rows(lefts, rights, blocks_at, pieces, turned):
    count = blocks_at.shape[0]
    width = lefts[0].shape[1]
    piece = width // pieces
    columns = rights[0].shape[1]
    tile = math.gcd(columns, 512)
    pairs = len(lefts)
    half = count // 2 * piece

    def kernel(at, *refs):
        keep, send = refs[-2:]
        total = None
        for p in range(pairs):
            left = jnp.concatenate([refs[p * count + i][...] for i in range(count)], 1)
            right = refs[pairs * count + p][...]
            term = dot(right, left, TN) if turned else dot(left, right, TN)
            total = term if total is None else total + term
        keep[...] = total[:, :half] if turned else total[:half]
        send[...] = (total[:, half:] if turned else total[half:]).astype(BF16)

    specs = [
        pl.BlockSpec((left.shape[0], piece), lambda j, at, i=i: (0, at[i]))
        for left in lefts
        for i in range(count)
    ] + [pl.BlockSpec((right.shape[0], tile), lambda j, at: (0, j)) for right in rights]
    tokens = sum(left.shape[0] for left in lefts)
    return pl.pallas_call(
        kernel,
        grid_spec=pltpu.PrefetchScalarGridSpec(
            num_scalar_prefetch=1,
            grid=(columns // tile,),
            in_specs=specs,
            out_specs=[
                pl.BlockSpec((tile, half), lambda j, at: (j, 0))
                if turned
                else pl.BlockSpec((half, tile), lambda j, at: (0, j))
            ]
            * 2,
        ),
        out_shape=[
            jax.ShapeDtypeStruct((columns, half) if turned else (half, columns), dtype)
            for dtype in (F32, BF16)
        ],
        compiler_params=params(),
        cost_estimate=cost(4 * tokens * half * columns, 2 * tokens * (2 * half + columns)),
        name="grad_rows",
    )(blocks_at, *[left for left in lefts for _ in range(count)], *rights)


def body(
    tokens,
    seg_ids,
    norm1_gain,
    w_query,
    w_keyval,
    w_out,
    norm2_gain,
    w_gate,
    w_up,
    w_down,
    cotangent,
):
    seqs, block, width = tokens.shape
    kv_local = w_keyval.shape[1]
    hd = w_keyval.shape[2] // 2
    q_width = w_query.shape[1]
    kv_width = kv_local * 2 * hd
    dp = lax.axis_size("dp")
    nt = lax.axis_size("tensor")
    split = nt // 2
    share = block // nt
    piece = width // dp
    part = seqs * block // 2
    d_at = lax.axis_index("dp")
    t_at = lax.axis_index("tensor")
    core = t_at & 1
    x_at = t_at >> 1
    x_bits = list(range(1, nt.bit_length() - 1))
    d_bits = list(range(dp.bit_length() - 1))
    shared = d_bits[-1]
    near = d_bits[:-1]

    def ordered(array, rel):
        array = array.reshape(seqs, split, 2, share, *array.shape[2:])
        array = lax.dynamic_index_in_dim(array, core ^ rel, 2, keepdims=False)
        return jnp.swapaxes(array, 0, 1)

    def own(array):
        return lax.dynamic_index_in_dim(array.reshape(split, seqs, share, width), x_at, 0, False)

    def other_core(array):
        return swap(array, "tensor", 1)

    def flat(array):
        return array.reshape(-1, array.shape[-1])

    def tie(*arrays):
        return lax.optimization_barrier(arrays)

    def scatter_x_start(total):
        total = total.reshape(-1, seqs, share, width)
        for bit in reversed(x_bits):
            total = total.reshape(2, -1, seqs, share, width)
            mine = (t_at >> bit) & 1
            send = lax.dynamic_index_in_dim(total, mine ^ 1, 0, False).astype(BF16)
            total = lax.dynamic_index_in_dim(total, mine, 0, False).astype(F32)
            got = swap(send, "tensor", 1 << bit)
            if bit == x_bits[0]:
                return total[0], got[0]
            total = total + got.astype(F32)

    def gather_x(total):
        total = total[None]
        for bit in x_bits:
            got = swap(total, "tensor", 1 << bit)
            low = (t_at >> bit) & 1 == 0
            total = jnp.concatenate(
                [jnp.where(low, total, got), jnp.where(low, got, total)], 0
            )
        return total

    class Summing:
        def __init__(self, keep, send, order, axis=0):
            self.terms, self.send, self.order, self.axis = [keep], send, list(order), axis
            self.size, self.result = keep.shape[axis], None

        def start(self):
            self.terms.append(swap(self.send, "dp", 1 << self.order.pop(0)))

        def add(self):
            self.size //= 2
            self.send = self.total(self.size).astype(BF16)

        def end(self):
            self.result = self.total(0)

        def total(self, first):
            return sum(
                lax.slice_in_dim(term, first, first + self.size, 1, self.axis).astype(F32)
                for term in self.terms
            )

    def weight_grad(lefts, rights, order, turned=False):
        slots = d_at ^ jnp.array(slot_order(order), jnp.int32)
        keep, send = grad_rows(lefts, rights, slots, dp, turned)
        return Summing(keep, send, order, int(turned))

    place = jnp.arange(block).reshape(2, split, share)
    place = ((place // share) % split * 2 + (place // (block // 2) ^ core)) * share + place % share
    positions = d_at * block + place.reshape(block)
    cosine, sine = rope_tables(positions, hd)
    cos_q = jnp.concatenate([cosine] * 4, 1)
    sin_q = jnp.concatenate([-sine, sine] * 2, 1)
    ones = jnp.ones((block, hd), F32)
    cos_kv = jnp.concatenate([cosine, cosine, ones], 1)
    sin_kv = jnp.concatenate([-sine, sine, 0.0 * ones], 1)
    keyval_weight = w_keyval.reshape(width, kv_width)
    order_first = d_bits
    order_last = d_bits[1:-1] + d_bits[:1] + d_bits[-1:]
    d_share = lax.dynamic_slice_in_dim(cotangent, t_at * share, share, 1)
    d_share = swap((RESID * d_share.astype(F32)).astype(BF16), "dp", 1 << shared)
    first_normed, *keyval = norm_keyval(
        tokens, seg_ids, norm1_gain, keyval_weight, cos_kv, sin_kv, core[None], hd // 2, split
    )
    cot = jnp.concatenate([flat(ordered(cotangent, rel)) for rel in range(2)], 0)
    d_ffn = (RESID * cot.astype(F32)).astype(BF16)
    cot_keep = flat(ordered(cotangent, 0))
    xf_keep = flat(ordered(tokens, 0))
    d_ffn, keyval[0], keyval[1] = tie(d_ffn, keyval[0], keyval[1])
    keyval_all = [array[None] for array in keyval]
    for at in range(len(d_bits)):
        got = [
            swap(array, "dp", 1 << order[-1 - at], up=at == 0)
            for array, order in zip(keyval_all, (order_first, order_last))
        ]
        if at == 0:
            d_hidden = hidden_back(d_ffn, w_down)
            *got, d_hidden, d_share = tie(*got, d_hidden, d_share)
            weights = {0: w_out}
            for bit in x_bits:
                for k in list(weights):
                    weights[k | 1 << bit] = swap(weights[k], "tensor", 1 << bit)
        if at == len(d_bits) - 1:
            query = project_query(first_normed, w_query, cos_q, sin_q, hd // 2)
            *got, query = tie(*got, query)
        if at == len(d_bits) - 1:
            keyval_all = [array for pair in zip(keyval_all, got) for array in pair]
        else:
            keyval_all = [jnp.concatenate([a, b], 0) for a, b in zip(keyval_all, got)]
    for k in list(weights):
        weights[k | 1] = other_core(weights[k])

    before = sum(
        jnp.sum(array[:, :, block // 2, :3].astype(F32), axis=0) for array in keyval_all[:2]
    ).astype(jnp.int32)
    seg_ordered = jnp.stack([ordered(seg_ids, rel) for rel in range(2)])
    seg_ordered = seg_ordered.transpose(2, 0, 1, 3).reshape(seqs, block)
    doc_start = jnp.sum(
        jnp.where(seg_ordered[:, :, None] > jnp.arange(3), before[:, None, :], 0), axis=2
    )
    start = jnp.min(doc_start, axis=1) // block
    clear = jnp.clip((jnp.max(doc_start, axis=1) + block - 1) // block, start, d_at)

    def slot_of(order):
        slots = slot_order(order)
        table = jnp.array([slots.index(k) for k in range(dp)], jnp.int32)
        return table[d_at ^ jnp.arange(dp)]

    scalars = jnp.concatenate(
        [d_at[None], core[None], start, clear, slot_of(order_first), slot_of(order_last)]
    ).astype(jnp.int32)
    doc_start = doc_start[:, None, :]
    attended_keep, attended_send, lse = attend(
        query, keyval_all, doc_start, scalars, kv_local, hd, split
    )
    parts = {0: flat(attended_keep), 1: other_core(flat(attended_send))}
    for bit in x_bits:
        for k in list(parts):
            parts[k | 1 << bit] = swap(parts[k], "tensor", 1 << bit)
    groups = sorted(parts)
    resid, second_keep = mix(
        [parts[k] for k in groups], [weights[k] for k in groups], xf_keep, norm2_gain
    )
    second_send = other_core(second_keep)
    second_other = swap(second_keep, "dp", 1 << shared)
    d_share, second_send = tie(d_share, second_send)
    d_ffn_other = flat(gather_x(d_share))
    hidden, d_gate, d_up, second, ffn_keep, ffn_send, d_keep, d_send = feed_forward(
        (second_keep, second_send), None, d_hidden, w_gate, w_up, w_down
    )
    second_other, d_ffn_other, d_keep = tie(second_other, d_ffn_other, d_keep)
    d_part = (d_keep.astype(F32) + other_core(d_send).astype(F32)).astype(BF16)
    terms = [d_part]
    for bit in x_bits:
        if len(terms) > 1:
            terms = [sum(term.astype(F32) for term in terms).astype(BF16)]
        terms = [terms[0], swap(terms[0], "tensor", 1 << bit)]
    second_others = (second_other, other_core(second_other))
    d_ffn_others = (d_ffn_other, other_core(d_ffn_other))
    ffn_sum = (ffn_keep.astype(F32) + other_core(ffn_send).astype(F32)).astype(BF16)
    second_other, ffn_sum, terms[0] = tie(second_other, ffn_sum, terms[0])
    second_others = (second_other, second_others[1])
    hidden_o, d_gate_o, d_up_o, second_o, d_ffn_o = feed_forward(
        second_others, d_ffn_others, None, w_gate, w_up, w_down
    )
    resid, hidden_o = tie(resid, hidden_o)
    chain = [resid]

    def step(*arrays):
        *arrays, chain[0] = tie(*arrays, chain[0])
        return arrays if len(arrays) > 1 else arrays[0]

    def done(*arrays):
        *arrays, chain[0] = tie(*arrays, chain[0])
        return arrays if len(arrays) > 1 else arrays[0]

    def arrive(*sums):
        for one in sums:
            one.terms[-1] = step(one.terms[-1])

    def more(*sums):
        for one in sums:
            if one.order:
                one.add()
                one.send = done(one.send)
                one.start()
            else:
                one.end()
                one.result = done(one.result)

    terms = step(*terms) if len(terms) > 1 else [step(*terms)]
    ffn, ffn_got = scatter_x_start(step(ffn_sum))
    d_resid, d_mixed_keep = done(*resid_back(terms, resid, cot_keep, norm2_gain))
    d_mixed_send = other_core(d_mixed_keep)
    d_gate = step(d_gate)
    gate = weight_grad([second, second_o], [d_gate, d_gate_o], near)
    gate.send = done(gate.send)
    gate.start()
    d_up = step(d_up)
    up = weight_grad([second, second_o], [d_up, d_up_o], near[1:] + near[:1])
    up.send = done(up.send)
    up.start()
    d_mixed_send, ffn_got = step(d_mixed_send, ffn_got)
    out = weight_grad(
        [d_mixed_keep, d_mixed_send], [flat(attended_keep), flat(attended_send)], order_last, True
    )
    out.send = done(out.send)
    out.start()
    hidden = step(hidden)
    down = weight_grad([d_ffn, d_ffn_o], [hidden, hidden_o], near, True)
    down.send = done(down.send)
    down.start()
    query = step(query)
    tokens_of = (split, seqs, share, width)
    d_query_keep, d_query_send, *d_keyval = done(
        *attend_back(
            query,
            keyval_all,
            doc_start,
            (attended_keep, attended_send),
            (d_mixed_keep.reshape(tokens_of), d_mixed_send.reshape(tokens_of)),
            w_out,
            lse,
            cos_q,
            sin_q,
            scalars,
            kv_local,
            hd,
        )
    )
    d_query_keep, d_query_send = flat(d_query_keep), flat(d_query_send)
    kv_first = Summing(d_keyval[0], d_keyval[1], order_first)
    kv_last = Summing(d_keyval[2], d_keyval[3], order_last)
    arrive(gate, out)
    kv_first.start()
    kv_last.start()
    arrive(up)
    first_normed = first_normed.reshape(2, part, width)
    d_query_keep = step(d_query_keep)
    grad_q = weight_grad([first_normed[0], first_normed[1]], [d_query_keep, d_query_send], d_bits)
    grad_q.send = done(grad_q.send)
    d_query_keep = step(d_query_keep)
    back_send, back_keep = done(dot(d_query_send, w_query, NT), dot(d_query_keep, w_query, NT))
    arrive(down, kv_first, kv_last)
    more(kv_first, kv_last)
    more(gate, up, out)
    arrive(kv_first, kv_last)
    more(kv_first, kv_last)
    more(down)
    arrive(gate, up, out)
    more(gate, up)
    for _ in range(3, len(d_bits)):
        arrive(kv_first, kv_last)
        more(kv_first, kv_last)
    arrive(kv_first, kv_last)
    d_keyval_keep, d_keyval_send = (
        flat(array)
        for array in done(
            *finish_keyval(kv_first.terms, kv_last.terms, cos_kv, sin_kv, hd // 2, split)
        )
    )
    back_send = done((back_send + dot(d_keyval_send, keyval_weight, NT)).astype(BF16))
    back_got = other_core(back_send)
    grad_q.start()
    d_keyval_keep = step(d_keyval_keep)
    grad_kv = weight_grad(
        [first_normed[0], first_normed[1]], [d_keyval_keep, d_keyval_send], order_last
    )
    grad_kv.send = done(grad_kv.send)
    grad_kv.start()
    more(out)
    back_got = step(back_got)
    back_keep = back_keep + dot(d_keyval_keep, keyval_weight, NT) + back_got.astype(F32)
    back_keep = done(back_keep)
    d_norm1, back_got = scatter_x_start(back_keep)
    arrive(down, grad_q)
    more(down, grad_q)
    arrive(grad_kv)
    more(grad_kv)
    d_norm1 = d_norm1 + step(back_got).astype(F32)
    xf_share = own(xf_keep).astype(F32)
    scale1 = lax.rsqrt(jnp.mean(xf_share * xf_share, axis=-1, keepdims=True) + EPS)
    scaled = norm1_gain * d_norm1
    grad_tokens = done(
        own(d_resid)
        + scale1 * scaled
        - xf_share * scale1**3 * jnp.mean(scaled * xf_share, axis=-1, keepdims=True)
    )
    live = [out, gate, up, down, grad_q, grad_kv]
    while live := [rows for rows in live if rows.result is None]:
        for rows in live:
            arrive(rows)
            more(rows)
    grad_gate, grad_up, grad_down = gate.result, up.result, down.result
    grad_outproj, grad_query, grad_keyval = out.result, grad_q.result, grad_kv.result
    ffn = ffn.astype(F32) + ffn_got.astype(F32)
    layer_out = (own(chain[0]) + RESID * ffn).astype(BF16)
    def own_rows(array):
        return lax.dynamic_slice_in_dim(array, d_at * piece, piece, 0).astype(F32)

    def gain_share(parts, gain):
        total = sum(jnp.sum(own_rows(w) * g, axis=1) for w, g in parts)
        total = (total / own_rows(gain)).reshape(nt, piece // nt)
        for bit in reversed([0] + x_bits):
            total = total.reshape(2, -1, piece // nt)
            mine = (t_at >> bit) & 1
            send = lax.dynamic_index_in_dim(total, mine ^ 1, 0, False)
            total = lax.dynamic_index_in_dim(total, mine, 0, False)
            total = total + swap(send, "tensor", 1 << bit)
        return total[0]

    grad_gain1 = gain_share([(w_query, grad_query), (keyval_weight, grad_keyval)], norm1_gain)
    grad_gain2 = gain_share([(w_gate, grad_gate), (w_up, grad_up)], norm2_gain)
    return (
        layer_out,
        grad_tokens,
        grad_gain1,
        grad_query,
        grad_keyval.reshape(piece, kv_local, 2 * hd),
        grad_outproj,
        grad_gain2,
        grad_gate,
        grad_up,
        grad_down,
    )


def solution(mesh):
    placed = (
        P(None, "dp", None),
        P(None, "dp"),
        P(),
        P(None, "tensor"),
        P(None, "tensor", None),
        P("tensor", None),
        P(),
        P(None, "tensor"),
        P(None, "tensor"),
        P("tensor", None),
        P(None, "dp", None),
    )
    return jax.shard_map(
        body,
        mesh=mesh,
        in_specs=placed,
        out_specs=(
            P(None, ("dp", "tensor"), None),
            P(None, ("dp", "tensor"), None),
            P(("dp", "tensor")),
            P("dp", "tensor"),
            P("dp", "tensor", None),
            P("tensor", "dp"),
            P(("dp", "tensor")),
            P("dp", "tensor"),
            P("dp", "tensor"),
            P("tensor", "dp"),
        ),
        check_vma=False,
    )
```

time: 895 us -> 548 us (0.61)
  waiting for transfers between devices: 491 us -> 166 us
  Pallas kernels: 117 us -> 200 us
  matrix products: 59.7 us -> 9.85 us
  other arithmetic: 85.6 us -> 54 us
  between operations: 23.1 us -> 1.82 us
  local copies, waits for them, and re-layouts: 30.5 us -> 18 us
  starting transfers between devices: 80.2 us -> 90.9 us
    ppermute x37 -> x50, waiting for transfers between devices: 432 us -> 166 us  [swap(): lax.ppermute(value, axis, [(i, j) for i, j in pairs if j > i or not up])]
    pallas_call x7 -> x14, Pallas kernels: 96.5 us -> 176 us  [the longest x2 78.2 us: feed_forward(): pl.pallas_call(kernel, grid=(steps,), in_specs=[once(part)] * 2 + ([pl.Bl...]
    all_gather x1 -> x0, waiting for transfers between devices: 58.9 us -> none  [body(): keyval_all = lax.all_gather(keyval, 'dp', axis=0)]
    dot_general x12 -> x0, matrix products: 44.2 us -> none  [dot(): return jnp.dot(a, b, preferred_element_type=F32)]
    convert_element_type x15 -> x19, other arithmetic: 40.2 us -> 22 us  [the longest x13 13.7 us: add(): self.send = self.total(self.size).astype(BF16)]
    ppermute x37 -> x50, starting transfers between devices: 80.2 us -> 90.9 us  [swap(): lax.ppermute(value, axis, [(i, j) for i, j in pairs if j > i or not up])]
    add x8 -> x9, other arithmetic: 5.43 us -> 15.9 us  [the longest x6 12.6 us: total(): sum((lax.slice_in_dim(term, first, first + self.size, 1, self.axis).astyp...]
  transfers between devices with their start and end apart: 38 -> 50, of which waited for: 19 -> 24; matrix products, arithmetic and copies ran while one was open for 16% -> 13% of each run, Pallas kernels for 5% -> 33%
where the time goes in v2:
time: 548 us; the launch traced here: 541 us
  Pallas kernels  200 us (36%)
  waiting for transfers between devices  166 us (30%)
  starting transfers between devices  90.9 us (17%)
  other arithmetic  54 us (10%)
  local copies, waits for them, and re-layouts  18 us (3%)
  matrix products  9.85 us (2%)
    ppermute x50, waiting for transfers between devices, swap(): lax.ppermute(value, axis, [(i, j) for i, j in pairs if j > i or not up])  166 us
    ppermute x50, starting transfers between devices, swap(): lax.ppermute(value, axis, [(i, j) for i, j in pairs if j > i or not up])  90.9 us
    pallas_call x2, Pallas kernels, feed_forward(): pl.pallas_call(kernel, grid=(steps,), in_specs=[once(part)] * 2 + ([pl.Bl...  78.2 us
    pallas_call x6, Pallas kernels, grad_rows(): pl.pallas_call(kernel, grid_spec=pltpu.PrefetchScalarGridSpec(num_scalar_...  53.5 us
    pallas_call x1, Pallas kernels, attend_back(): pl.pallas_call(kernel, grid_spec=pltpu.PrefetchScalarGridSpec(num_scalar_...  16.1 us
    convert_element_type x13, other arithmetic, add(): self.send = self.total(self.size).astype(BF16)  13.7 us
    add x6, other arithmetic, total(): sum((lax.slice_in_dim(term, first, first + self.size, 1, self.axis).astyp...  12.6 us
    pallas_call x1, Pallas kernels, hidden_back(): pl.pallas_call(kernel, grid=(hidden // tile,), in_specs=[whole(d_ffn), pl...  11.4 us
  transfers between devices with their start and end apart: 50, of which 24 were waited for; matrix products, arithmetic and copies ran while one was open for 13% of the time, Pallas kernels for 33%

profile of v2, /device:TPU:0, one launch (start us, length us, event | category | flops | bytes accessed | tf_op | source)
XLA Modules:
  0.0 540.8 jit_solution(3925387707487147765)
XLA Ops:
  14.0 5.9 %norm_keyval.1 = (bf16[2,2,3,64,2048]{4,3,2,1,0:T(8,128)(2,1)}, bf16[3,144,256]{2,1,0:T(8,128)(2,1)}, bf16[3,128,256]{2,1,0:T(8,128)(2,1)}) custom-call(s32[1]{0:T(128)} %bitcast.at, bf16[3,256,2048]{2,1,0:T(8,128)(2,1)} %tok_ref.1, s32[3,1,256]{2,1,0:T(1,128)} %broadcast_in_dim.47.seg_ref, f32[1,2048]{1,0:T(1,128)} %bitcast.194, ...), custom_call_target="tpu_custom_call" | custom-call | flops 786432 | bytes 6144 | tf_op jit(solution)/shard_map/norm_keyval/pallas_call | solution.py:100
  26.3 11.4 %hidden_back.1.refs_0_ = f32[768,2048]{1,0:T(8,128)} custom-call(bf16[768,2048]{1,0:T(8,128)(2,1)} %multiply_convert_fusion.dy_ref.refs_0_.refs_1_.refs_2_.refs_3_, bf16[2048,2048]{1,0:T(8,128)(2,1)} %refs_4_.3), custom_call_target="tpu_custom_call" | custom-call | flops 6291456 | bytes 11264 | tf_op jit(solution)/shard_map/hidden_back/pallas_call | solution.py:534
  40.5 18.7 %collective-permute-start.3 = (bf16[2,3,144,256]{3,2,1,0:T(8,128)(2,1)S(1)}, bf16[2,3,144,256]{3,2,1,0:T(8,128)(2,1)S(1)}, u32[]{:S(2)}, u32[]{:S(2)}) collective-permute-start(bf16[2,3,144,256]{3,2,1,0:T(8,128)(2,1)S(1)} %pad_maximum_fusion.3), channel_id=1, source_target_pairs={{0,8},{4,12},{8,0},{12,4},{16,24},{20,28},{24,16},{28,20},{1,9},{5... | collective-permute-start | bytes 1327112 | tf_op jit(solution)/shard_map/ppermute | solution.py:46
  60.8 8.7 %collective-permute-done.3 = bf16[2,3,144,256]{3,2,1,0:T(8,128)(2,1)S(1)} collective-permute-done((bf16[2,3,144,256]{3,2,1,0:T(8,128)(2,1)S(1)}, bf16[2,3,144,256]{3,2,1,0:T(8,128)(2,1)S(1)}, u32[]{:S(2)}, u32[]{:S(2)}) %collective-permute-start.3) | collective-permute-done | bytes 442400 | tf_op jit(solution)/shard_map/ppermute | solution.py:46
  76.8 6.0 %project_query.1.q_ref = bf16[3,256,512]{2,1,0:T(8,128)(2,1)} custom-call(bf16[2,2,3,64,2048]{4,3,2,1,0:T(8,128)(2,1)} %get-tuple-element.213.n_ref, bf16[2048,512]{1,0:T(8,128)(2,1)} %w_ref.3, f32[256,128]{1,0:T(8,128)} %get-tuple-element.430.cos_ref.refs_11_, f32[256,128]{1,0:T(8,128)} %get-tuple-element.444.sin_ref.refs_12_), custom_call_target="tpu_custom_call" | custom-call | flops 1572864 | bytes 3072 | tf_op jit(solution)/shard_map/project_query/pallas_call | solution.py:139
  83.6 8.4 %collective-permute-done.6.refs_3_ = bf16[4,3,128,256]{3,2,1,0:T(8,128)(2,1)} collective-permute-done((bf16[4,3,128,256]{3,2,1,0:T(8,128)(2,1)}, bf16[4,3,128,256]{3,2,1,0:T(8,128)(2,1)}, u32[]{:S(2)}, u32[]{:S(2)}) %collective-permute-start.6) | collective-permute-done | bytes 786464 | tf_op jit(solution)/shard_map/ppermute | solution.py:46
  94.3 8.3 %attend.1 = (bf16[2,3,64,512]{3,2,1,0:T(8,128)(2,1)}, bf16[2,3,64,512]{3,2,1,0:T(8,128)(2,1)}, f32[3,2,1,1024]{3,2,1,0:T(1,128)}) custom-call(s32[24]{0:T(128)} %concatenate.44.sc, bf16[3,256,512]{2,1,0:T(8,128)(2,1)} %project_query.1.q_ref, bf16[4,3,144,256]{3,2,1,0:T(8,128)(2,1)} %pad_maximum_fusion.1.refs_0_, ...), custom_call_target="tpu_custom_call" | custom-call | flops 6291456 | bytes 3072 | tf_op jit(solution)/shard_map/attend/pallas_call | solution.py:263
  107.5 7.4 %collective-permute-done.8.refs_2_ = bf16[384,512]{1,0:T(8,128)(2,1)S(1)} collective-permute-done((bf16[384,512]{1,0:T(8,128)(2,1)}, bf16[384,512]{1,0:T(8,128)(2,1)S(1)}, u32[]{:S(2)}, u32[]{:S(2)}) %collective-permute-start.8) | collective-permute-done | bytes 393248 | tf_op jit(solution)/shard_map/ppermute | solution.py:46
  114.9 8.0 %collective-permute-done.9.refs_3_ = bf16[384,512]{1,0:T(8,128)(2,1)S(1)} collective-permute-done((bf16[384,512]{1,0:T(8,128)(2,1)S(1)}, bf16[384,512]{1,0:T(8,128)(2,1)S(1)}, u32[]{:S(2)}, u32[]{:S(2)}) %collective-permute-start.9) | collective-permute-done | bytes 393248 | tf_op jit(solution)/shard_map/ppermute | solution.py:46
  123.7 9.6 %mix.1 = (f32[384,2048]{1,0:T(8,128)}, bf16[384,2048]{1,0:T(8,128)(2,1)}) custom-call(bf16[384,512]{1,0:T(8,128)(2,1)} %bitcast.171, bf16[384,512]{1,0:T(8,128)(2,1)} %copy-done.46, bf16[384,512]{1,0:T(8,128)(2,1)} %copy-done.47, bf16[384,512]{1,0:T(8,128)(2,1)} %copy-done.48, bf16[512,2048]{1,0:T(8,128)(2,1)} %refs_9_.1, ...), custom_call_target="tpu_custom_call" | custom-call | flops 3145728 | bytes 8192 | tf_op jit(solution)/shard_map/mix/pallas_call | solution.py:476
  138.4 14.2 %collective-permute-start.13 = (bf16[384,2048]{1,0:T(8,128)(2,1)}, bf16[384,2048]{1,0:T(8,128)(2,1)}, u32[]{:S(2)}, u32[]{:S(2)}) collective-permute-start(bf16[384,2048]{1,0:T(8,128)(2,1)} %get-tuple-element.226.nk), channel_id=1, source_target_pairs={{0,16},{4,20},{8,24},{12,28},{16,0},{20,4},{24,8},{28,12},{1,17},{... | collective-permute-start | bytes 4718600 | tf_op jit(solution)/shard_map/ppermute | solution.py:46
  152.7 49.6 %feed_forward.1 = (bf16[768,2048]{1,0:T(8,128)(2,1)}, bf16[768,2048]{1,0:T(8,128)(2,1)}, bf16[768,2048]{1,0:T(8,128)(2,1)}, bf16[768,2048]{1,0:T(8,128)(2,1)}, b...) custom-call(bf16[384,2048]{1,0:T(8,128)(2,1)} %get-tuple-element.226, ...), custom_call_target="tpu_custom_call" | custom-call | flops 31457280 | bytes 24576 | tf_op jit(solution)/shard_map/feed_forward/pallas_call | solution.py:609
  203.2 17.5 %collective-permute-done.13.nk = bf16[384,2048]{1,0:T(8,128)(2,1)} collective-permute-done((bf16[384,2048]{1,0:T(8,128)(2,1)}, bf16[384,2048]{1,0:T(8,128)(2,1)}, u32[]{:S(2)}, u32[]{:S(2)}) %collective-permute-start.13) | collective-permute-done | bytes 1572896 | tf_op jit(solution)/shard_map/ppermute | solution.py:46
  227.4 28.6 %feed_forward_other.1 = (bf16[768,2048]{1,0:T(8,128)(2,1)}, bf16[768,2048]{1,0:T(8,128)(2,1)}, bf16[768,2048]{1,0:T(8,128)(2,1)}, bf16[768,2048]{1,0:T(8,128)(2,1)}, bf16[768,2048]{1,0:T(8,128)(2,1)}) custom-call(bf16[384,2048]{1,0:T(8,128)(2,1)} %collective-permute-done.13.nk, bf16[384,2048]{1,0:T(8,128)(2,1)} %copy-done.30, bf16[384,2048]{1,0:T(8,128)(2,1)} %bitcast.166, ...), custom_call_target="tpu_custom_call" | custom-call | flops 18874368 | bytes 24576 | tf_op jit(solution)/shard_map/feed_forward_other/pallas_call | solution.py:609
  259.4 7.2 %resid_back.1 = (f32[384,2048]{1,0:T(8,128)}, bf16[384,2048]{1,0:T(8,128)(2,1)}) custom-call(bf16[384,2048]{1,0:T(8,128)(2,1)} %copy-done.13, bf16[384,2048]{1,0:T(8,128)(2,1)} %copy-done.29, f32[384,2048]{1,0:T(8,128)} %get-tuple-element.407.refs_2_, bf16[384,2048]{1,0:T(8,128)(2,1)} %bitcast.153, f32[1,2048]{1,0:T(1,128)} %bitcast.196), custom_call_target="tpu_custom_call" | custom-call | bytes 12288 | tf_op jit(solution)/shard_map/resid_back/pallas_call | solution.py:511
  267.2 11.6 %grad_rows.6 = (f32[512,2048]{1,0:T(8,128)}, bf16[512,2048]{1,0:T(8,128)(2,1)}) custom-call(s32[4]{0:T(128)} %get-tuple-element.440.at, bf16[768,2048]{1,0:T(8,128)(2,1)} %get-tuple-element.254.refs_0_.refs_1_.refs_2_.refs_3_, bf16[768,2048]{1,0:T(8,128)(2,1)} %get-tuple-element.254.refs_0_.refs_1_.refs_2_.refs_3_, ...), custom_call_target="tpu_custom_call" | custom-call | flops 6291456 | bytes 9216 | tf_op jit(solution)/shard_map/grad_rows/pallas_call | solution.py:662
  283.4 11.7 %grad_rows.7 = (f32[512,2048]{1,0:T(8,128)}, bf16[512,2048]{1,0:T(8,128)(2,1)}) custom-call(s32[4]{0:T(128)} %get-tuple-element.439.at, bf16[768,2048]{1,0:T(8,128)(2,1)} %get-tuple-element.254.refs_0_.refs_1_.refs_2_.refs_3_, bf16[768,2048]{1,0:T(8,128)(2,1)} %get-tuple-element.254.refs_0_.refs_1_.refs_2_.refs_3_, ...), custom_call_target="tpu_custom_call" | custom-call | flops 6291456 | bytes 9216 | tf_op jit(solution)/shard_map/grad_rows/pallas_call | solution.py:662
  295.7 6.8 %collective-permute-done.22 = bf16[1,3,64,2048]{3,2,1,0:T(8,128)(2,1)S(1)} collective-permute-done((bf16[1,3,64,2048]{3,2,1,0:T(8,128)(2,1)S(1)}, bf16[1,3,64,2048]{3,2,1,0:T(8,128)(2,1)S(1)}, u32[]{:S(2)}, u32[]{:S(2)}) %collective-permute-start.22) | collective-permute-done | bytes 786464 | tf_op jit(solution)/shard_map/ppermute | solution.py:46
  303.6 6.3 %grad_rows.8 = (f32[512,1024]{1,0:T(8,128)}, bf16[512,1024]{1,0:T(8,128)(2,1)}) custom-call(s32[8]{0:T(128)} %get-tuple-element.442.at, bf16[384,2048]{1,0:T(8,128)(2,1)} %get-tuple-element.252.refs_0_.refs_1_.refs_2_.refs_3_.refs_4_.refs_5_.refs_6_.refs_7_, ...), custom_call_target="tpu_custom_call" | custom-call | flops 1572864 | bytes 3840 | tf_op jit(solution)/shard_map/grad_rows/pallas_call | solution.py:662
  310.0 11.6 %grad_rows.9 = (f32[2048,512]{1,0:T(8,128)}, bf16[2048,512]{1,0:T(8,128)(2,1)}) custom-call(s32[4]{0:T(128)} %get-tuple-element.440.at, bf16[768,2048]{1,0:T(8,128)(2,1)} %multiply_convert_fusion.dy_ref.refs_0_.refs_1_.refs_2_.refs_3_, bf16[768,2048]{1,0:T(8,128)(2,1)} %multiply_convert_fusion.dy_ref.refs_0_.refs_1_.refs_2_.refs_3_, ...), custom_call_target="tpu_custom_call" | custom-call | flops 6291456 | bytes 9216 | tf_op jit(solution)/shard_map/grad_rows/pallas_call | solution.py:662
  324.0 16.1 %attend_back.1 = (bf16[2,3,64,512]{3,2,1,0:T(8,128)(2,1)}, bf16[2,3,64,512]{3,2,1,0:T(8,128)(2,1)}, bf16[4,3,128,256]{3,2,1,0:T(8,128)(2,1)}, bf16[4,3,128,256]{...) custom-call(s32[24]{0:T(128)} %concatenate.44.sc, ...), custom_call_target="tpu_custom_call" | custom-call | flops 15728640 | bytes 6144 | tf_op jit(solution)/shard_map/attend_back/pallas_call | solution.py:388
  340.2 6.3 %collective-permute-start.23 = (bf16[4,3,128,256]{3,2,1,0:T(8,128)(2,1)}, bf16[4,3,128,256]{3,2,1,0:T(8,128)(2,1)S(1)}, u32[]{:S(2)}, u32[]{:S(2)}) collective-permute-start(bf16[4,3,128,256]{3,2,1,0:T(8,128)(2,1)} %get-tuple-element.288), channel_id=1, source_target_pairs={{0,4},{4,0},{8,12},{12,8},{16,20},{20,16},{24,28},{28,24},{1,5},{5... | collective-permute-start | bytes 2359304 | tf_op jit(solution)/shard_map/ppermute | solution.py:46
  348.6 6.5 %collective-permute-start.28 = (bf16[4,3,128,256]{3,2,1,0:T(8,128)(2,1)}, bf16[4,3,128,256]{3,2,1,0:T(8,128)(2,1)}, u32[]{:S(2)}, u32[]{:S(2)}) collective-permute-start(bf16[4,3,128,256]{3,2,1,0:T(8,128)(2,1)} %get-tuple-element.308), channel_id=1, source_target_pairs={{0,8},{4,12},{8,0},{12,4},{16,24},{20,28},{24,16},{28,20},{1,9},{5... | collective-permute-start | bytes 2359304 | tf_op jit(solution)/shard_map/ppermute | solution.py:46
  357.6 8.6 %collective-permute-done.26 = bf16[512,1024]{1,0:T(8,128)(2,1)S(1)} collective-permute-done((bf16[512,1024]{1,0:T(8,128)(2,1)}, bf16[512,1024]{1,0:T(8,128)(2,1)S(1)}, u32[]{:S(2)}, u32[]{:S(2)}) %collective-permute-start.26) | collective-permute-done | bytes 1048608 | tf_op jit(solution)/shard_map/ppermute | solution.py:46
  367.2 6.8 %grad_rows.10 = (f32[1024,512]{1,0:T(8,128)}, bf16[1024,512]{1,0:T(8,128)(2,1)}) custom-call(s32[8]{0:T(128)} %get-tuple-element.441.at, bf16[384,2048]{1,0:T(8,128)(2,1)} %bitcast.131, bf16[384,2048]{1,0:T(8,128)(2,1)} %bitcast.132, bf16[384,2048]{1,0:T(8,128)(2,1)} %bitcast.133, bf16[384,2048]{1,0:T(8,128)(2,1)} %bitcast.134, bf16[384,2048]{1,0:T(8,128)(2,1)} %bitcast.135, ...), custom_call_target="tpu_custom_call" | custom-call | flops 1572864 | bytes 3840 | tf_op jit(solution)/shard_map/grad_rows/pallas_call | solution.py:662
  378.8 12.2 %collective-permute-done.23.refs_1_ = bf16[4,3,128,256]{3,2,1,0:T(8,128)(2,1)S(1)} collective-permute-done((bf16[4,3,128,256]{3,2,1,0:T(8,128)(2,1)}, bf16[4,3,128,256]{3,2,1,0:T(8,128)(2,1)S(1)}, u32[]{:S(2)}, u32[]{:S(2)}) %collective-permute-start.23) | collective-permute-done | bytes 786464 | tf_op jit(solution)/shard_map/ppermute | solution.py:46
  401.3 24.6 %collective-permute-done.29.refs_2_ = bf16[2,3,128,256]{3,2,1,0:T(8,128)(2,1)S(1)} collective-permute-done((bf16[2,3,128,256]{3,2,1,0:T(8,128)(2,1)S(1)}, bf16[2,3,128,256]{3,2,1,0:T(8,128)(2,1)S(1)}, u32[]{:S(2)}, u32[]{:S(2)}) %collective-permute-start.29) | collective-permute-done | bytes 393248 | tf_op jit(solution)/shard_map/ppermute | solution.py:46
  437.4 5.9 %collective-permute-done.31.refs_3_ = bf16[1,3,128,256]{3,2,1,0:T(8,128)(2,1)S(1)} collective-permute-done((bf16[1,3,128,256]{3,2,1,0:T(8,128)(2,1)S(1)}, bf16[1,3,128,256]{3,2,1,0:T(8,128)(2,1)S(1)}, u32[]{:S(2)}, u32[]{:S(2)}) %collective-permute-start.31) | collective-permute-done | bytes 196640 | tf_op jit(solution)/shard_map/ppermute | solution.py:46
  463.9 5.5 %grad_rows.11 = (f32[1024,256]{1,0:T(8,128)}, bf16[1024,256]{1,0:T(8,128)(2,1)}) custom-call(s32[8]{0:T(128)} %get-tuple-element.442.at, bf16[384,2048]{1,0:T(8,128)(2,1)} %bitcast.139, bf16[384,2048]{1,0:T(8,128)(2,1)} %bitcast.140, bf16[384,2048]{1,0:T(8,128)(2,1)} %bitcast.141, bf16[384,2048]{1,0:T(8,128)(2,1)} %bitcast.142, bf16[384,2048]{1,0:T(8,128)(2,1)} %bitcast.143, ...), custom_call_target="tpu_custom_call" | custom-call | flops 786432 | bytes 3456 | tf_op jit(solution)/shard_map/grad_rows/pallas_call | solution.py:662
  475.9 11.1 %collective-permute-done.38 = bf16[2048,256]{1,0:T(8,128)(2,1)} collective-permute-done((bf16[2048,256]{1,0:T(8,128)(2,1)}, bf16[2048,256]{1,0:T(8,128)(2,1)}, u32[]{:S(2)}, u32[]{:S(2)}) %collective-permute-start.38) | collective-permute-done | bytes 1048608 | tf_op jit(solution)/shard_map/ppermute | solution.py:46
  498.4 7.0 %collective-permute-done.43 = bf16[1,3,64,2048]{3,2,1,0:T(8,128)(2,1)S(1)} collective-permute-done((bf16[1,3,64,2048]{3,2,1,0:T(8,128)(2,1)S(1)}, bf16[1,3,64,2048]{3,2,1,0:T(8,128)(2,1)S(1)}, u32[]{:S(2)}, u32[]{:S(2)}) %collective-permute-start.43) | collective-permute-done | bytes 786464 | tf_op jit(solution)/shard_map/ppermute | solution.py:46
  515.1 13.1 %collective-permute-done.45 = bf16[256,512]{1,0:T(8,128)(2,1)S(1)} collective-permute-done((bf16[256,512]{1,0:T(8,128)(2,1)S(1)}, bf16[256,512]{1,0:T(8,128)(2,1)S(1)}, u32[]{:S(2)}, u32[]{:S(2)}) %collective-permute-start.45) | collective-permute-done | bytes 262176 | tf_op jit(solution)/shard_map/ppermute | solution.py:46
  (288 shorter events, 157.6 us)
Async XLA Ops:
  1.9 38.5 %collective-permute-start.2 = (bf16[3,64,2048]{2,1,0:T(8,128)(2,1)S(1)}, bf16[3,64,2048]{2,1,0:T(8,128)(2,1)S(1)}, u32[]{:S(2)}, u32[]{:S(2)}) collective-permute-start(bf16[3,64,2048]{2,1,0:T(8,128)(2,1)S(1)} %multiply_convert_fusion.1), channel_id=1, source_target_pairs={{0,16},{4,20},{8,24},{12,28},{16,0},{20,4},{24,8},{28,12},{1,17},{... | collective-permute-start | bytes 2359304 | tf_op jit(solution)/shard_map/ppermute | solution.py:46
  6.0 68.8 %collective-permute-start.11 = (bf16[512,2048]{1,0:T(8,128)(2,1)}, bf16[512,2048]{1,0:T(8,128)(2,1)}, u32[]{:S(2)}, u32[]{:S(2)}) collective-permute-start(bf16[512,2048]{1,0:T(8,128)(2,1)} %refs_9_.1), channel_id=1, source_target_pairs={{0,2},{1,3},{2,0},{3,1},{4,6},{5,7},{6,4},{7,5},{8,10},{9,11},{10,... | collective-permute-start | bytes 6291464 | tf_op jit(solution)/shard_map/ppermute | solution.py:46
  40.5 29.1 %collective-permute-start.3 = (bf16[2,3,144,256]{3,2,1,0:T(8,128)(2,1)S(1)}, bf16[2,3,144,256]{3,2,1,0:T(8,128)(2,1)S(1)}, u32[]{:S(2)}, u32[]{:S(2)}) collective-permute-start(bf16[2,3,144,256]{3,2,1,0:T(8,128)(2,1)S(1)} %pad_maximum_fusion.3), channel_id=1, source_target_pairs={{0,8},{4,12},{8,0},{12,4},{16,24},{20,28},{24,16},{28,20},{1,9},{5... | collective-permute-start | bytes 1327112 | tf_op jit(solution)/shard_map/ppermute | solution.py:46
  70.6 21.5 %collective-permute-start.4 = (bf16[4,3,144,256]{3,2,1,0:T(8,128)(2,1)}, bf16[4,3,144,256]{3,2,1,0:T(8,128)(2,1)}, u32[]{:S(2)}, u32[]{:S(2)}) collective-permute-start(bf16[4,3,144,256]{3,2,1,0:T(8,128)(2,1)} %pad_maximum_fusion.1.refs_0_), channel_id=1, source_target_pairs={{0,4},{4,0},{8,12},{12,8},{16,20},{20,16},{24,28},{28,24},{1,5},{5... | collective-permute-start | bytes 2654216 | tf_op jit(solution)/shard_map/ppermute | solution.py:46
  73.1 19.0 %collective-permute-start.6 = (bf16[4,3,128,256]{3,2,1,0:T(8,128)(2,1)}, bf16[4,3,128,256]{3,2,1,0:T(8,128)(2,1)}, u32[]{:S(2)}, u32[]{:S(2)}) collective-permute-start(bf16[4,3,128,256]{3,2,1,0:T(8,128)(2,1)} %pad_maximum_fusion.2.refs_2_), channel_id=1, source_target_pairs={{0,8},{4,12},{8,0},{12,4},{16,24},{20,28},{24,16},{28,20},{1,9},{5... | collective-permute-start | bytes 2359304 | tf_op jit(solution)/shard_map/ppermute | solution.py:46
  74.8 32.7 %collective-permute-start.10 = (bf16[512,2048]{1,0:T(8,128)(2,1)}, bf16[512,2048]{1,0:T(8,128)(2,1)}, u32[]{:S(2)}, u32[]{:S(2)}) collective-permute-start(bf16[512,2048]{1,0:T(8,128)(2,1)} %refs_9_.1), channel_id=1, source_target_pairs={{0,1},{1,0},{2,3},{3,2},{4,5},{5,4},{6,7},{7,6},{8,9},{9,8},{10,11... | collective-permute-start | bytes 6291464 | tf_op jit(solution)/shard_map/ppermute | solution.py:46
  74.9 48.0 %collective-permute-start.12 = (bf16[512,2048]{1,0:T(8,128)(2,1)}, bf16[512,2048]{1,0:T(8,128)(2,1)}, u32[]{:S(2)}, u32[]{:S(2)}) collective-permute-start(bf16[512,2048]{1,0:T(8,128)(2,1)} %collective-permute-done.11.refs_6_), channel_id=1, source_target_pairs={{0,1},{1,0},{2,3},{3,2},{4,5},{5,4},{6,7},{7,6},{8,9},{9,8},{10,11... | collective-permute-start | bytes 6291464 | tf_op jit(solution)/shard_map/ppermute | solution.py:46
  104.7 18.2 %collective-permute-start.9 = (bf16[384,512]{1,0:T(8,128)(2,1)S(1)}, bf16[384,512]{1,0:T(8,128)(2,1)S(1)}, u32[]{:S(2)}, u32[]{:S(2)}) collective-permute-start(bf16[384,512]{1,0:T(8,128)(2,1)S(1)} %collective-permute-done.7.refs_1_), channel_id=1, source_target_pairs={{0,2},{1,3},{2,0},{3,1},{4,6},{5,7},{6,4},{7,5},{8,10},{9,11},{10,... | collective-permute-start | bytes 1179656 | tf_op jit(solution)/shard_map/ppermute | solution.py:46
  136.9 65.9 %collective-permute-start.15 = (bf16[1,3,64,2048]{3,2,1,0:T(8,128)(2,1)S(1)}, bf16[1,3,64,2048]{3,2,1,0:T(8,128)(2,1)S(1)}, u32[]{:S(2)}, u32[]{:S(2)}) collective-permute-start(bf16[1,3,64,2048]{3,2,1,0:T(8,128)(2,1)S(1)} %bitcast.193), channel_id=1, source_target_pairs={{0,2},{1,3},{2,0},{3,1},{4,6},{5,7},{6,4},{7,5},{8,10},{9,11},{10,... | collective-permute-start | bytes 2359304 | tf_op jit(solution)/shard_map/ppermute | solution.py:46
  138.4 82.2 %collective-permute-start.13 = (bf16[384,2048]{1,0:T(8,128)(2,1)}, bf16[384,2048]{1,0:T(8,128)(2,1)}, u32[]{:S(2)}, u32[]{:S(2)}) collective-permute-start(bf16[384,2048]{1,0:T(8,128)(2,1)} %get-tuple-element.226.nk), channel_id=1, source_target_pairs={{0,16},{4,20},{8,24},{12,28},{16,0},{20,4},{24,8},{28,12},{1,17},{... | collective-permute-start | bytes 4718600 | tf_op jit(solution)/shard_map/ppermute | solution.py:46
  202.3 18.9 %collective-permute-start.17 = (bf16[384,2048]{1,0:T(8,128)(2,1)}, bf16[384,2048]{1,0:T(8,128)(2,1)S(1)}, u32[]{:S(2)}, u32[]{:S(2)}) collective-permute-start(bf16[384,2048]{1,0:T(8,128)(2,1)} %get-tuple-element.236), channel_id=1, source_target_pairs={{0,1},{1,0},{2,3},{3,2},{4,5},{5,4},{6,7},{7,6},{8,9},{9,8},{10,11... | collective-permute-start | bytes 4718600 | tf_op jit(solution)/shard_map/ppermute | solution.py:46
  202.4 20.1 %collective-permute-start.16 = (bf16[384,2048]{1,0:T(8,128)(2,1)}, bf16[384,2048]{1,0:T(8,128)(2,1)S(1)}, u32[]{:S(2)}, u32[]{:S(2)}) collective-permute-start(bf16[384,2048]{1,0:T(8,128)(2,1)} %get-tuple-element.234), channel_id=1, source_target_pairs={{0,1},{1,0},{2,3},{3,2},{4,5},{5,4},{6,7},{7,6},{8,9},{9,8},{10,11... | collective-permute-start | bytes 4718600 | tf_op jit(solution)/shard_map/ppermute | solution.py:46
  221.8 36.4 %collective-permute-start.20 = (bf16[384,2048]{1,0:T(8,128)(2,1)S(1)}, bf16[384,2048]{1,0:T(8,128)(2,1)S(1)}, u32[]{:S(2)}, u32[]{:S(2)}) collective-permute-start(bf16[384,2048]{1,0:T(8,128)(2,1)S(1)} %add_convert_fusion.1.refs_0_), channel_id=1, source_target_pairs={{0,2},{1,3},{2,0},{3,1},{4,6},{5,7},{6,4},{7,5},{8,10},{9,11},{10,... | collective-permute-start | bytes 4718600 | tf_op jit(solution)/shard_map/ppermute | solution.py:46
  266.6 35.9 %collective-permute-start.21 = (bf16[384,2048]{1,0:T(8,128)(2,1)}, bf16[384,2048]{1,0:T(8,128)(2,1)S(1)}, u32[]{:S(2)}, u32[]{:S(2)}) collective-permute-start(bf16[384,2048]{1,0:T(8,128)(2,1)} %get-tuple-element.252.refs_0_.refs_1_.refs_2_.refs_3_.refs_4_.refs_5_.refs_6_.refs_7_), channel_id=1, source_target_pairs={{0,1},{1,0},{2,3},{3,2},{4,5},{5,4},{6,7},{7,6},{8,9},{9,8},{10,11... | collective-permute-start | bytes 4718600 | tf_op jit(solution)/shard_map/ppermute | solution.py:46
  278.8 69.8 %collective-permute-start.27 = (bf16[512,2048]{1,0:T(8,128)(2,1)}, bf16[512,2048]{1,0:T(8,128)(2,1)}, u32[]{:S(2)}, u32[]{:S(2)}) collective-permute-start(bf16[512,2048]{1,0:T(8,128)(2,1)} %get-tuple-element.294), channel_id=1, source_target_pairs={{0,4},{4,0},{8,12},{12,8},{16,20},{20,16},{24,28},{28,24},{1,5},{5... | collective-permute-start | bytes 6291464 | tf_op jit(solution)/shard_map/ppermute | solution.py:46
  282.7 19.7 %collective-permute-start.22 = (bf16[1,3,64,2048]{3,2,1,0:T(8,128)(2,1)S(1)}, bf16[1,3,64,2048]{3,2,1,0:T(8,128)(2,1)S(1)}, u32[]{:S(2)}, u32[]{:S(2)}) collective-permute-start(bf16[1,3,64,2048]{3,2,1,0:T(8,128)(2,1)S(1)} %dynamic-slice_bitcast_fusion.1), channel_id=1, source_target_pairs={{0,2},{1,3},{2,0},{3,1},{4,6},{5,7},{6,4},{7,5},{8,10},{9,11},{10,... | collective-permute-start | bytes 2359304 | tf_op jit(solution)/shard_map/ppermute | solution.py:46
  295.1 71.2 %collective-permute-start.25 = (bf16[512,2048]{1,0:T(8,128)(2,1)}, bf16[512,2048]{1,0:T(8,128)(2,1)}, u32[]{:S(2)}, u32[]{:S(2)}) collective-permute-start(bf16[512,2048]{1,0:T(8,128)(2,1)} %get-tuple-element.292), channel_id=1, source_target_pairs={{0,8},{4,12},{8,0},{12,4},{16,24},{20,28},{24,16},{28,20},{1,9},{5... | collective-permute-start | bytes 6291464 | tf_op jit(solution)/shard_map/ppermute | solution.py:46
  321.6 44.7 %collective-permute-start.26 = (bf16[512,1024]{1,0:T(8,128)(2,1)}, bf16[512,1024]{1,0:T(8,128)(2,1)S(1)}, u32[]{:S(2)}, u32[]{:S(2)}) collective-permute-start(bf16[512,1024]{1,0:T(8,128)(2,1)} %get-tuple-element.293), channel_id=1, source_target_pairs={{0,8},{4,12},{8,0},{12,4},{16,24},{20,28},{24,16},{28,20},{1,9},{5... | collective-permute-start | bytes 3145736 | tf_op jit(solution)/shard_map/ppermute | solution.py:46
  321.6 57.2 %collective-permute-start.24 = (bf16[2048,512]{1,0:T(8,128)(2,1)}, bf16[2048,512]{1,0:T(8,128)(2,1)}, u32[]{:S(2)}, u32[]{:S(2)}) collective-permute-start(bf16[2048,512]{1,0:T(8,128)(2,1)} %get-tuple-element.289), channel_id=1, source_target_pairs={{0,4},{4,0},{8,12},{12,8},{16,20},{20,16},{24,28},{28,24},{1,5},{5... | collective-permute-start | bytes 6291464 | tf_op jit(solution)/shard_map/ppermute | solution.py:46
  340.2 50.8 %collective-permute-start.23 = (bf16[4,3,128,256]{3,2,1,0:T(8,128)(2,1)}, bf16[4,3,128,256]{3,2,1,0:T(8,128)(2,1)S(1)}, u32[]{:S(2)}, u32[]{:S(2)}) collective-permute-start(bf16[4,3,128,256]{3,2,1,0:T(8,128)(2,1)} %get-tuple-element.288), channel_id=1, source_target_pairs={{0,4},{4,0},{8,12},{12,8},{16,20},{20,16},{24,28},{28,24},{1,5},{5... | collective-permute-start | bytes 2359304 | tf_op jit(solution)/shard_map/ppermute | solution.py:46
  348.6 42.4 %collective-permute-start.28 = (bf16[4,3,128,256]{3,2,1,0:T(8,128)(2,1)}, bf16[4,3,128,256]{3,2,1,0:T(8,128)(2,1)}, u32[]{:S(2)}, u32[]{:S(2)}) collective-permute-start(bf16[4,3,128,256]{3,2,1,0:T(8,128)(2,1)} %get-tuple-element.308), channel_id=1, source_target_pairs={{0,8},{4,12},{8,0},{12,4},{16,24},{20,28},{24,16},{28,20},{1,9},{5... | collective-permute-start | bytes 2359304 | tf_op jit(solution)/shard_map/ppermute | solution.py:46
  392.4 39.1 %collective-permute-start.33 = (bf16[256,2048]{1,0:T(8,128)(2,1)S(1)}, bf16[256,2048]{1,0:T(8,128)(2,1)S(1)}, u32[]{:S(2)}, u32[]{:S(2)}) collective-permute-start(bf16[256,2048]{1,0:T(8,128)(2,1)S(1)} %copy-done.36), channel_id=1, source_target_pairs={{0,8},{4,12},{8,0},{12,4},{16,24},{20,28},{24,16},{28,20},{1,9},{5... | collective-permute-start | bytes 3145736 | tf_op jit(solution)/shard_map/ppermute | solution.py:46
  392.5 39.0 %collective-permute-start.32 = (bf16[256,2048]{1,0:T(8,128)(2,1)S(1)}, bf16[256,2048]{1,0:T(8,128)(2,1)S(1)}, u32[]{:S(2)}, u32[]{:S(2)}) collective-permute-start(bf16[256,2048]{1,0:T(8,128)(2,1)S(1)} %add_convert_fusion.5), channel_id=1, source_target_pairs={{0,4},{4,0},{8,12},{12,8},{16,20},{20,16},{24,28},{28,24},{1,5},{5... | collective-permute-start | bytes 3145736 | tf_op jit(solution)/shard_map/ppermute | solution.py:46
  394.4 32.5 %collective-permute-start.30 = (bf16[2,3,128,256]{3,2,1,0:T(8,128)(2,1)S(1)}, bf16[2,3,128,256]{3,2,1,0:T(8,128)(2,1)S(1)}, u32[]{:S(2)}, u32[]{:S(2)}) collective-permute-start(bf16[2,3,128,256]{3,2,1,0:T(8,128)(2,1)S(1)} %add_convert_fusion.8), channel_id=1, source_target_pairs={{0,4},{4,0},{8,12},{12,8},{16,20},{20,16},{24,28},{28,24},{1,5},{5... | collective-permute-start | bytes 1179656 | tf_op jit(solution)/shard_map/ppermute | solution.py:46
  394.8 31.1 %collective-permute-start.29 = (bf16[2,3,128,256]{3,2,1,0:T(8,128)(2,1)S(1)}, bf16[2,3,128,256]{3,2,1,0:T(8,128)(2,1)S(1)}, u32[]{:S(2)}, u32[]{:S(2)}) collective-permute-start(bf16[2,3,128,256]{3,2,1,0:T(8,128)(2,1)S(1)} %add_convert_fusion.9), channel_id=1, source_target_pairs={{0,8},{4,12},{8,0},{12,4},{16,24},{20,28},{24,16},{28,20},{1,9},{5... | collective-permute-start | bytes 1179656 | tf_op jit(solution)/shard_map/ppermute | solution.py:46
  396.7 40.7 %collective-permute-start.34 = (bf16[512,512]{1,0:T(8,128)(2,1)S(1)}, bf16[512,512]{1,0:T(8,128)(2,1)}, u32[]{:S(2)}, u32[]{:S(2)}) collective-permute-start(bf16[512,512]{1,0:T(8,128)(2,1)S(1)} %add_convert_fusion.7), channel_id=1, source_target_pairs={{0,4},{4,0},{8,12},{12,8},{16,20},{20,16},{24,28},{28,24},{1,5},{5... | collective-permute-start | bytes 1572872 | tf_op jit(solution)/shard_map/ppermute | solution.py:46
  453.8 18.8 %collective-permute-start.39 = (bf16[384,2048]{1,0:T(8,128)(2,1)}, bf16[384,2048]{1,0:T(8,128)(2,1)}, u32[]{:S(2)}, u32[]{:S(2)}) collective-permute-start(bf16[384,2048]{1,0:T(8,128)(2,1)} %add_convert_fusion), channel_id=1, source_target_pairs={{0,1},{1,0},{2,3},{3,2},{4,5},{5,4},{6,7},{7,6},{8,9},{9,8},{10,11... | collective-permute-start | bytes 4718600 | tf_op jit(solution)/shard_map/ppermute | solution.py:46
  453.8 37.4 %collective-permute-start.37 = (bf16[1024,512]{1,0:T(8,128)(2,1)}, bf16[1024,512]{1,0:T(8,128)(2,1)}, u32[]{:S(2)}, u32[]{:S(2)}) collective-permute-start(bf16[1024,512]{1,0:T(8,128)(2,1)} %get-tuple-element.364), channel_id=1, source_target_pairs={{0,4},{4,0},{8,12},{12,8},{16,20},{20,16},{24,28},{28,24},{1,5},{5... | collective-permute-start | bytes 3145736 | tf_op jit(solution)/shard_map/ppermute | solution.py:46
  455.1 31.9 %collective-permute-start.38 = (bf16[2048,256]{1,0:T(8,128)(2,1)}, bf16[2048,256]{1,0:T(8,128)(2,1)}, u32[]{:S(2)}, u32[]{:S(2)}) collective-permute-start(bf16[2048,256]{1,0:T(8,128)(2,1)} %add_convert_fusion.3), channel_id=1, source_target_pairs={{0,8},{4,12},{8,0},{12,4},{16,24},{20,28},{24,16},{28,20},{1,9},{5... | collective-permute-start | bytes 3145736 | tf_op jit(solution)/shard_map/ppermute | solution.py:46
  469.3 28.2 %collective-permute-start.36 = (bf16[1024,256]{1,0:T(8,128)(2,1)}, bf16[1024,256]{1,0:T(8,128)(2,1)S(1)}, u32[]{:S(2)}, u32[]{:S(2)}) collective-permute-start(bf16[1024,256]{1,0:T(8,128)(2,1)} %get-tuple-element.362), channel_id=1, source_target_pairs={{0,8},{4,12},{8,0},{12,4},{16,24},{20,28},{24,16},{28,20},{1,9},{5... | collective-permute-start | bytes 1572872 | tf_op jit(solution)/shard_map/ppermute | solution.py:46
  471.3 36.4 %collective-permute-start.42 = (bf16[512,256]{1,0:T(8,128)(2,1)S(1)}, bf16[512,256]{1,0:T(8,128)(2,1)S(1)}, u32[]{:S(2)}, u32[]{:S(2)}) collective-permute-start(bf16[512,256]{1,0:T(8,128)(2,1)S(1)} %add_convert_fusion.12), channel_id=1, source_target_pairs={{0,16},{4,20},{8,24},{12,28},{16,0},{20,4},{24,8},{28,12},{1,17},{... | collective-permute-start | bytes 786440 | tf_op jit(solution)/shard_map/ppermute | solution.py:46
  513.5 19.4 %collective-permute-start.49 = (f32[1,64]{1,0:T(1,128)S(1)}, f32[1,64]{1,0:T(1,128)S(1)}, u32[]{:S(2)}, u32[]{:S(2)}) collective-permute-start(f32[1,64]{1,0:T(1,128)S(1)} %constant_dynamic-slice_fusion), channel_id=1, source_target_pairs={{0,1},{1,0},{2,3},{3,2},{4,5},{5,4},{6,7},{7,6},{8,9},{9,8},{10,11... | collective-permute-start | bytes 776 | tf_op jit(solution)/shard_map/ppermute | solution.py:46
  (73 other events, 858.6 us)

commit v3 on v2

--- a/solution.py
+++ b/solution.py
@@ -172,13 +172,15 @@
     return jnp.concatenate(parts, 0)
 
 
-def keyval_of(chunk, sc, base, refs, blocks, half):
+def keyval_of(last, count, sc, base, refs, blocks, half):
     parts = []
-    for low, high, table in ((refs[0], refs[1], 0), (refs[2], refs[3], blocks)):
-        at = sc[base + table + chunk]
-        one = low[jnp.minimum(at, blocks // 2 - 1), 0, :half, :]
-        two = high[jnp.maximum(at - blocks // 2, 0), 0, :half, :]
-        parts.append(jnp.where(at < blocks // 2, one, two))
+    for back in reversed(range(count)):
+        chunk = jnp.maximum(last - back, 0) if back else last
+        for low, high, table in ((refs[0], refs[1], 0), (refs[2], refs[3], blocks)):
+            at = sc[base + table + chunk]
+            one = low[jnp.minimum(at, blocks // 2 - 1), 0, :half, :]
+            two = high[jnp.maximum(at - blocks // 2, 0), 0, :half, :]
+            parts.append(jnp.where(at < blocks // 2, one, two))
     return jnp.concatenate(parts, 0)
 
 
@@ -189,20 +191,30 @@
     ]
 
 
-def mask_bias(chunk, block, position_block, doc_start, core, share, group):
+def mask_bias(last, count, block, position_block, doc_start, core, share, group):
     half = block // 2
 
     def place(axis):
-        row = lax.broadcasted_iota(jnp.int32, (block, block), axis)
+        row = lax.broadcasted_iota(jnp.int32, (count * block, block), axis)
+        chunk = row // block * block if axis == 0 else 0
+        row = row - chunk
         rel = jnp.where(row >= half, 1, 0)
         row = row - half * rel
-        return (row // share * 2 + (rel ^ core)) * share + row % share
-
-    key_pos = chunk * block + place(0)
+        return (row // share * 2 + (rel ^ core)) * share + row % share + chunk
+
+    key_pos = (last - count + 1) * block + place(0)
     query_pos = position_block * block + place(1)
     visible = (key_pos >= doc_start) & (key_pos <= query_pos)
     bias = jnp.where(visible, 0.0, NEG)
     return jnp.concatenate([bias] * group, 1)
+
+
+def pair_loops(mine, start, clear, visit, carry):
+    whole_pairs = jnp.maximum(mine - 1 - clear, 0) // 2
+    pairs = (mine - start) // 2
+    run = lambda masked: lambda p, carry: visit(mine - 2 * p, masked, carry)
+    carry = lax.fori_loop(1, 1 + whole_pairs, run(False), carry)
+    return lax.fori_loop(1 + whole_pairs, 1 + pairs, run(True), carry)
 
 
 def attend(query, keyval_all, doc_start, scalars, kv_local, hd, split):
@@ -225,11 +237,11 @@
         q_lanes = stacked_lanes((q_ref[0].astype(F32) * SCALE).T.astype(BF16), group, hd, True)
         doc = doc_ref[0]
 
-        def scores_of(chunk, masked):
-            kv = keyval_of(chunk, sc, base, kv_refs, blocks, half)
+        def scores_of(last, masked):
+            kv = keyval_of(last, 2, sc, base, kv_refs, blocks, half)
             scores = dot(kv, q_lanes)
             if masked:
-                scores = scores + mask_bias(chunk, block, mine, doc, core, share, group)
+                scores = scores + mask_bias(last, 2, block, mine, doc, core, share, group)
             return kv, scores
 
         kv, scores = scores_of(mine, True)
@@ -238,21 +250,17 @@
         total = jnp.sum(probs, axis=0, keepdims=True)
         acc[...] = dot(kv, probs.astype(BF16), TN)
 
-        def step(masked):
-            def run(chunk, carry):
-                peak, total = carry
-                kv, scores = scores_of(chunk, masked)
-                higher = jnp.maximum(peak, jnp.max(scores, axis=0, keepdims=True))
-                shrink = jnp.exp(peak - higher)
-                probs = jnp.exp(scores - higher)
-                total = total * shrink + jnp.sum(probs, axis=0, keepdims=True)
-                acc[...] = acc[...] * shrink + dot(kv, probs.astype(BF16), TN)
-                return higher, total
-
-            return run
-
-        carry = lax.fori_loop(start, clear, step(True), (peak, total))
-        peak, total = lax.fori_loop(clear, mine, step(False), carry)
+        def visit(last, masked, carry):
+            peak, total = carry
+            kv, scores = scores_of(last, masked)
+            higher = jnp.maximum(peak, jnp.max(scores, axis=0, keepdims=True))
+            shrink = jnp.exp(peak - higher)
+            probs = jnp.exp(scores - higher)
+            total = total * shrink + jnp.sum(probs, axis=0, keepdims=True)
+            acc[...] = acc[...] * shrink + dot(kv, probs.astype(BF16), TN)
+            return higher, total
+
+        peak, total = pair_loops(mine, start, clear, visit, (peak, total))
         lse_ref[0, 0] = peak + jnp.log(total)
         result = acc[hd:] / total
         result = jnp.concatenate([result[:, h * block : (h + 1) * block] for h in range(group)], 0)
@@ -346,10 +354,10 @@
                 sent[jnp.where(at < blocks // 2, blocks // 2, at - blocks // 2)] = rows
 
         def work(chunk, masked):
-            kv = keyval_of(chunk, sc, base, kv_refs, blocks, half)
+            kv = keyval_of(chunk, 1, sc, base, kv_refs, blocks, half)
             scores = dot(kv, q_lanes)
             if masked:
-                scores = scores + mask_bias(chunk, block, mine, doc, core, share, group)
+                scores = scores + mask_bias(chunk, 1, block, mine, doc, core, share, group)
             probs = jnp.exp(scores - total)
             d_probs = dot(kv, d_lanes)
             d_scores = (probs * (d_probs - delta)).astype(BF16)
@@ -633,7 +641,7 @@
     )(*normed, *sources, w_gate, w_up, w_down)
 
 
-def grad_rows(lefts, rights, blocks_at, pieces, turned):
+def grad_rows(lefts, rights, blocks_at, pieces, turned, base=(), dtypes=(F32, BF16)):
     count = blocks_at.shape[0]
     width = lefts[0].shape[1]
     piece = width // pieces
@@ -650,8 +658,12 @@
             right = refs[pairs * count + p][...]
             term = dot(right, left, TN) if turned else dot(left, right, TN)
             total = term if total is None else total + term
-        keep[...] = total[:, :half] if turned else total[:half]
-        send[...] = (total[:, half:] if turned else total[half:]).astype(BF16)
+        if base:
+            total = total + jnp.concatenate(
+                [refs[-4][...].astype(F32), refs[-3][...].astype(F32)], int(turned)
+            )
+        keep[...] = (total[:, :half] if turned else total[:half]).astype(dtypes[0])
+        send[...] = (total[:, half:] if turned else total[half:]).astype(dtypes[1])
 
     specs = [
         pl.BlockSpec((left.shape[0], piece), lambda j, at, i=i: (0, at[i]))
@@ -659,27 +671,27 @@
         for i in range(count)
     ] + [pl.BlockSpec((right.shape[0], tile), lambda j, at: (0, j)) for right in rights]
     tokens = sum(left.shape[0] for left in lefts)
+    halves = [
+        pl.BlockSpec((tile, half), lambda j, at: (j, 0))
+        if turned
+        else pl.BlockSpec((half, tile), lambda j, at: (0, j))
+    ] * 2
     return pl.pallas_call(
         kernel,
         grid_spec=pltpu.PrefetchScalarGridSpec(
             num_scalar_prefetch=1,
             grid=(columns // tile,),
-            in_specs=specs,
-            out_specs=[
-                pl.BlockSpec((tile, half), lambda j, at: (j, 0))
-                if turned
-                else pl.BlockSpec((half, tile), lambda j, at: (0, j))
-            ]
-            * 2,
+            in_specs=specs + halves[: len(base)],
+            out_specs=halves,
         ),
         out_shape=[
             jax.ShapeDtypeStruct((columns, half) if turned else (half, columns), dtype)
-            for dtype in (F32, BF16)
+            for dtype in dtypes
         ],
         compiler_params=params(),
         cost_estimate=cost(4 * tokens * half * columns, 2 * tokens * (2 * half + columns)),
         name="grad_rows",
-    )(blocks_at, *[left for left in lefts for _ in range(count)], *rights)
+    )(blocks_at, *[left for left in lefts for _ in range(count)], *rights, *base)
 
 
 def body(
@@ -732,14 +744,14 @@
     def tie(*arrays):
         return lax.optimization_barrier(arrays)
 
-    def scatter_x_start(total):
+    def scatter_x_start(total, keep_order=lambda array: array):
         total = total.reshape(-1, seqs, share, width)
         for bit in reversed(x_bits):
             total = total.reshape(2, -1, seqs, share, width)
             mine = (t_at >> bit) & 1
             send = lax.dynamic_index_in_dim(total, mine ^ 1, 0, False).astype(BF16)
             total = lax.dynamic_index_in_dim(total, mine, 0, False).astype(F32)
-            got = swap(send, "tensor", 1 << bit)
+            got = swap(keep_order(send), "tensor", 1 << bit)
             if bit == x_bits[0]:
                 return total[0], got[0]
             total = total + got.astype(F32)
@@ -775,9 +787,11 @@
                 for term in self.terms
             )
 
-    def weight_grad(lefts, rights, order, turned=False):
-        slots = d_at ^ jnp.array(slot_order(order), jnp.int32)
-        keep, send = grad_rows(lefts, rights, slots, dp, turned)
+    def slots_of(order):
+        return d_at ^ jnp.array(slot_order(order), jnp.int32)
+
+    def weight_grad(lefts, rights, order, turned=False, base=()):
+        keep, send = grad_rows(lefts, rights, slots_of(order), dp, turned, base)
         return Summing(keep, send, order, int(turned))
 
     place = jnp.arange(block).reshape(2, split, share)
@@ -792,8 +806,6 @@
     keyval_weight = w_keyval.reshape(width, kv_width)
     order_first = d_bits
     order_last = d_bits[1:-1] + d_bits[:1] + d_bits[-1:]
-    d_share = lax.dynamic_slice_in_dim(cotangent, t_at * share, share, 1)
-    d_share = swap((RESID * d_share.astype(F32)).astype(BF16), "dp", 1 << shared)
     first_normed, *keyval = norm_keyval(
         tokens, seg_ids, norm1_gain, keyval_weight, cos_kv, sin_kv, core[None], hd // 2, split
     )
@@ -810,14 +822,16 @@
         ]
         if at == 0:
             d_hidden = hidden_back(d_ffn, w_down)
-            *got, d_hidden, d_share = tie(*got, d_hidden, d_share)
+            *got, d_hidden = tie(*got, d_hidden)
             weights = {0: w_out}
             for bit in x_bits:
                 for k in list(weights):
                     weights[k | 1 << bit] = swap(weights[k], "tensor", 1 << bit)
         if at == len(d_bits) - 1:
             query = project_query(first_normed, w_query, cos_q, sin_q, hd // 2)
-            *got, query = tie(*got, query)
+            d_share = lax.dynamic_slice_in_dim(cotangent, t_at * share, share, 1)
+            *got, query, d_share = tie(*got, query, d_share)
+            d_share = swap((RESID * d_share.astype(F32)).astype(BF16), "dp", 1 << shared)
         if at == len(d_bits) - 1:
             keyval_all = [array for pair in zip(keyval_all, got) for array in pair]
         else:
@@ -853,6 +867,7 @@
         for k in list(parts):
             parts[k | 1 << bit] = swap(parts[k], "tensor", 1 << bit)
     groups = sorted(parts)
+    d_share, parts[groups[nt // 2]] = tie(d_share, parts[groups[nt // 2]])
     resid, second_keep = mix(
         [parts[k] for k in groups], [weights[k] for k in groups], xf_keep, norm2_gain
     )
@@ -863,7 +878,11 @@
     hidden, d_gate, d_up, second, ffn_keep, ffn_send, d_keep, d_send = feed_forward(
         (second_keep, second_send), None, d_hidden, w_gate, w_up, w_down
     )
-    second_other, d_ffn_other, d_keep = tie(second_other, d_ffn_other, d_keep)
+    up_order = near[1:] + near[:1]
+    gate_own = grad_rows([second], [d_gate], slots_of(near), dp, False, (), (BF16, BF16))
+    d_up, *gate_own = tie(d_up, *gate_own)
+    up_own = grad_rows([second], [d_up], slots_of(up_order), dp, False, (), (BF16, BF16))
+    second_other, d_ffn_other, d_keep, *up_own = tie(second_other, d_ffn_other, d_keep, *up_own)
     d_part = (d_keep.astype(F32) + other_core(d_send).astype(F32)).astype(BF16)
     terms = [d_part]
     for bit in x_bits:
@@ -878,6 +897,17 @@
     hidden_o, d_gate_o, d_up_o, second_o, d_ffn_o = feed_forward(
         second_others, d_ffn_others, None, w_gate, w_up, w_down
     )
+    def own_rows(array):
+        return lax.dynamic_slice_in_dim(array, d_at * piece, piece, 0).astype(F32)
+
+    def gain_share(total, gain):
+        total = (total / own_rows(gain)).reshape(nt, piece // nt)
+        pieces = [lax.dynamic_index_in_dim(total, t_at ^ k, 0, False) for k in range(nt)]
+        return sum([pieces[0]] + [swap(pieces[k], "tensor", k) for k in range(1, nt)])
+
+    def row_sum(weight, grad):
+        return jnp.sum(own_rows(weight) * grad, axis=1)
+
     resid, hidden_o = tie(resid, hidden_o)
     chain = [resid]
 
@@ -907,15 +937,15 @@
     ffn, ffn_got = scatter_x_start(step(ffn_sum))
     d_resid, d_mixed_keep = done(*resid_back(terms, resid, cot_keep, norm2_gain))
     d_mixed_send = other_core(d_mixed_keep)
-    d_gate = step(d_gate)
-    gate = weight_grad([second, second_o], [d_gate, d_gate_o], near)
+    d_gate_o = step(d_gate_o)
+    gate = weight_grad([second_o], [d_gate_o], near, False, gate_own)
     gate.send = done(gate.send)
     gate.start()
-    d_up = step(d_up)
-    up = weight_grad([second, second_o], [d_up, d_up_o], near[1:] + near[:1])
+    d_up_o = step(d_up_o)
+    up = weight_grad([second_o], [d_up_o], up_order, False, up_own)
     up.send = done(up.send)
     up.start()
-    d_mixed_send, ffn_got = step(d_mixed_send, ffn_got)
+    d_mixed_send = step(d_mixed_send)
     out = weight_grad(
         [d_mixed_keep, d_mixed_send], [flat(attended_keep), flat(attended_send)], order_last, True
     )
@@ -947,6 +977,7 @@
     kv_first = Summing(d_keyval[0], d_keyval[1], order_first)
     kv_last = Summing(d_keyval[2], d_keyval[3], order_last)
     arrive(gate, out)
+    ffn_got = step(ffn_got)
     kv_first.start()
     kv_last.start()
     arrive(up)
@@ -958,12 +989,15 @@
     back_send, back_keep = done(dot(d_query_send, w_query, NT), dot(d_query_keep, w_query, NT))
     arrive(down, kv_first, kv_last)
     more(kv_first, kv_last)
-    more(gate, up, out)
+    for rows in (gate, up, out):
+        rows.add()
+        rows.send = done(rows.send)
     arrive(kv_first, kv_last)
     more(kv_first, kv_last)
+    for rows in (gate, up, out):
+        rows.send = step(rows.send)
+        rows.start()
     more(down)
-    arrive(gate, up, out)
-    more(gate, up)
     for _ in range(3, len(d_bits)):
         arrive(kv_first, kv_last)
         more(kv_first, kv_last)
@@ -976,6 +1010,7 @@
     )
     back_send = done((back_send + dot(d_keyval_send, keyval_weight, NT)).astype(BF16))
     back_got = other_core(back_send)
+    arrive(gate, up, out)
     grad_q.start()
     d_keyval_keep = step(d_keyval_keep)
     grad_kv = weight_grad(
@@ -987,7 +1022,8 @@
     back_got = step(back_got)
     back_keep = back_keep + dot(d_keyval_keep, keyval_weight, NT) + back_got.astype(F32)
     back_keep = done(back_keep)
-    d_norm1, back_got = scatter_x_start(back_keep)
+    d_norm1, back_got = scatter_x_start(back_keep, done)
+    more(gate, up)
     arrive(down, grad_q)
     more(down, grad_q)
     arrive(grad_kv)
@@ -1001,31 +1037,27 @@
         + scale1 * scaled
         - xf_share * scale1**3 * jnp.mean(scaled * xf_share, axis=-1, keepdims=True)
     )
+    def second_gain():
+        gate.result, up.result = step(gate.result, up.result)
+        total = done(row_sum(w_gate, gate.result) + row_sum(w_up, up.result))
+        return gain_share(total, norm2_gain)
+
+    early = len(near) == 2
+    if early:
+        grad_gain2 = second_gain()
     live = [out, gate, up, down, grad_q, grad_kv]
     while live := [rows for rows in live if rows.result is None]:
         for rows in live:
             arrive(rows)
             more(rows)
+    if not early:
+        grad_gain2 = second_gain()
     grad_gate, grad_up, grad_down = gate.result, up.result, down.result
     grad_outproj, grad_query, grad_keyval = out.result, grad_q.result, grad_kv.result
     ffn = ffn.astype(F32) + ffn_got.astype(F32)
     layer_out = (own(chain[0]) + RESID * ffn).astype(BF16)
-    def own_rows(array):
-        return lax.dynamic_slice_in_dim(array, d_at * piece, piece, 0).astype(F32)
-
-    def gain_share(parts, gain):
-        total = sum(jnp.sum(own_rows(w) * g, axis=1) for w, g in parts)
-        total = (total / own_rows(gain)).reshape(nt, piece // nt)
-        for bit in reversed([0] + x_bits):
-            total = total.reshape(2, -1, piece // nt)
-            mine = (t_at >> bit) & 1
-            send = lax.dynamic_index_in_dim(total, mine ^ 1, 0, False)
-            total = lax.dynamic_index_in_dim(total, mine, 0, False)
-            total = total + swap(send, "tensor", 1 << bit)
-        return total[0]
-
-    grad_gain1 = gain_share([(w_query, grad_query), (keyval_weight, grad_keyval)], norm1_gain)
-    grad_gain2 = gain_share([(w_gate, grad_gate), (w_up, grad_up)], norm2_gain)
+    total = row_sum(w_query, grad_query) + row_sum(keyval_weight, grad_keyval)
+    grad_gain1 = gain_share(total, norm1_gain)
     return (
         layer_out,
         grad_tokens,

time: 548 us -> 524 us (0.956)
  waiting for transfers between devices: 166 us -> 123 us
  Pallas kernels: 200 us -> 214 us
  starting transfers between devices: 90.9 us -> 80.5 us
  other arithmetic: 54 us -> 59.5 us
    ppermute x50 -> x52, waiting for transfers between devices: 166 us -> 123 us  [swap(): lax.ppermute(value, axis, [(i, j) for i, j in pairs if j > i or not up])]
    ppermute x50 -> x52, starting transfers between devices: 90.9 us -> 80.5 us  [swap(): lax.ppermute(value, axis, [(i, j) for i, j in pairs if j > i or not up])]
    pallas_call x6 -> x8, Pallas kernels: 53.5 us -> 63.8 us  [grad_rows(): pl.pallas_call(kernel, grid_spec=pltpu.PrefetchScalarGridSpec(num_scalar_...]
  transfers between devices with their start and end apart: 50 -> 52, of which waited for: 24 -> 18; matrix products, arithmetic and copies ran while one was open for 13% -> 15% of each run, Pallas kernels for 33% -> 38%
where the time goes in v3:
time: 524 us; the launch traced here: 513 us
  Pallas kernels  214 us (41%)
  waiting for transfers between devices  123 us (23%)
  starting transfers between devices  80.5 us (15%)
  other arithmetic  59.5 us (11%)
  local copies, waits for them, and re-layouts  22.6 us (4%)
  matrix products  11.6 us (2%)
    ppermute x52, waiting for transfers between devices, swap(): lax.ppermute(value, axis, [(i, j) for i, j in pairs if j > i or not up])  123 us
    ppermute x52, starting transfers between devices, swap(): lax.ppermute(value, axis, [(i, j) for i, j in pairs if j > i or not up])  80.5 us
    pallas_call x2, Pallas kernels, feed_forward(): pl.pallas_call(kernel, grid=(steps,), in_specs=[once(part)] * 2 + ([pl.Bl...  78 us
    pallas_call x8, Pallas kernels, grad_rows(): pl.pallas_call(kernel, grid_spec=pltpu.PrefetchScalarGridSpec(num_scalar_...  63.8 us
    convert_element_type x13, other arithmetic, add(): self.send = self.total(self.size).astype(BF16)  17.3 us
    pallas_call x1, Pallas kernels, attend_back(): pl.pallas_call(kernel, grid_spec=pltpu.PrefetchScalarGridSpec(num_scalar_...  17 us
    add x6, other arithmetic, total(): sum((lax.slice_in_dim(term, first, first + self.size, 1, self.axis).astyp...  14.4 us
    dot_general x4, matrix products, dot(): return lax.dot_general(a, b, dims, preferred_element_type=F32)  11.6 us
  transfers between devices with their start and end apart: 52, of which 18 were waited for; matrix products, arithmetic and copies ran while one was open for 15% of the time, Pallas kernels for 38%

profile of v3, /device:TPU:0, one launch (start us, length us, event | category | flops | bytes accessed | tf_op | source)
XLA Modules:
  0.0 513.5 jit_solution(10198693914527159531)
XLA Ops:
  11.5 5.9 %norm_keyval.1 = (bf16[2,2,3,64,2048]{4,3,2,1,0:T(8,128)(2,1)}, bf16[3,144,256]{2,1,0:T(8,128)(2,1)}, bf16[3,128,256]{2,1,0:T(8,128)(2,1)}) custom-call(s32[1]{0:T(128)} %bitcast.at, bf16[3,256,2048]{2,1,0:T(8,128)(2,1)} %tok_ref.1, s32[3,1,256]{2,1,0:T(1,128)} %broadcast_in_dim.47.seg_ref, f32[1,2048]{1,0:T(1,128)} %bitcast.205, ...), custom_call_target="tpu_custom_call" | custom-call | flops 786432 | bytes 6144 | tf_op jit(solution)/shard_map/norm_keyval/pallas_call | solution.py:100
  20.1 4.5 collective-permute-start
  25.9 11.5 %hidden_back.1.refs_0_ = f32[768,2048]{1,0:T(8,128)} custom-call(bf16[768,2048]{1,0:T(8,128)(2,1)} %multiply_convert_fusion.dy_ref.refs_0_.refs_1_.refs_2_.refs_3_, bf16[2048,2048]{1,0:T(8,128)(2,1)} %refs_4_.3), custom_call_target="tpu_custom_call" | custom-call | flops 6291456 | bytes 11264 | tf_op jit(solution)/shard_map/hidden_back/pallas_call | solution.py:542
  37.5 6.2 %collective-permute-start.2 = (bf16[2,3,144,256]{3,2,1,0:T(8,128)(2,1)S(1)}, bf16[2,3,144,256]{3,2,1,0:T(8,128)(2,1)S(1)}, u32[]{:S(2)}, u32[]{:S(2)}) collective-permute-start(bf16[2,3,144,256]{3,2,1,0:T(8,128)(2,1)S(1)} %pad_maximum_fusion.3), channel_id=1, source_target_pairs={{0,8},{4,12},{8,0},{12,4},{16,24},{20,28},{24,16},{28,20},{1,9},{5... | collective-permute-start | bytes 1327112 | tf_op jit(solution)/shard_map/ppermute | solution.py:46
  45.4 8.6 %collective-permute-done.2 = bf16[2,3,144,256]{3,2,1,0:T(8,128)(2,1)S(1)} collective-permute-done((bf16[2,3,144,256]{3,2,1,0:T(8,128)(2,1)S(1)}, bf16[2,3,144,256]{3,2,1,0:T(8,128)(2,1)S(1)}, u32[]{:S(2)}, u32[]{:S(2)}) %collective-permute-start.2) | collective-permute-done | bytes 442400 | tf_op jit(solution)/shard_map/ppermute | solution.py:46
  60.0 6.0 %project_query.1.q_ref = bf16[3,256,512]{2,1,0:T(8,128)(2,1)} custom-call(bf16[2,2,3,64,2048]{4,3,2,1,0:T(8,128)(2,1)} %get-tuple-element.238.n_ref, bf16[2048,512]{1,0:T(8,128)(2,1)} %w_ref.3, f32[256,128]{1,0:T(8,128)} %get-tuple-element.480.cos_ref.refs_11_, f32[256,128]{1,0:T(8,128)} %get-tuple-element.500.sin_ref.refs_12_), custom_call_target="tpu_custom_call" | custom-call | flops 1572864 | bytes 3072 | tf_op jit(solution)/shard_map/project_query/pallas_call | solution.py:139
  67.4 8.3 %collective-permute-done.5.refs_3_ = bf16[4,3,128,256]{3,2,1,0:T(8,128)(2,1)S(1)} collective-permute-done((bf16[4,3,128,256]{3,2,1,0:T(8,128)(2,1)S(1)}, bf16[4,3,128,256]{3,2,1,0:T(8,128)(2,1)S(1)}, u32[]{:S(2)}, u32[]{:S(2)}) %collective-permute-start.5) | collective-permute-done | bytes 786464 | tf_op jit(solution)/shard_map/ppermute | solution.py:46
  84.1 11.4 %attend.1 = (bf16[2,3,64,512]{3,2,1,0:T(8,128)(2,1)}, bf16[2,3,64,512]{3,2,1,0:T(8,128)(2,1)}, f32[3,2,1,1024]{3,2,1,0:T(1,128)}) custom-call(s32[24]{0:T(128)} %concatenate.44.sc, bf16[3,256,512]{2,1,0:T(8,128)(2,1)} %project_query.1.q_ref, bf16[4,3,144,256]{3,2,1,0:T(8,128)(2,1)} %copy-done.14, bf16[4,3,144,256]{3,2,1,0:T(8,128)(2,1)} %copy-done.24, ...), custom_call_target="tpu_custom_call" | custom-call | flops 6291456 | bytes 3072 | tf_op jit(solution)/shard_map/attend/pallas_call | solution.py:271
  99.4 8.4 %collective-permute-done.8.refs_2_ = bf16[384,512]{1,0:T(8,128)(2,1)S(1)} collective-permute-done((bf16[384,512]{1,0:T(8,128)(2,1)}, bf16[384,512]{1,0:T(8,128)(2,1)S(1)}, u32[]{:S(2)}, u32[]{:S(2)}) %collective-permute-start.8) | collective-permute-done | bytes 393248 | tf_op jit(solution)/shard_map/ppermute | solution.py:46
  107.8 7.4 %collective-permute-done.7 = bf16[3,64,2048]{2,1,0:T(8,128)(2,1)} collective-permute-done((bf16[3,64,2048]{2,1,0:T(8,128)(2,1)}, bf16[3,64,2048]{2,1,0:T(8,128)(2,1)}, u32[]{:S(2)}, u32[]{:S(2)}) %collective-permute-start.7) | collective-permute-done | bytes 786464 | tf_op jit(solution)/shard_map/ppermute | solution.py:46
  116.5 9.5 %mix.1 = (f32[384,2048]{1,0:T(8,128)}, bf16[384,2048]{1,0:T(8,128)(2,1)}) custom-call(bf16[384,512]{1,0:T(8,128)(2,1)} %bitcast.183, bf16[384,512]{1,0:T(8,128)(2,1)} %copy-done.50, bf16[384,512]{1,0:T(8,128)(2,1)} %copy-done.51, bf16[384,512]{1,0:T(8,128)(2,1)} %copy-done.52, bf16[512,2048]{1,0:T(8,128)(2,1)} %refs_9_.1, ...), custom_call_target="tpu_custom_call" | custom-call | flops 3145728 | bytes 8192 | tf_op jit(solution)/shard_map/mix/pallas_call | solution.py:484
  134.5 49.6 %feed_forward.1 = (bf16[768,2048]{1,0:T(8,128)(2,1)}, bf16[768,2048]{1,0:T(8,128)(2,1)}, bf16[768,2048]{1,0:T(8,128)(2,1)}, bf16[768,2048]{1,0:T(8,128)(2,1)}, b...) custom-call(bf16[384,2048]{1,0:T(8,128)(2,1)} %get-tuple-element.253, ...), custom_call_target="tpu_custom_call" | custom-call | flops 31457280 | bytes 24576 | tf_op jit(solution)/shard_map/feed_forward/pallas_call | solution.py:617
  184.7 7.6 %grad_rows.8 = (bf16[512,2048]{1,0:T(8,128)(2,1)}, bf16[512,2048]{1,0:T(8,128)(2,1)}) custom-call(s32[4]{0:T(128)} %get-tuple-element.496.at, bf16[768,2048]{1,0:T(8,128)(2,1)} %get-tuple-element.259.refs_0_.refs_1_.refs_2_.refs_3_, bf16[768,2048]{1,0:T(8,128)(2,1)} %get-tuple-element.259.refs_0_.refs_1_.refs_2_.refs_3_, ...), custom_call_target="tpu_custom_call" | custom-call | flops 3145728 | bytes 4608 | tf_op jit(solution)/shard_map/grad_rows/pallas_call | solution.py:679
  192.9 7.8 %grad_rows.9 = (bf16[512,2048]{1,0:T(8,128)(2,1)}, bf16[512,2048]{1,0:T(8,128)(2,1)}) custom-call(s32[4]{0:T(128)} %get-tuple-element.495.at, bf16[768,2048]{1,0:T(8,128)(2,1)} %get-tuple-element.259.refs_0_.refs_1_.refs_2_.refs_3_, bf16[768,2048]{1,0:T(8,128)(2,1)} %get-tuple-element.259.refs_0_.refs_1_.refs_2_.refs_3_, ...), custom_call_target="tpu_custom_call" | custom-call | flops 3145728 | bytes 4608 | tf_op jit(solution)/shard_map/grad_rows/pallas_call | solution.py:679
  209.9 28.4 %feed_forward_other.1 = (bf16[768,2048]{1,0:T(8,128)(2,1)}, bf16[768,2048]{1,0:T(8,128)(2,1)}, bf16[768,2048]{1,0:T(8,128)(2,1)}, bf16[768,2048]{1,0:T(8,128)(2,1)}, bf16[768,2048]{1,0:T(8,128)(2,1)}) custom-call(bf16[384,2048]{1,0:T(8,128)(2,1)} %collective-permute-done.13.nk, bf16[384,2048]{1,0:T(8,128)(2,1)} %copy-done.37, bf16[384,2048]{1,0:T(8,128)(2,1)} %bitcast.178, ...), custom_call_target="tpu_custom_call" | custom-call | flops 18874368 | bytes 24576 | tf_op jit(solution)/shard_map/feed_forward_other/pallas_call | solution.py:617
  242.2 7.2 %resid_back.1 = (f32[384,2048]{1,0:T(8,128)}, bf16[384,2048]{1,0:T(8,128)(2,1)}) custom-call(bf16[384,2048]{1,0:T(8,128)(2,1)} %copy-done.17, bf16[384,2048]{1,0:T(8,128)(2,1)} %copy-done.36, f32[384,2048]{1,0:T(8,128)} %get-tuple-element.458.refs_2_, bf16[384,2048]{1,0:T(8,128)(2,1)} %bitcast.165, f32[1,2048]{1,0:T(1,128)} %bitcast.207), custom_call_target="tpu_custom_call" | custom-call | bytes 12288 | tf_op jit(solution)/shard_map/resid_back/pallas_call | solution.py:519
  249.4 9.0 %grad_rows.10 = (f32[512,2048]{1,0:T(8,128)}, bf16[512,2048]{1,0:T(8,128)(2,1)}) custom-call(s32[4]{0:T(128)} %get-tuple-element.496.at, bf16[768,2048]{1,0:T(8,128)(2,1)} %get-tuple-element.288.refs_0_.refs_1_.refs_2_.refs_3_, bf16[768,2048]{1,0:T(8,128)(2,1)} %get-tuple-element.288.refs_0_.refs_1_.refs_2_.refs_3_, ...), custom_call_target="tpu_custom_call" | custom-call | flops 3145728 | bytes 4608 | tf_op jit(solution)/shard_map/grad_rows/pallas_call | solution.py:679
  260.9 9.1 %grad_rows.11 = (f32[512,2048]{1,0:T(8,128)}, bf16[512,2048]{1,0:T(8,128)(2,1)}) custom-call(s32[4]{0:T(128)} %get-tuple-element.495.at, bf16[768,2048]{1,0:T(8,128)(2,1)} %get-tuple-element.288.refs_0_.refs_1_.refs_2_.refs_3_, bf16[768,2048]{1,0:T(8,128)(2,1)} %get-tuple-element.288.refs_0_.refs_1_.refs_2_.refs_3_, ...), custom_call_target="tpu_custom_call" | custom-call | flops 3145728 | bytes 4608 | tf_op jit(solution)/shard_map/grad_rows/pallas_call | solution.py:679
  270.0 5.5 %collective-permute-start.24 = (bf16[512,2048]{1,0:T(8,128)(2,1)}, bf16[512,2048]{1,0:T(8,128)(2,1)}, u32[]{:S(2)}, u32[]{:S(2)}) collective-permute-start(bf16[512,2048]{1,0:T(8,128)(2,1)} %get-tuple-element.327), channel_id=1, source_target_pairs={{0,8},{4,12},{8,0},{12,4},{16,24},{20,28},{24,16},{28,20},{1,9},{5... | collective-permute-start | bytes 6291464 | tf_op jit(solution)/shard_map/ppermute | solution.py:46
  277.1 6.4 %grad_rows.12 = (f32[512,1024]{1,0:T(8,128)}, bf16[512,1024]{1,0:T(8,128)(2,1)}) custom-call(s32[8]{0:T(128)} %get-tuple-element.498.at, bf16[384,2048]{1,0:T(8,128)(2,1)} %get-tuple-element.287.refs_0_.refs_1_.refs_2_.refs_3_.refs_4_.refs_5_.refs_6_.refs_7_, ...), custom_call_target="tpu_custom_call" | custom-call | flops 1572864 | bytes 3840 | tf_op jit(solution)/shard_map/grad_rows/pallas_call | solution.py:679
  283.5 11.6 %grad_rows.13 = (f32[2048,512]{1,0:T(8,128)}, bf16[2048,512]{1,0:T(8,128)(2,1)}) custom-call(s32[4]{0:T(128)} %get-tuple-element.496.at, bf16[768,2048]{1,0:T(8,128)(2,1)} %multiply_convert_fusion.dy_ref.refs_0_.refs_1_.refs_2_.refs_3_, bf16[768,2048]{1,0:T(8,128)(2,1)} %multiply_convert_fusion.dy_ref.refs_0_.refs_1_.refs_2_.refs_3_, ...), custom_call_target="tpu_custom_call" | custom-call | flops 6291456 | bytes 9216 | tf_op jit(solution)/shard_map/grad_rows/pallas_call | solution.py:679
  298.9 17.0 %attend_back.1 = (bf16[2,3,64,512]{3,2,1,0:T(8,128)(2,1)}, bf16[2,3,64,512]{3,2,1,0:T(8,128)(2,1)}, bf16[4,3,128,256]{3,2,1,0:T(8,128)(2,1)}, bf16[4,3,128,256]{...) custom-call(s32[24]{0:T(128)} %concatenate.44.sc, ...), custom_call_target="tpu_custom_call" | custom-call | flops 15728640 | bytes 6144 | tf_op jit(solution)/shard_map/attend_back/pallas_call | solution.py:396
  319.8 7.2 %collective-permute-start.22 = (bf16[4,3,128,256]{3,2,1,0:T(8,128)(2,1)}, bf16[4,3,128,256]{3,2,1,0:T(8,128)(2,1)S(1)}, u32[]{:S(2)}, u32[]{:S(2)}) collective-permute-start(bf16[4,3,128,256]{3,2,1,0:T(8,128)(2,1)} %get-tuple-element.323), channel_id=1, source_target_pairs={{0,4},{4,0},{8,12},{12,8},{16,20},{20,16},{24,28},{28,24},{1,5},{5... | collective-permute-start | bytes 2359304 | tf_op jit(solution)/shard_map/ppermute | solution.py:46
  327.0 17.2 %collective-permute-done.26 = bf16[512,1024]{1,0:T(8,128)(2,1)S(1)} collective-permute-done((bf16[512,1024]{1,0:T(8,128)(2,1)}, bf16[512,1024]{1,0:T(8,128)(2,1)S(1)}, u32[]{:S(2)}, u32[]{:S(2)}) %collective-permute-start.26) | collective-permute-done | bytes 1048608 | tf_op jit(solution)/shard_map/ppermute | solution.py:46
  348.4 6.8 %grad_rows.14 = (f32[1024,512]{1,0:T(8,128)}, bf16[1024,512]{1,0:T(8,128)(2,1)}) custom-call(s32[8]{0:T(128)} %get-tuple-element.497.at, bf16[384,2048]{1,0:T(8,128)(2,1)} %bitcast.143, bf16[384,2048]{1,0:T(8,128)(2,1)} %bitcast.144, bf16[384,2048]{1,0:T(8,128)(2,1)} %bitcast.145, bf16[384,2048]{1,0:T(8,128)(2,1)} %bitcast.146, bf16[384,2048]{1,0:T(8,128)(2,1)} %bitcast.147, ...), custom_call_target="tpu_custom_call" | custom-call | flops 1572864 | bytes 3840 | tf_op jit(solution)/shard_map/grad_rows/pallas_call | solution.py:679
  358.0 11.2 %collective-permute-done.22.refs_1_ = bf16[4,3,128,256]{3,2,1,0:T(8,128)(2,1)S(1)} collective-permute-done((bf16[4,3,128,256]{3,2,1,0:T(8,128)(2,1)}, bf16[4,3,128,256]{3,2,1,0:T(8,128)(2,1)S(1)}, u32[]{:S(2)}, u32[]{:S(2)}) %collective-permute-start.22) | collective-permute-done | bytes 786464 | tf_op jit(solution)/shard_map/ppermute | solution.py:46
  371.2 5.5 %collective-permute-start.29 = (bf16[2,3,128,256]{3,2,1,0:T(8,128)(2,1)S(1)}, bf16[2,3,128,256]{3,2,1,0:T(8,128)(2,1)S(1)}, u32[]{:S(2)}, u32[]{:S(2)}) collective-permute-start(bf16[2,3,128,256]{3,2,1,0:T(8,128)(2,1)S(1)} %add_convert_fusion.9), channel_id=1, source_target_pairs={{0,8},{4,12},{8,0},{12,4},{16,24},{20,28},{24,16},{28,20},{1,9},{5... | collective-permute-start | bytes 1179656 | tf_op jit(solution)/shard_map/ppermute | solution.py:46
  380.3 5.1 collective-permute-done.29.refs_2_
  396.8 21.8 %collective-permute-done.31.refs_3_ = bf16[1,3,128,256]{3,2,1,0:T(8,128)(2,1)S(1)} collective-permute-done((bf16[1,3,128,256]{3,2,1,0:T(8,128)(2,1)}, bf16[1,3,128,256]{3,2,1,0:T(8,128)(2,1)S(1)}, u32[]{:S(2)}, u32[]{:S(2)}) %collective-permute-start.31) | collective-permute-done | bytes 196640 | tf_op jit(solution)/shard_map/ppermute | solution.py:46
  439.4 5.5 %grad_rows.15 = (f32[1024,256]{1,0:T(8,128)}, bf16[1024,256]{1,0:T(8,128)(2,1)}) custom-call(s32[8]{0:T(128)} %get-tuple-element.498.at, bf16[384,2048]{1,0:T(8,128)(2,1)} %bitcast.151, bf16[384,2048]{1,0:T(8,128)(2,1)} %bitcast.152, bf16[384,2048]{1,0:T(8,128)(2,1)} %bitcast.153, bf16[384,2048]{1,0:T(8,128)(2,1)} %bitcast.154, bf16[384,2048]{1,0:T(8,128)(2,1)} %bitcast.155, ...), custom_call_target="tpu_custom_call" | custom-call | flops 786432 | bytes 3456 | tf_op jit(solution)/shard_map/grad_rows/pallas_call | solution.py:679
  459.2 5.9 %collective-permute-done.36 = bf16[1024,256]{1,0:T(8,128)(2,1)S(1)} collective-permute-done((bf16[1024,256]{1,0:T(8,128)(2,1)}, bf16[1024,256]{1,0:T(8,128)(2,1)S(1)}, u32[]{:S(2)}, u32[]{:S(2)}) %collective-permute-start.36) | collective-permute-done | bytes 524320 | tf_op jit(solution)/shard_map/ppermute | solution.py:46
  487.2 14.5 %collective-permute-done.45 = bf16[256,512]{1,0:T(8,128)(2,1)S(1)} collective-permute-done((bf16[256,512]{1,0:T(8,128)(2,1)S(1)}, bf16[256,512]{1,0:T(8,128)(2,1)S(1)}, u32[]{:S(2)}, u32[]{:S(2)}) %collective-permute-start.45) | collective-permute-done | bytes 262176 | tf_op jit(solution)/shard_map/ppermute | solution.py:46
  (300 shorter events, 164.3 us)
Async XLA Ops:
  0.6 66.6 %collective-permute-start.11 = (bf16[512,2048]{1,0:T(8,128)(2,1)}, bf16[512,2048]{1,0:T(8,128)(2,1)}, u32[]{:S(2)}, u32[]{:S(2)}) collective-permute-start(bf16[512,2048]{1,0:T(8,128)(2,1)} %refs_9_.1), channel_id=1, source_target_pairs={{0,2},{1,3},{2,0},{3,1},{4,6},{5,7},{6,4},{7,5},{8,10},{9,11},{10,... | collective-permute-start | bytes 6291464 | tf_op jit(solution)/shard_map/ppermute | solution.py:46
  45.3 69.8 %collective-permute-start.10 = (bf16[512,2048]{1,0:T(8,128)(2,1)}, bf16[512,2048]{1,0:T(8,128)(2,1)}, u32[]{:S(2)}, u32[]{:S(2)}) collective-permute-start(bf16[512,2048]{1,0:T(8,128)(2,1)} %refs_9_.1), channel_id=1, source_target_pairs={{0,1},{1,0},{2,3},{3,2},{4,5},{5,4},{6,7},{7,6},{8,9},{9,8},{10,11... | collective-permute-start | bytes 6291464 | tf_op jit(solution)/shard_map/ppermute | solution.py:46
  54.1 21.5 %collective-permute-start.3 = (bf16[4,3,144,256]{3,2,1,0:T(8,128)(2,1)S(1)}, bf16[4,3,144,256]{3,2,1,0:T(8,128)(2,1)S(1)}, u32[]{:S(2)}, u32[]{:S(2)}) collective-permute-start(bf16[4,3,144,256]{3,2,1,0:T(8,128)(2,1)S(1)} %pad_maximum_fusion.1.refs_0_), channel_id=1, source_target_pairs={{0,4},{4,0},{8,12},{12,8},{16,20},{20,16},{24,28},{28,24},{1,5},{5... | collective-permute-start | bytes 2654216 | tf_op jit(solution)/shard_map/ppermute | solution.py:46
  56.8 18.8 %collective-permute-start.5 = (bf16[4,3,128,256]{3,2,1,0:T(8,128)(2,1)S(1)}, bf16[4,3,128,256]{3,2,1,0:T(8,128)(2,1)S(1)}, u32[]{:S(2)}, u32[]{:S(2)}) collective-permute-start(bf16[4,3,128,256]{3,2,1,0:T(8,128)(2,1)S(1)} %pad_maximum_fusion.2.refs_2_), channel_id=1, source_target_pairs={{0,8},{4,12},{8,0},{12,4},{16,24},{20,28},{24,16},{28,20},{1,9},{5... | collective-permute-start | bytes 2359304 | tf_op jit(solution)/shard_map/ppermute | solution.py:46
  67.3 48.5 %collective-permute-start.12 = (bf16[512,2048]{1,0:T(8,128)(2,1)}, bf16[512,2048]{1,0:T(8,128)(2,1)}, u32[]{:S(2)}, u32[]{:S(2)}) collective-permute-start(bf16[512,2048]{1,0:T(8,128)(2,1)} %collective-permute-done.11.refs_6_), channel_id=1, source_target_pairs={{0,1},{1,0},{2,3},{3,2},{4,5},{5,4},{6,7},{7,6},{8,9},{9,8},{10,11... | collective-permute-start | bytes 6291464 | tf_op jit(solution)/shard_map/ppermute | solution.py:46
  78.5 36.6 %collective-permute-start.7 = (bf16[3,64,2048]{2,1,0:T(8,128)(2,1)}, bf16[3,64,2048]{2,1,0:T(8,128)(2,1)}, u32[]{:S(2)}, u32[]{:S(2)}) collective-permute-start(bf16[3,64,2048]{2,1,0:T(8,128)(2,1)} %multiply_convert_fusion.1), channel_id=1, source_target_pairs={{0,16},{4,20},{8,24},{12,28},{16,0},{20,4},{24,8},{28,12},{1,17},{... | collective-permute-start | bytes 2359304 | tf_op jit(solution)/shard_map/ppermute | solution.py:46
  97.5 18.2 %collective-permute-start.9 = (bf16[384,512]{1,0:T(8,128)(2,1)S(1)}, bf16[384,512]{1,0:T(8,128)(2,1)S(1)}, u32[]{:S(2)}, u32[]{:S(2)}) collective-permute-start(bf16[384,512]{1,0:T(8,128)(2,1)S(1)} %collective-permute-done.6.refs_1_), channel_id=1, source_target_pairs={{0,2},{1,3},{2,0},{3,1},{4,6},{5,7},{6,4},{7,5},{8,10},{9,11},{10,... | collective-permute-start | bytes 1179656 | tf_op jit(solution)/shard_map/ppermute | solution.py:46
  129.7 71.0 %collective-permute-start.15 = (bf16[1,3,64,2048]{3,2,1,0:T(8,128)(2,1)}, bf16[1,3,64,2048]{3,2,1,0:T(8,128)(2,1)S(1)}, u32[]{:S(2)}, u32[]{:S(2)}) collective-permute-start(bf16[1,3,64,2048]{3,2,1,0:T(8,128)(2,1)} %bitcast.29), channel_id=1, source_target_pairs={{0,2},{1,3},{2,0},{3,1},{4,6},{5,7},{6,4},{7,5},{8,10},{9,11},{10,... | collective-permute-start | bytes 2359304 | tf_op jit(solution)/shard_map/ppermute | solution.py:46
  130.3 72.7 %collective-permute-start.13 = (bf16[384,2048]{1,0:T(8,128)(2,1)}, bf16[384,2048]{1,0:T(8,128)(2,1)}, u32[]{:S(2)}, u32[]{:S(2)}) collective-permute-start(bf16[384,2048]{1,0:T(8,128)(2,1)} %get-tuple-element.253.nk), channel_id=1, source_target_pairs={{0,16},{4,20},{8,24},{12,28},{16,0},{20,4},{24,8},{28,12},{1,17},{... | collective-permute-start | bytes 4718600 | tf_op jit(solution)/shard_map/ppermute | solution.py:46
  184.1 19.4 %collective-permute-start.17 = (bf16[384,2048]{1,0:T(8,128)(2,1)}, bf16[384,2048]{1,0:T(8,128)(2,1)S(1)}, u32[]{:S(2)}, u32[]{:S(2)}) collective-permute-start(bf16[384,2048]{1,0:T(8,128)(2,1)} %get-tuple-element.271), channel_id=1, source_target_pairs={{0,1},{1,0},{2,3},{3,2},{4,5},{5,4},{6,7},{7,6},{8,9},{9,8},{10,11... | collective-permute-start | bytes 4718600 | tf_op jit(solution)/shard_map/ppermute | solution.py:46
  204.6 36.4 %collective-permute-start.20 = (bf16[384,2048]{1,0:T(8,128)(2,1)S(1)}, bf16[384,2048]{1,0:T(8,128)(2,1)S(1)}, u32[]{:S(2)}, u32[]{:S(2)}) collective-permute-start(bf16[384,2048]{1,0:T(8,128)(2,1)S(1)} %add_convert_fusion.1.refs_0_), channel_id=1, source_target_pairs={{0,2},{1,3},{2,0},{3,1},{4,6},{5,7},{6,4},{7,5},{8,10},{9,11},{10,... | collective-permute-start | bytes 4718600 | tf_op jit(solution)/shard_map/ppermute | solution.py:46
  249.4 26.6 %collective-permute-start.21 = (bf16[384,2048]{1,0:T(8,128)(2,1)}, bf16[384,2048]{1,0:T(8,128)(2,1)S(1)}, u32[]{:S(2)}, u32[]{:S(2)}) collective-permute-start(bf16[384,2048]{1,0:T(8,128)(2,1)} %get-tuple-element.287.refs_0_.refs_1_.refs_2_.refs_3_.refs_4_.refs_5_.refs_6_.refs_7_), channel_id=1, source_target_pairs={{0,1},{1,0},{2,3},{3,2},{4,5},{5,4},{6,7},{7,6},{8,9},{9,8},{10,11... | collective-permute-start | bytes 4718600 | tf_op jit(solution)/shard_map/ppermute | solution.py:46
  258.3 61.4 %collective-permute-start.27 = (bf16[512,2048]{1,0:T(8,128)(2,1)}, bf16[512,2048]{1,0:T(8,128)(2,1)}, u32[]{:S(2)}, u32[]{:S(2)}) collective-permute-start(bf16[512,2048]{1,0:T(8,128)(2,1)} %get-tuple-element.330), channel_id=1, source_target_pairs={{0,4},{4,0},{8,12},{12,8},{16,20},{20,16},{24,28},{28,24},{1,5},{5... | collective-permute-start | bytes 6291464 | tf_op jit(solution)/shard_map/ppermute | solution.py:46
  270.0 78.4 %collective-permute-start.24 = (bf16[512,2048]{1,0:T(8,128)(2,1)}, bf16[512,2048]{1,0:T(8,128)(2,1)}, u32[]{:S(2)}, u32[]{:S(2)}) collective-permute-start(bf16[512,2048]{1,0:T(8,128)(2,1)} %get-tuple-element.327), channel_id=1, source_target_pairs={{0,8},{4,12},{8,0},{12,4},{16,24},{20,28},{24,16},{28,20},{1,9},{5... | collective-permute-start | bytes 6291464 | tf_op jit(solution)/shard_map/ppermute | solution.py:46
  295.1 49.0 %collective-permute-start.26 = (bf16[512,1024]{1,0:T(8,128)(2,1)}, bf16[512,1024]{1,0:T(8,128)(2,1)S(1)}, u32[]{:S(2)}, u32[]{:S(2)}) collective-permute-start(bf16[512,1024]{1,0:T(8,128)(2,1)} %get-tuple-element.329), channel_id=1, source_target_pairs={{0,8},{4,12},{8,0},{12,4},{16,24},{20,28},{24,16},{28,20},{1,9},{5... | collective-permute-start | bytes 3145736 | tf_op jit(solution)/shard_map/ppermute | solution.py:46
  295.1 62.9 %collective-permute-start.23 = (bf16[2048,512]{1,0:T(8,128)(2,1)}, bf16[2048,512]{1,0:T(8,128)(2,1)}, u32[]{:S(2)}, u32[]{:S(2)}) collective-permute-start(bf16[2048,512]{1,0:T(8,128)(2,1)} %get-tuple-element.324), channel_id=1, source_target_pairs={{0,4},{4,0},{8,12},{12,8},{16,20},{20,16},{24,28},{28,24},{1,5},{5... | collective-permute-start | bytes 6291464 | tf_op jit(solution)/shard_map/ppermute | solution.py:46
  297.3 51.1 %collective-permute-start.25 = (bf16[1,3,64,2048]{3,2,1,0:T(8,128)(2,1)S(1)}, bf16[1,3,64,2048]{3,2,1,0:T(8,128)(2,1)S(1)}, u32[]{:S(2)}, u32[]{:S(2)}) collective-permute-start(bf16[1,3,64,2048]{3,2,1,0:T(8,128)(2,1)S(1)} %dynamic-slice_bitcast_fusion.1), channel_id=1, source_target_pairs={{0,2},{1,3},{2,0},{3,1},{4,6},{5,7},{6,4},{7,5},{8,10},{9,11},{10,... | collective-permute-start | bytes 2359304 | tf_op jit(solution)/shard_map/ppermute | solution.py:46
  319.8 49.4 %collective-permute-start.22 = (bf16[4,3,128,256]{3,2,1,0:T(8,128)(2,1)}, bf16[4,3,128,256]{3,2,1,0:T(8,128)(2,1)S(1)}, u32[]{:S(2)}, u32[]{:S(2)}) collective-permute-start(bf16[4,3,128,256]{3,2,1,0:T(8,128)(2,1)} %get-tuple-element.323), channel_id=1, source_target_pairs={{0,4},{4,0},{8,12},{12,8},{16,20},{20,16},{24,28},{28,24},{1,5},{5... | collective-permute-start | bytes 2359304 | tf_op jit(solution)/shard_map/ppermute | solution.py:46
  344.1 25.1 %collective-permute-start.28 = (bf16[4,3,128,256]{3,2,1,0:T(8,128)(2,1)}, bf16[4,3,128,256]{3,2,1,0:T(8,128)(2,1)S(1)}, u32[]{:S(2)}, u32[]{:S(2)}) collective-permute-start(bf16[4,3,128,256]{3,2,1,0:T(8,128)(2,1)} %get-tuple-element.345), channel_id=1, source_target_pairs={{0,8},{4,12},{8,0},{12,4},{16,24},{20,28},{24,16},{28,20},{1,9},{5... | collective-permute-start | bytes 2359304 | tf_op jit(solution)/shard_map/ppermute | solution.py:46
  387.0 40.5 %collective-permute-start.35 = (bf16[256,2048]{1,0:T(8,128)(2,1)}, bf16[256,2048]{1,0:T(8,128)(2,1)S(1)}, u32[]{:S(2)}, u32[]{:S(2)}) collective-permute-start(bf16[256,2048]{1,0:T(8,128)(2,1)} %add_convert_fusion.4), channel_id=1, source_target_pairs={{0,8},{4,12},{8,0},{12,4},{16,24},{20,28},{24,16},{28,20},{1,9},{5... | collective-permute-start | bytes 3145736 | tf_op jit(solution)/shard_map/ppermute | solution.py:46
  388.8 38.8 %collective-permute-start.34 = (bf16[256,2048]{1,0:T(8,128)(2,1)}, bf16[256,2048]{1,0:T(8,128)(2,1)}, u32[]{:S(2)}, u32[]{:S(2)}) collective-permute-start(bf16[256,2048]{1,0:T(8,128)(2,1)} %add_convert_fusion.5), channel_id=1, source_target_pairs={{0,4},{4,0},{8,12},{12,8},{16,20},{20,16},{24,28},{28,24},{1,5},{5... | collective-permute-start | bytes 3145736 | tf_op jit(solution)/shard_map/ppermute | solution.py:46
  389.3 30.1 %collective-permute-start.32 = (bf16[1,3,128,256]{3,2,1,0:T(8,128)(2,1)}, bf16[1,3,128,256]{3,2,1,0:T(8,128)(2,1)S(1)}, u32[]{:S(2)}, u32[]{:S(2)}) collective-permute-start(bf16[1,3,128,256]{3,2,1,0:T(8,128)(2,1)} %add_convert_fusion.13), channel_id=1, source_target_pairs={{0,16},{4,20},{8,24},{12,28},{16,0},{20,4},{24,8},{28,12},{1,17},{... | collective-permute-start | bytes 589832 | tf_op jit(solution)/shard_map/ppermute | solution.py:46
  390.0 28.7 %collective-permute-start.31 = (bf16[1,3,128,256]{3,2,1,0:T(8,128)(2,1)}, bf16[1,3,128,256]{3,2,1,0:T(8,128)(2,1)S(1)}, u32[]{:S(2)}, u32[]{:S(2)}) collective-permute-start(bf16[1,3,128,256]{3,2,1,0:T(8,128)(2,1)} %add_convert_fusion.14), channel_id=1, source_target_pairs={{0,16},{4,20},{8,24},{12,28},{16,0},{20,4},{24,8},{28,12},{1,17},{... | collective-permute-start | bytes 589832 | tf_op jit(solution)/shard_map/ppermute | solution.py:46
  392.2 35.4 %collective-permute-start.33 = (bf16[512,512]{1,0:T(8,128)(2,1)}, bf16[512,512]{1,0:T(8,128)(2,1)}, u32[]{:S(2)}, u32[]{:S(2)}) collective-permute-start(bf16[512,512]{1,0:T(8,128)(2,1)} %add_convert_fusion.7), channel_id=1, source_target_pairs={{0,4},{4,0},{8,12},{12,8},{16,20},{20,16},{24,28},{28,24},{1,5},{5... | collective-permute-start | bytes 1572872 | tf_op jit(solution)/shard_map/ppermute | solution.py:46
  418.6 38.3 %collective-permute-start.37 = (bf16[1024,512]{1,0:T(8,128)(2,1)}, bf16[1024,512]{1,0:T(8,128)(2,1)}, u32[]{:S(2)}, u32[]{:S(2)}) collective-permute-start(bf16[1024,512]{1,0:T(8,128)(2,1)} %get-tuple-element.403), channel_id=1, source_target_pairs={{0,4},{4,0},{8,12},{12,8},{16,20},{20,16},{24,28},{28,24},{1,5},{5... | collective-permute-start | bytes 3145736 | tf_op jit(solution)/shard_map/ppermute | solution.py:46
  419.4 32.7 %collective-permute-start.38 = (bf16[2048,256]{1,0:T(8,128)(2,1)}, bf16[2048,256]{1,0:T(8,128)(2,1)}, u32[]{:S(2)}, u32[]{:S(2)}) collective-permute-start(bf16[2048,256]{1,0:T(8,128)(2,1)} %add_convert_fusion.3), channel_id=1, source_target_pairs={{0,8},{4,12},{8,0},{12,4},{16,24},{20,28},{24,16},{28,20},{1,9},{5... | collective-permute-start | bytes 3145736 | tf_op jit(solution)/shard_map/ppermute | solution.py:46
  427.6 21.0 %collective-permute-start.39 = (bf16[384,2048]{1,0:T(8,128)(2,1)}, bf16[384,2048]{1,0:T(8,128)(2,1)}, u32[]{:S(2)}, u32[]{:S(2)}) collective-permute-start(bf16[384,2048]{1,0:T(8,128)(2,1)} %add_convert_fusion), channel_id=1, source_target_pairs={{0,1},{1,0},{2,3},{3,2},{4,5},{5,4},{6,7},{7,6},{8,9},{9,8},{10,11... | collective-permute-start | bytes 4718600 | tf_op jit(solution)/shard_map/ppermute | solution.py:46
  444.9 20.1 %collective-permute-start.36 = (bf16[1024,256]{1,0:T(8,128)(2,1)}, bf16[1024,256]{1,0:T(8,128)(2,1)S(1)}, u32[]{:S(2)}, u32[]{:S(2)}) collective-permute-start(bf16[1024,256]{1,0:T(8,128)(2,1)} %get-tuple-element.401), channel_id=1, source_target_pairs={{0,8},{4,12},{8,0},{12,4},{16,24},{20,28},{24,16},{28,20},{1,9},{5... | collective-permute-start | bytes 1572872 | tf_op jit(solution)/shard_map/ppermute | solution.py:46
  445.6 34.2 %collective-permute-start.42 = (bf16[512,256]{1,0:T(8,128)(2,1)}, bf16[512,256]{1,0:T(8,128)(2,1)}, u32[]{:S(2)}, u32[]{:S(2)}) collective-permute-start(bf16[512,256]{1,0:T(8,128)(2,1)} %add_convert_fusion.12), channel_id=1, source_target_pairs={{0,16},{4,20},{8,24},{12,28},{16,0},{20,4},{24,8},{28,12},{1,17},{... | collective-permute-start | bytes 786440 | tf_op jit(solution)/shard_map/ppermute | solution.py:46
  452.0 19.4 %collective-permute-start.43 = (bf16[1,3,64,2048]{3,2,1,0:T(8,128)(2,1)S(1)}, bf16[1,3,64,2048]{3,2,1,0:T(8,128)(2,1)S(1)}, u32[]{:S(2)}, u32[]{:S(2)}) collective-permute-start(bf16[1,3,64,2048]{3,2,1,0:T(8,128)(2,1)S(1)} %fusion.8), channel_id=1, source_target_pairs={{0,2},{1,3},{2,0},{3,1},{4,6},{5,7},{6,4},{7,5},{8,10},{9,11},{10,... | collective-permute-start | bytes 2359304 | tf_op jit(solution)/shard_map/ppermute | solution.py:46
  483.5 18.1 %collective-permute-start.45 = (bf16[256,512]{1,0:T(8,128)(2,1)S(1)}, bf16[256,512]{1,0:T(8,128)(2,1)S(1)}, u32[]{:S(2)}, u32[]{:S(2)}) collective-permute-start(bf16[256,512]{1,0:T(8,128)(2,1)S(1)} %add_convert_fusion.10), channel_id=1, source_target_pairs={{0,16},{4,20},{8,24},{12,28},{16,0},{20,4},{24,8},{28,12},{1,17},{... | collective-permute-start | bytes 786440 | tf_op jit(solution)/shard_map/ppermute | solution.py:46
  484.0 20.3 %collective-permute-start.44 = (bf16[256,256]{1,0:T(8,128)(2,1)S(1)}, bf16[256,256]{1,0:T(8,128)(2,1)S(1)}, u32[]{:S(2)}, u32[]{:S(2)}) collective-permute-start(bf16[256,256]{1,0:T(8,128)(2,1)S(1)} %add_convert_fusion.15), channel_id=1, source_target_pairs={{0,16},{4,20},{8,24},{12,28},{16,0},{20,4},{24,8},{28,12},{1,17},{... | collective-permute-start | bytes 393224 | tf_op jit(solution)/shard_map/ppermute | solution.py:46
  (79 other events, 870.9 us)
